TPU v7x, 512 devices: a whole 4x4x16 slice. The times are simulated.
512 devices in a mesh: lon: 32 (over x_lo, z), lat: 16 (over x_hi, y, core).
Axes of the slice: x: 4 (x_hi: 2, x_lo: 2; x = x_hi * 2 + x_lo), y: 4, z: 16, core: 2. Of those that a mesh axis runs over, the one named last changes fastest.
Arguments:
- tokens: bfloat16 [2, 384, 384, 192], P(None, 'lat', 'lon'), may hold values from -6 to 6
- cotangent: bfloat16 [2, 384, 384, 192], P(None, 'lat', 'lon'), may hold values from -6 to 6
- w_qkv: bfloat16 [192, 576], replicated, may hold values from -0.4375 to 0.4375
- w_proj: bfloat16 [192, 192], replicated, may hold values from -0.4375 to 0.4375
- w_up: bfloat16 [192, 768], replicated, may hold values from -0.4375 to 0.4375
- w_down: bfloat16 [768, 192], replicated, may hold values from -0.21875 to 0.21875
- bias_table: bfloat16 [32, 19872], replicated, may hold values from -4 to 220
- band_rows: int32 [16], replicated, may hold values from 1 to 4, 32 in all
- lon_shift: int32 [32], replicated, may hold values from 1 to 11
Outputs:
- output: bfloat16 [2, 384, 384, 192], P(None, 'lat', 'lon')
- grad_tokens: bfloat16 [2, 384, 384, 192], P(None, 'lat', 'lon')
- grad_qkv: float32 [192, 576], P('lat', 'lon')
- grad_proj: float32 [192, 192], P('lat', 'lon')
- grad_up: float32 [192, 768], P('lat', 'lon')
- grad_down: float32 [768, 192], P('lat', 'lon')
- grad_table: float32 [32, 19872], P('lat', 'lon')
Inputs may be any that keep to these rules, and one draw needn't show every extreme that they name: Band b holds its rows in its first band_rows[b] slots; the entries sum to 32 and the largest is exactly 4.
All inputs are finite; a program needn't handle non-finite values.
Results may differ from a plain program's by a relative error of at most 0.04.
Values may be sent and summed in bfloat16 or wider, within the bound.
No kernel may reach another device: no remote copies, remote signals or barrier semaphores. Data moves between devices by JAX's collectives and lax.ppermute only.
A program may use at most 192 MiB of HBM per device.

v0:
```python
import jax
import jax.numpy as jnp
from jax import lax
from jax.sharding import PartitionSpec as P

HEADS = 6
WZ = 2
WH = 6
WW = 12
LEVELS = 2
WTOK = 144
POS = 3312


epsilon = 1e-05


def from_behind(x, axis, by):
    count = lax.axis_size(axis)
    return lax.ppermute(x, axis, [(i, (i + by) % count) for i in range(count)])


def product(form, left, right):
    return jnp.einsum(form, left, right, preferred_element_type=jnp.float32)


def offset_table():
    rel_span = 2 * WW - 1
    spans = jnp.arange(rel_span, dtype=jnp.int32)[:, None, None]
    col_q = jnp.arange(WW, dtype=jnp.int32)[None, :, None]
    col_k = jnp.arange(WW, dtype=jnp.int32)[None, None, :]
    return (col_q - col_k + WW - 1 == spans).astype(jnp.float32)


def make_bias(table_rows, spread):
    n_rows = table_rows.shape[0]
    rel_span = 2 * WW - 1
    shaped = table_rows.astype(jnp.float32).reshape(n_rows, HEADS, WZ, WZ, WH, WH, rel_span)
    full = jnp.einsum("rhabcde,epq->rhbdpacq", shaped, spread, precision=lax.Precision.HIGHEST)
    return full.reshape(n_rows, HEADS, WTOK, WTOK)


def table_grad(grad_bias, spread):
    n_rows = grad_bias.shape[0]
    shaped = grad_bias.reshape(n_rows, HEADS, WZ, WH, WW, WZ, WH, WW)
    summed = jnp.einsum("rhbdpacq,epq->rhabcde", shaped, spread, precision=lax.Precision.HIGHEST)
    return summed.reshape(n_rows, HEADS * POS)


def to_windows(grid, n_rows, n_win):
    model_width = grid.shape[-1]
    parted = grid.reshape(LEVELS, n_rows, WH, n_win, WW, model_width)
    return parted.transpose(1, 3, 0, 2, 4, 5).reshape(n_rows, n_win, WTOK, model_width)


def from_windows(blocks):
    n_rows = blocks.shape[0]
    n_win = blocks.shape[1]
    model_width = blocks.shape[3]
    parted = blocks.reshape(n_rows, n_win, LEVELS, WH, WW, model_width)
    return parted.transpose(2, 0, 3, 1, 4, 5).reshape(LEVELS, n_rows * WH, n_win * WW, model_width)


def slice_rows(grid, starts, n_rows, width):
    shaped = grid.reshape(grid.shape[0], grid.shape[1], n_rows, WH, grid.shape[3], grid.shape[4])

    def cut_row(piece_row, first_col):
        return lax.dynamic_slice_in_dim(piece_row, first_col, width, 3)

    cut = jax.vmap(cut_row, in_axes=(2, 0), out_axes=2)(shaped, starts)
    return cut.reshape(grid.shape[0], grid.shape[1], n_rows * WH, width, grid.shape[4])


def place_rows(blank, pieces, starts, n_rows):
    shaped_blank = blank.reshape(
        blank.shape[0], blank.shape[1], n_rows, WH, blank.shape[3], blank.shape[4]
    )
    shaped_piece = pieces.reshape(
        pieces.shape[0], pieces.shape[1], n_rows, WH, pieces.shape[3], pieces.shape[4]
    )

    def put_row(blank_row, piece_row, first_col):
        return lax.dynamic_update_slice_in_dim(blank_row, piece_row, first_col, 3)

    placed = jax.vmap(put_row, in_axes=(2, 2, 0), out_axes=2)(shaped_blank, shaped_piece, starts)
    return placed.reshape(blank.shape)


def normalize(values):
    centre = jnp.mean(values, axis=-1, keepdims=True)
    shifted = values - centre
    inv_std = lax.rsqrt(jnp.mean(shifted * shifted, axis=-1, keepdims=True) + epsilon)
    return (shifted * inv_std, inv_std)


def norm_back(normed, inv_std, grad_normed):
    mean_grad = jnp.mean(grad_normed, axis=-1, keepdims=True)
    mean_proj = jnp.mean(grad_normed * normed, axis=-1, keepdims=True)
    return inv_std * (grad_normed - mean_grad - normed * mean_proj)


def gelu_parts(pre_act):
    gauss_cdf = 0.5 * (1.0 + lax.erf(pre_act * 0.7071067811865476))
    density = jnp.exp(-0.5 * pre_act * pre_act) * 0.3989422804014327
    return (pre_act * gauss_cdf, gauss_cdf + pre_act * density)


def window_pass(windows, cotan, bias, keep_mask, w_qkv, w_proj, w_up, w_down):
    n_rows, n_win, n_tok, model_width = windows.shape
    n_heads = bias.shape[1]
    head_dim = model_width // n_heads
    q_scale = head_dim ** (-0.5)
    head_shape = (n_rows, n_win, n_tok, n_heads, head_dim)
    tokens_f = windows.astype(jnp.float32)
    normed_a, inv_a = normalize(tokens_f)
    normed_a_b = normed_a.astype(jnp.bfloat16)
    qkv_all = product("rntd,de->rnte", normed_a_b, w_qkv)
    query = (qkv_all[..., :model_width] * q_scale).astype(jnp.bfloat16).reshape(head_shape)
    key_cells = qkv_all[..., model_width : 2 * model_width].astype(jnp.bfloat16).reshape(head_shape)
    values = qkv_all[..., 2 * model_width :].astype(jnp.bfloat16).reshape(head_shape)
    scores = product("rnqhc,rnkhc->rnhqk", query, key_cells) + bias[:, None]
    row_top = jnp.max(scores, axis=-1, keepdims=True)
    exp_scores = jnp.exp(scores - row_top)
    probs_f = exp_scores / jnp.sum(exp_scores, axis=-1, keepdims=True)
    probs_b = probs_f.astype(jnp.bfloat16)
    attended = product("rnhqk,rnkhc->rnqhc", probs_b, values)
    attended = attended.reshape(n_rows, n_win, n_tok, model_width).astype(jnp.bfloat16)
    hidden = tokens_f + product("rntd,de->rnte", attended, w_proj)
    normed_b, inv_b = normalize(hidden)
    normed_b_b = normed_b.astype(jnp.bfloat16)
    pre_act = product("rntd,df->rntf", normed_b_b, w_up)
    act_f, gelu_slope = gelu_parts(pre_act)
    act_b = act_f.astype(jnp.bfloat16)
    output = (hidden + product("rntf,fd->rntd", act_b, w_down)).astype(jnp.bfloat16)
    keep_b = keep_mask[:, :, None, None].astype(jnp.bfloat16)
    grad_down = product("rntf,rntd->fd", act_b * keep_b, cotan)
    grad_act = product("rntd,fd->rntf", cotan, w_down)
    grad_pre = (grad_act * gelu_slope).astype(jnp.bfloat16)
    grad_up = product("rntd,rntf->df", normed_b_b * keep_b, grad_pre)
    grad_normed = product("rntf,df->rntd", grad_pre, w_up)
    grad_hidden = cotan.astype(jnp.float32) + norm_back(normed_b, inv_b, grad_normed)
    grad_hidden_b = grad_hidden.astype(jnp.bfloat16)
    grad_proj = product("rnte,rntd->ed", attended * keep_b, grad_hidden_b)
    grad_att = (
        product("rntd,ed->rnte", grad_hidden_b, w_proj).astype(jnp.bfloat16).reshape(head_shape)
    )
    grad_probs = product("rnqhc,rnkhc->rnhqk", grad_att, values)
    grad_scores = probs_f * (grad_probs - jnp.sum(probs_f * grad_probs, axis=-1, keepdims=True))
    grad_bias = jnp.sum(grad_scores * keep_mask[:, :, None, None, None], axis=1)
    grad_scores_b = grad_scores.astype(jnp.bfloat16)
    grad_query = product("rnhqk,rnkhc->rnqhc", grad_scores_b, key_cells) * q_scale
    grad_keys = product("rnhqk,rnqhc->rnkhc", grad_scores_b, query)
    grad_values = product("rnhqk,rnqhc->rnkhc", probs_b, grad_att)
    flat_shape = (n_rows, n_win, n_tok, model_width)
    grad_cells = jnp.concatenate(
        [
            grad_query.reshape(flat_shape),
            grad_keys.reshape(flat_shape),
            grad_values.reshape(flat_shape),
        ],
        axis=-1,
    ).astype(jnp.bfloat16)
    grad_qkv = product("rntd,rnte->de", normed_a_b * keep_b, grad_cells)
    grad_in = product("rnte,de->rntd", grad_cells, w_qkv)
    grad_tokens = (grad_hidden + norm_back(normed_a, inv_a, grad_in)).astype(jnp.bfloat16)
    return (output, grad_tokens, (grad_qkv, grad_proj, grad_up, grad_down), grad_bias)


def local(tokens, cotangent, w_qkv, w_proj, w_up, w_down, bias_table, band_rows, lon_shift):
    levels, lat_cells, lon_cells, model_width = tokens.shape
    n_slots = lat_cells // WH
    n_own = lon_cells // WW
    latwin = bias_table.shape[0]
    lat_index = lax.axis_index("lat")
    band_ends = jnp.cumsum(band_rows)
    band_starts = band_ends - band_rows
    my_count = band_rows[lat_index]
    my_start = band_starts[lat_index]
    slot_ids = jnp.arange(n_slots, dtype=jnp.int32)
    live_rows = slot_ids < my_count
    row_ids = jnp.minimum(my_start + slot_ids, latwin - 1)
    spread = offset_table()
    stacked = jnp.stack([tokens, cotangent])
    global_ids = jnp.arange(latwin, dtype=jnp.int32)
    work_cells = n_slots * WH
    offsets = jnp.take(lon_shift, row_ids, axis=0)
    bias = make_bias(jnp.take(bias_table, row_ids, axis=0), spread)
    edge_cols = from_behind(stacked, "lon", -1)
    joined = jnp.concatenate([stacked, edge_cols], axis=3)
    framed = slice_rows(joined, offsets, n_slots, n_own * WW)
    counted = jnp.ones((n_own,), jnp.bool_)
    keep_mask = (live_rows[:, None] & counted[None, :]).astype(jnp.float32)
    out_win, grad_win, grad_sums, grad_bias = window_pass(
        to_windows(framed[0], n_slots, n_own),
        to_windows(framed[1], n_slots, n_own),
        bias,
        keep_mask,
        w_qkv,
        w_proj,
        w_up,
        w_down,
    )
    live_b = live_rows[:, None, None, None].astype(jnp.bfloat16)
    results = jnp.stack([from_windows(out_win * live_b), from_windows(grad_win * live_b)])
    blank = jnp.zeros((2, levels, work_cells, lon_cells + WW, model_width), jnp.bfloat16)
    placed = place_rows(blank, results, offsets, n_slots)
    back_cols = from_behind(placed[:, :, :, lon_cells:], "lon", 1)
    own_cells = jnp.concatenate(
        [placed[:, :, :, :WW] + back_cols, placed[:, :, :, WW:lon_cells]], axis=3
    )
    scale_grad = float(latwin * WH * levels * lon_cells * lax.axis_size("lon")) ** (-0.5)
    slab = table_grad(grad_bias, spread)
    onehot = ((global_ids[:, None] == row_ids[None, :]) & live_rows[None, :]).astype(jnp.float32)
    sum_qkv, sum_proj, sum_up, sum_down = grad_sums
    lon_parts = (
        lax.psum_scatter(
            sum_qkv.astype(jnp.bfloat16), "lon", scatter_dimension=1, tiled=True
        ).astype(jnp.float32),
        lax.psum_scatter(
            sum_proj.astype(jnp.bfloat16), "lon", scatter_dimension=1, tiled=True
        ).astype(jnp.float32),
        lax.psum_scatter(
            sum_up.astype(jnp.bfloat16), "lon", scatter_dimension=1, tiled=True
        ).astype(jnp.float32),
        lax.psum_scatter(
            sum_down.astype(jnp.bfloat16), "lon", scatter_dimension=1, tiled=True
        ).astype(jnp.float32),
        lax.psum_scatter(slab.astype(jnp.bfloat16), "lon", scatter_dimension=1, tiled=True).astype(
            jnp.float32
        ),
    )
    rows_full = jnp.dot(onehot, lon_parts[4], precision=lax.Precision.HIGHEST)
    final_parts = (
        lax.psum_scatter(
            lon_parts[0].astype(jnp.bfloat16), "lat", scatter_dimension=0, tiled=True
        ).astype(jnp.float32),
        lax.psum_scatter(
            lon_parts[1].astype(jnp.bfloat16), "lat", scatter_dimension=0, tiled=True
        ).astype(jnp.float32),
        lax.psum_scatter(
            lon_parts[2].astype(jnp.bfloat16), "lat", scatter_dimension=0, tiled=True
        ).astype(jnp.float32),
        lax.psum_scatter(
            lon_parts[3].astype(jnp.bfloat16), "lat", scatter_dimension=0, tiled=True
        ).astype(jnp.float32),
        lax.psum_scatter(
            rows_full.astype(jnp.bfloat16), "lat", scatter_dimension=0, tiled=True
        ).astype(jnp.float32),
    )
    table_part = final_parts[4]
    return (
        own_cells[0],
        own_cells[1],
        final_parts[0] * scale_grad,
        final_parts[1] * scale_grad,
        final_parts[2] * scale_grad,
        final_parts[3] * scale_grad,
        table_part,
    )


def solution(mesh):
    return jax.shard_map(
        local,
        mesh=mesh,
        in_specs=(
            P(None, "lat", "lon", None),
            P(None, "lat", "lon", None),
            P(),
            P(),
            P(),
            P(),
            P(),
            P(),
            P(),
        ),
        out_specs=(
            P(None, "lat", "lon", None),
            P(None, "lat", "lon", None),
            P("lat", "lon"),
            P("lat", "lon"),
            P("lat", "lon"),
            P("lat", "lon"),
            P("lat", "lon"),
        ),
        check_vma=False,
    )
```

profile of v0, /device:TPU:1, one launch (start us, length us, event | category | flops | bytes accessed | tf_op | source)
XLA Modules:
  0.0 732.4 jit_solution(13398772738582957972)
XLA Ops:
  9.8 12.9 %collective-permute-start = (bf16[2,2,24,12,192]{4,2,3,1,0:T(8,128)(2,1)S(1)}, bf16[2,2,24,12,192]{4,2,3,1,0:T(8,128)(2,1)S(1)}, u32[]{:S(2)}, u32[]{:S(2)}) collective-permute-start(bf16[2,2,24,12,192]{4,2,3,1,0:T(8,128)(2,1)S(1)} %copy.139), channel_id=1, source_target_pairs={{0,496},{16,0},{32,16},{48,32},{64,48},{80,64},{96,80},{112,96},{1... | collective-permute-start | bytes 1327112 | tf_op jit(solution)/shard_map/ppermute | solution.py:20
  37.7 11.4 %convolution_bitcast_fusion = f32[4,6,2,6,12,2,6,12]{7,3,6,2,5,1,0,4:T(8,128)} fusion(bf16[4,6,2,2,6,6,23]{6,5,4,3,2,1,0:T(8,128)(2,1)S(1)} %gather.19, pred[4]{0:T(512)(128)(4,1)S(1)} %compare_and_fusion, s32[12,12]{1,0:T(8,128)S(1)} %subtract_add_fusion), kind=kOutput, calls=%fused_computation.8 | convolution fusion | flops 22975344 | bytes 2150212 | tf_op jit(solution)/shard_map/rhabcde,epq->rhbdpacq/dot_general | solution.py:39
  49.0 36.6 %copy.191 = f32[4,6,2,6,12,2,6,12]{4,3,2,7,6,5,1,0:T(8,128)} copy(f32[4,6,2,6,12,2,6,12]{7,3,6,2,5,1,0,4:T(8,128)} %convolution_bitcast_fusion) | data formatting | bytes 3981312 | tf_op jit(solution)/shard_map/broadcast_in_dim;reshape | solution.py:121
  85.6 20.0 %reshape.591 = f32[4,6,144,144]{2,3,1,0:T(8,128)} reshape(f32[4,6,2,6,12,2,6,12]{4,3,2,7,6,5,1,0:T(8,128)} %copy.191) | data formatting | bytes 3981312 | tf_op jit(solution)/shard_map/broadcast_in_dim;reshape | solution.py:121
  113.9 2.8 convolution_add_fusion
  116.7 2.8 fusion.81
  119.6 4.8 bitcast_multiply_fusion
  131.2 4.9 convolution_convert_fusion
  136.1 3.2 multiply_reduce_fusion
  139.4 2.9 broadcast_multiply_fusion
  155.3 52.7 %fusion.76 = (bf16[192,24]{0,1:T(8,128)(2,1)S(1)}, bf16[192,8]{0,1:T(8,128)(2,1)S(1)}, bf16[768,8]{0,1:T(8,128)(2,1)S(1)}) fusion(bf16[192,576]{0,1:T(8,128)(2,1)} %fusion.15, bf16[192,192]{0,1:T(8,128)(2,1)S(1)} %fusion.22, bf16[768,192]{0,1:T(8,128)(2,1)} %fusion.16), kind=kCustom, calls=%all-reduce-scatter.3 | all-reduce-scatter fusion | flops 393218 | bytes 616448
  209.3 7.9 %collective-permute-start.23 = (bf16[768,8]{0,1:T(8,128)(2,1)S(1)}, bf16[768,8]{0,1:T(8,128)(2,1)S(1)}, u32[]{:S(2)}, u32[]{:S(2)}) collective-permute-start(bf16[768,8]{0,1:T(8,128)(2,1)S(1)} %get-tuple-element.76), channel_id=1, source_target_pairs={{0,96},{16,112},{32,128},{48,144},{64,160},{80,176},{96,192},{112,... | collective-permute-start | bytes 36872
  217.3 6.2 collective-permute-start.22
  223.4 3.1 collective-permute-start.21
  228.7 9.1 %collective-permute-start.25 = (bf16[768,6]{0,1:T(8,128)(2,1)S(1)}, bf16[768,6]{0,1:T(8,128)(2,1)S(1)}, u32[]{:S(2)}, u32[]{:S(2)}) collective-permute-start(bf16[768,6]{0,1:T(8,128)(2,1)S(1)} %slice.95), channel_id=1, source_target_pairs={{0,128},{16,144},{32,160},{48,176},{64,192},{80,208},{96,224},{112... | collective-permute-start | bytes 27656
  240.0 4.4 collective-permute-start.19
  246.7 37.7 %while.1 = (s32[]{:T(128)}, bf16[4,2,2,6,24,192]{5,4,3,0,2,1:T(8,128)(2,1)S(1)}, s32[4,6]{1,0:T(4,128)}, bf16[4,2,2,6,12,192]{5,4,3,2,1,0:T(8,128)(2,1)S(1)}, s32[]{:T(128)}, /*index=5*/s32[6]{0:T(128)S(1)}, s32[]{:T(128)}) while((s32[]{:T(128)}, bf16[4,2,2,6,24,192]{5,4,3,0,2,1:T(8,128)(2,1)S(1)}, s32[4,6]{1,0:T(4,128)}, ...), condition=%wide.while_cond, body=%wide.while_body.sunk | while | flops 55321 | bytes 553259 | solution.py:83
  248.0 3.9 concatenate.38
  257.4 3.9 concatenate.38
  266.8 3.9 concatenate.38
  276.3 3.9 concatenate.38
  284.4 18.5 %reshape.592 = f32[4,6,2,6,12,2,6,12]{4,3,2,7,6,5,1,0:T(8,128)} reshape(f32[4,6,144,144]{2,3,1,0:T(8,128)} %get-tuple-element.85) | data formatting | bytes 3981312 | tf_op jit(solution)/shard_map/reshape | solution.py:45
  302.9 38.2 %copy.176 = f32[4,6,2,6,12,2,6,12]{7,6,4,5,3,2,1,0:T(8,128)} copy(f32[4,6,2,6,12,2,6,12]{4,3,2,7,6,5,1,0:T(8,128)} %reshape.592) | data formatting | bytes 3981312 | tf_op jit(solution)/shard_map/reshape | solution.py:45
  341.2 12.7 %collective-permute-start.16 = (bf16[192,8]{0,1:T(8,128)(2,1)S(1)}, bf16[192,8]{0,1:T(8,128)(2,1)S(1)}, u32[]{:S(2)}, u32[]{:S(2)}) collective-permute-start(bf16[192,8]{0,1:T(8,128)(2,1)S(1)} %get-tuple-element.75), channel_id=1, source_target_pairs={{0,112},{16,128},{32,144},{48,160},{64,176},{80,192},{96,208},{112... | collective-permute-start | bytes 9224
  353.9 2.8 collective-permute-start.15
  366.5 21.6 %fusion.11 = bf16[4,6,2,2,6,6,23]{6,4,2,5,3,1,0:T(8,128)(2,1)S(1)} fusion(f32[4,6,2,6,12,2,6,12]{7,6,4,5,3,2,1,0:T(8,128)} %copy.176, s32[12,12]{1,0:T(8,128)S(1)} %subtract_add_fusion), kind=kOutput, calls=%fused_computation.27 | convolution fusion | flops 137438064 | bytes 2150208 | tf_op jit(solution)/shard_map/rhbdpacq,epq->rhabcde/dot_general | solution.py:46
  389.6 3.1 convert_element_type.218
  396.8 11.4 %collective-permute-start.8 = (bf16[192,24]{0,1:T(8,128)(2,1)S(1)}, bf16[192,24]{0,1:T(8,128)(2,1)S(1)}, u32[]{:S(2)}, u32[]{:S(2)}) collective-permute-start(bf16[192,24]{0,1:T(8,128)(2,1)S(1)} %get-tuple-element.74), channel_id=1, source_target_pairs={{0,112},{16,128},{32,144},{48,160},{64,176},{80,192},{96,208},{112... | collective-permute-start | bytes 27656
  408.2 2.9 collective-permute-start.7
  429.8 27.6 %reduce-scatter.17.cloned.1.call-done = bf16[48,6]{1,0:T(8,128)(2,1)} async-done(((bf16[768,6]{1,0:T(8,128)(2,1)}), bf16[48,6]{1,0:T(8,128)(2,1)}) %reduce-scatter.17.cloned.1.call-update) | async-done | bytes 592
  458.8 175.7 %all-reduce.15.cloned.1.call-done = bf16[4,19872]{1,0:T(4,128)(2,1)} async-done(((bf16[4,19872]{1,0:T(4,128)(2,1)}), bf16[4,19872]{1,0:T(4,128)(2,1)}) %all-reduce.15.cloned.1.call-update) | async-done | bytes 158992
  638.4 83.5 %all-reduce.11 = (bf16[192,18]{0,1:T(8,128)(2,1)S(1)}, bf16[192,6]{0,1:T(8,128)(2,1)S(1)}, bf16[192,24]{0,1:T(8,128)(2,1)S(1)}, bf16[32,621]{1,0:T(8,128)(2,1)S(1)}) all-reduce(bf16[192,18]{0,1:T(8,128)(2,1)S(1)} %constant_dynamic-slice_fusion.3, ...), channel_id=3, replica_groups=mesh['lon'=32,'lat'=16] {'lat'}, use_global_device_ids=true, to_apply=%region_14.15.clone | all-reduce | flops 29088 | bytes 116352
  (259 shorter events, 113.0 us)
Async XLA Ops:
  8.0 449.4 %reduce-scatter.17.cloned.1.call-start = ((), (), s32[]{:S(2)}) async-start(), calls=%async_computation.3 | async-start | bytes 208896
  9.8 98.4 %collective-permute-start = (bf16[2,2,24,12,192]{4,2,3,1,0:T(8,128)(2,1)S(1)}, bf16[2,2,24,12,192]{4,2,3,1,0:T(8,128)(2,1)S(1)}, u32[]{:S(2)}, u32[]{:S(2)}) collective-permute-start(bf16[2,2,24,12,192]{4,2,3,1,0:T(8,128)(2,1)S(1)} %copy.139), channel_id=1, source_target_pairs={{0,496},{16,0},{32,16},{48,32},{64,48},{80,64},{96,80},{112,96},{1... | collective-permute-start | bytes 1327112 | tf_op jit(solution)/shard_map/ppermute | solution.py:20
  23.9 95.6 %copy-start.35 = (bf16[4]{0:T(256)(128)(2,1)}, bf16[4]{0:T(256)(128)(2,1)S(1)}, u32[]{:S(2)}) copy-start(bf16[4]{0:T(256)(128)(2,1)S(1)} %convert_convert_fusion) | copy-start | bytes 28
  208.0 31.9 %collective-permute-start.24 = (bf16[768,8]{0,1:T(8,128)(2,1)S(1)}, bf16[768,8]{0,1:T(8,128)(2,1)S(1)}, u32[]{:S(2)}, u32[]{:S(2)}) collective-permute-start(bf16[768,8]{0,1:T(8,128)(2,1)S(1)} %get-tuple-element.76), channel_id=1, source_target_pairs={{0,112},{16,128},{32,144},{48,160},{64,176},{80,192},{96,208},{112... | collective-permute-start | bytes 36872
  209.3 35.1 %collective-permute-start.23 = (bf16[768,8]{0,1:T(8,128)(2,1)S(1)}, bf16[768,8]{0,1:T(8,128)(2,1)S(1)}, u32[]{:S(2)}, u32[]{:S(2)}) collective-permute-start(bf16[768,8]{0,1:T(8,128)(2,1)S(1)} %get-tuple-element.76), channel_id=1, source_target_pairs={{0,96},{16,112},{32,128},{48,144},{64,160},{80,176},{96,192},{112,... | collective-permute-start | bytes 36872
  217.3 123.9 %collective-permute-start.22 = (bf16[768,8]{0,1:T(8,128)(2,1)S(1)}, bf16[768,8]{0,1:T(8,128)(2,1)S(1)}, u32[]{:S(2)}, u32[]{:S(2)}) collective-permute-start(bf16[768,8]{0,1:T(8,128)(2,1)S(1)} %get-tuple-element.76), channel_id=1, source_target_pairs={{0,80},{16,96},{32,112},{48,128},{64,144},{80,160},{96,176},{112,1... | collective-permute-start | bytes 36872
  223.4 130.5 %collective-permute-start.21 = (bf16[768,8]{0,1:T(8,128)(2,1)S(1)}, bf16[768,8]{0,1:T(8,128)(2,1)S(1)}, u32[]{:S(2)}, u32[]{:S(2)}) collective-permute-start(bf16[768,8]{0,1:T(8,128)(2,1)S(1)} %get-tuple-element.76), channel_id=1, source_target_pairs={{0,64},{16,80},{32,96},{48,112},{64,128},{80,144},{96,160},{112,17... | collective-permute-start | bytes 36872
  228.7 10.0 %collective-permute-start.25 = (bf16[768,6]{0,1:T(8,128)(2,1)S(1)}, bf16[768,6]{0,1:T(8,128)(2,1)S(1)}, u32[]{:S(2)}, u32[]{:S(2)}) collective-permute-start(bf16[768,6]{0,1:T(8,128)(2,1)S(1)} %slice.95), channel_id=1, source_target_pairs={{0,128},{16,144},{32,160},{48,176},{64,192},{80,208},{96,224},{112... | collective-permute-start | bytes 27656
  238.7 118.0 %collective-permute-start.20 = (bf16[768,8]{0,1:T(8,128)(2,1)S(1)}, bf16[768,8]{0,1:T(8,128)(2,1)S(1)}, u32[]{:S(2)}, u32[]{:S(2)}) collective-permute-start(bf16[768,8]{0,1:T(8,128)(2,1)S(1)} %get-tuple-element.76), channel_id=1, source_target_pairs={{0,48},{16,64},{32,80},{48,96},{64,112},{80,128},{96,144},{112,160... | collective-permute-start | bytes 36872
  240.0 118.8 %collective-permute-start.19 = (bf16[768,8]{0,1:T(8,128)(2,1)S(1)}, bf16[768,8]{0,1:T(8,128)(2,1)S(1)}, u32[]{:S(2)}, u32[]{:S(2)}) collective-permute-start(bf16[768,8]{0,1:T(8,128)(2,1)S(1)} %get-tuple-element.76), channel_id=1, source_target_pairs={{0,32},{16,48},{32,64},{48,80},{64,96},{80,112},{96,128},{112,144}... | collective-permute-start | bytes 36872
  244.4 116.2 %collective-permute-start.18 = (bf16[768,8]{0,1:T(8,128)(2,1)S(1)}, bf16[768,8]{0,1:T(8,128)(2,1)S(1)}, u32[]{:S(2)}, u32[]{:S(2)}) collective-permute-start(bf16[768,8]{0,1:T(8,128)(2,1)S(1)} %get-tuple-element.76), channel_id=1, source_target_pairs={{0,16},{16,32},{32,48},{48,64},{64,80},{80,96},{96,112},{112,128},... | collective-permute-start | bytes 36872
  341.2 51.5 %collective-permute-start.16 = (bf16[192,8]{0,1:T(8,128)(2,1)S(1)}, bf16[192,8]{0,1:T(8,128)(2,1)S(1)}, u32[]{:S(2)}, u32[]{:S(2)}) collective-permute-start(bf16[192,8]{0,1:T(8,128)(2,1)S(1)} %get-tuple-element.75), channel_id=1, source_target_pairs={{0,112},{16,128},{32,144},{48,160},{64,176},{80,192},{96,208},{112... | collective-permute-start | bytes 9224
  353.9 40.9 %collective-permute-start.15 = (bf16[192,8]{0,1:T(8,128)(2,1)S(1)}, bf16[192,8]{0,1:T(8,128)(2,1)S(1)}, u32[]{:S(2)}, u32[]{:S(2)}) collective-permute-start(bf16[192,8]{0,1:T(8,128)(2,1)S(1)} %get-tuple-element.75), channel_id=1, source_target_pairs={{0,96},{16,112},{32,128},{48,144},{64,160},{80,176},{96,192},{112,... | collective-permute-start | bytes 9224
  356.7 40.1 %collective-permute-start.14 = (bf16[192,8]{0,1:T(8,128)(2,1)S(1)}, bf16[192,8]{0,1:T(8,128)(2,1)S(1)}, u32[]{:S(2)}, u32[]{:S(2)}) collective-permute-start(bf16[192,8]{0,1:T(8,128)(2,1)S(1)} %get-tuple-element.75), channel_id=1, source_target_pairs={{0,80},{16,96},{32,112},{48,128},{64,144},{80,160},{96,176},{112,1... | collective-permute-start | bytes 9224
  358.8 49.4 %collective-permute-start.13 = (bf16[192,8]{0,1:T(8,128)(2,1)S(1)}, bf16[192,8]{0,1:T(8,128)(2,1)S(1)}, u32[]{:S(2)}, u32[]{:S(2)}) collective-permute-start(bf16[192,8]{0,1:T(8,128)(2,1)S(1)} %get-tuple-element.75), channel_id=1, source_target_pairs={{0,64},{16,80},{32,96},{48,112},{64,128},{80,144},{96,160},{112,17... | collective-permute-start | bytes 9224
  360.7 3.8 collective-permute-start.17
  364.4 270.1 %all-reduce.15.cloned.1.call-start = ((), (), s32[]{:S(2)}) async-start(), calls=%async_computation.4 | async-start | bytes 319488
  364.4 46.7 %collective-permute-start.12 = (bf16[192,8]{0,1:T(8,128)(2,1)S(1)}, bf16[192,8]{0,1:T(8,128)(2,1)S(1)}, u32[]{:S(2)}, u32[]{:S(2)}) collective-permute-start(bf16[192,8]{0,1:T(8,128)(2,1)S(1)} %get-tuple-element.75), channel_id=1, source_target_pairs={{0,48},{16,64},{32,80},{48,96},{64,112},{80,128},{96,144},{112,160... | collective-permute-start | bytes 9224
  392.6 245.7 %reduce-scatter.15.cloned.1.call-start = ((), (), s32[]{:S(2)}) async-start(), calls=%async_computation.2 | async-start | bytes 405504 | tf_op jit(solution)/shard_map/reduce_scatter | solution.py:222
  392.7 22.4 %collective-permute-start.11 = (bf16[192,8]{0,1:T(8,128)(2,1)S(1)}, bf16[192,8]{0,1:T(8,128)(2,1)S(1)}, u32[]{:S(2)}, u32[]{:S(2)}) collective-permute-start(bf16[192,8]{0,1:T(8,128)(2,1)S(1)} %get-tuple-element.75), channel_id=1, source_target_pairs={{0,32},{16,48},{32,64},{48,80},{64,96},{80,112},{96,128},{112,144}... | collective-permute-start | bytes 9224
  394.8 22.3 %collective-permute-start.10 = (bf16[192,8]{0,1:T(8,128)(2,1)S(1)}, bf16[192,8]{0,1:T(8,128)(2,1)S(1)}, u32[]{:S(2)}, u32[]{:S(2)}) collective-permute-start(bf16[192,8]{0,1:T(8,128)(2,1)S(1)} %get-tuple-element.75), channel_id=1, source_target_pairs={{0,16},{16,32},{32,48},{48,64},{64,80},{80,96},{96,112},{112,128},... | collective-permute-start | bytes 9224
  396.8 25.3 %collective-permute-start.8 = (bf16[192,24]{0,1:T(8,128)(2,1)S(1)}, bf16[192,24]{0,1:T(8,128)(2,1)S(1)}, u32[]{:S(2)}, u32[]{:S(2)}) collective-permute-start(bf16[192,24]{0,1:T(8,128)(2,1)S(1)} %get-tuple-element.74), channel_id=1, source_target_pairs={{0,112},{16,128},{32,144},{48,160},{64,176},{80,192},{96,208},{112... | collective-permute-start | bytes 27656
  408.2 15.9 %collective-permute-start.7 = (bf16[192,24]{0,1:T(8,128)(2,1)S(1)}, bf16[192,24]{0,1:T(8,128)(2,1)S(1)}, u32[]{:S(2)}, u32[]{:S(2)}) collective-permute-start(bf16[192,24]{0,1:T(8,128)(2,1)S(1)} %get-tuple-element.74), channel_id=1, source_target_pairs={{0,96},{16,112},{32,128},{48,144},{64,160},{80,176},{96,192},{112,... | collective-permute-start | bytes 27656
  411.1 8.9 %collective-permute-start.9 = (bf16[192,18]{0,1:T(8,128)(2,1)S(1)}, bf16[192,18]{0,1:T(8,128)(2,1)S(1)}, u32[]{:S(2)}, u32[]{:S(2)}) collective-permute-start(bf16[192,18]{0,1:T(8,128)(2,1)S(1)} %slice.93), channel_id=1, source_target_pairs={{0,128},{16,144},{32,160},{48,176},{64,192},{80,208},{96,224},{112... | collective-permute-start | bytes 20744
  414.5 220.0 %copy-start.29 = (pred[4]{0:T(512)(128)(4,1)S(1)}, pred[4]{0:T(512)(128)(4,1)}, u32[]{:S(2)}) copy-start(pred[4]{0:T(512)(128)(4,1)} %iota_compare_fusion.2) | copy-start | bytes 16
  414.5 220.0 %copy-start.30 = (s32[4]{0:T(128)S(1)}, s32[4]{0:T(128)}, u32[]{:S(2)}) copy-start(s32[4]{0:T(128)} %add_minimum_fusion) | copy-start | bytes 52
  415.1 11.3 %collective-permute-start.6 = (bf16[192,24]{0,1:T(8,128)(2,1)S(1)}, bf16[192,24]{0,1:T(8,128)(2,1)S(1)}, u32[]{:S(2)}, u32[]{:S(2)}) collective-permute-start(bf16[192,24]{0,1:T(8,128)(2,1)S(1)} %get-tuple-element.74), channel_id=1, source_target_pairs={{0,80},{16,96},{32,112},{48,128},{64,144},{80,160},{96,176},{112,1... | collective-permute-start | bytes 27656
  417.1 11.5 %collective-permute-start.5 = (bf16[192,24]{0,1:T(8,128)(2,1)S(1)}, bf16[192,24]{0,1:T(8,128)(2,1)S(1)}, u32[]{:S(2)}, u32[]{:S(2)}) collective-permute-start(bf16[192,24]{0,1:T(8,128)(2,1)S(1)} %get-tuple-element.74), channel_id=1, source_target_pairs={{0,64},{16,80},{32,96},{48,112},{64,128},{80,144},{96,160},{112,17... | collective-permute-start | bytes 27656
  420.0 8.6 %collective-permute-start.4 = (bf16[192,24]{0,1:T(8,128)(2,1)S(1)}, bf16[192,24]{0,1:T(8,128)(2,1)S(1)}, u32[]{:S(2)}, u32[]{:S(2)}) collective-permute-start(bf16[192,24]{0,1:T(8,128)(2,1)S(1)} %get-tuple-element.74), channel_id=1, source_target_pairs={{0,48},{16,64},{32,80},{48,96},{64,112},{80,128},{96,144},{112,160... | collective-permute-start | bytes 27656
  422.1 6.5 collective-permute-start.3
  424.2 4.5 collective-permute-start.2
  426.4 209.0 %collective-permute-start.1 = (bf16[2,2,24,12,192]{4,2,3,1,0:T(8,128)(2,1)S(1)}, bf16[2,2,24,12,192]{4,2,3,1,0:T(8,128)(2,1)}, u32[]{:S(2)}, u32[]{:S(2)}) collective-permute-start(bf16[2,2,24,12,192]{4,2,3,1,0:T(8,128)(2,1)S(1)} %copy.171), channel_id=1, source_target_pairs={{0,16},{16,32},{32,48},{48,64},{64,80},{80,96},{96,112},{112,128},... | collective-permute-start | bytes 1327112 | tf_op jit(solution)/shard_map/ppermute | solution.py:20
  (36 other events, 551.4 us)
Sparse Core Ops, SparseCore 0:
  364.5 92.8 reduce-scatter.16
  460.2 111.7 reduce-scatter.14
Sparse Core Ops, SparseCore 1:
  392.7 241.7 all-reduce.14
where the time goes:
time: 746 us; the launch traced here: 732 us
  waiting for transfers between devices  204 us (27%)
  local copies, waits for them, and re-layouts  172 us (23%)
  blocking collectives  136 us (18%)
  starting transfers between devices  105 us (14%)
  matrix products  65.1 us (9%)
  other arithmetic  30.7 us (4%)
  between operations  20.2 us (3%)
    unnamed x29, waiting for transfers between devices  204 us
    unnamed x2, blocking collectives  136 us
    unnamed x26, starting transfers between devices  89.5 us
    reshape x2, local copies, waits for them, and re-layouts, table_grad(): shaped = grad_bias.reshape(n_rows, HEADS, WZ, WH, WW, WZ, WH, WW)  56.7 us
    another operation x2, local copies, waits for them, and re-layouts, window_pass(): scores = product('rnqhc,rnkhc->rnhqk', query, key_cells) + bias[:, None]  56.6 us
    dot_general x18, matrix products, product(): return jnp.einsum(form, left, right, preferred_element_type=jnp.float32)  31.3 us
    scatter x16, local copies, waits for them, and re-layouts  27.3 us
    dot_general x1, matrix products, table_grad(): jnp.einsum('rhbdpacq,epq->rhabcde', shaped, spread, precision=lax.Precisi...  21.6 us
  transfers between devices with their start and end apart: 29, of which 3 were waited for; matrix products, arithmetic and copies ran while one was open for 30% of the time, Pallas kernels for 0%

commit v1 on v0

v1 whole, which is shorter than its diff:
```python
import functools

import jax
import jax.numpy as jnp
import numpy as np
from jax import lax
from jax.experimental import pallas as pl
from jax.experimental.pallas import tpu as pltpu
from jax.sharding import PartitionSpec as P

HEADS = 6
HEAD = 32
WIDTH = 192
HID = 768
WH = 6
WW = 12
LEVELS = 2
SLOTS = 4
WTOK = 144
CELL_ROWS = 72
POS = 3312
SPAN = 23
LEFT = 5
RIGHT = 6
LAT = 24
NLAT = 16
NLON = 32
ALL_Q = HEADS * WTOK
GROUP = 4
PARTS = WW // GROUP
LANES_V = 384

bf16 = jnp.bfloat16
f32 = jnp.float32
epsilon = 1e-05

NN = (((1,), (0,)), ((), ()))
NT = (((1,), (1,)), ((), ()))


def mm(left, right, dims=NN):
    return lax.dot_general(left, right, dims, preferred_element_type=f32)


def one_hot(condition):
    return jnp.where(condition, 1.0, 0.0).astype(bf16)


def eye(count):
    rows = lax.broadcasted_iota(jnp.int32, (count, count), 0)
    cols = lax.broadcasted_iota(jnp.int32, (count, count), 1)
    return one_hot(rows == cols)


def spread_table():
    table = np.zeros((PARTS, LANES_V, WTOK), np.float32)
    for part in range(PARTS):
        for level in range(LEVELS):
            for row in range(WH):
                for col in range(WW):
                    e = col - GROUP * part + WW - GROUP
                    table[part, (level * WH + row) * SPAN + e, level * 72 + col * WH + row] = 1
    return table


def regroup_table():
    table = np.zeros((288, 288), np.float32)
    for head_level in range(12):
        for step in range(GROUP):
            for row in range(WH):
                table[(head_level * GROUP + step) * WH + row, step * 72 + head_level * WH + row] = 1
    return table


def entry_table():
    table = np.zeros((288, 288), np.float32)
    for head in range(HEADS):
        for zk in range(LEVELS):
            for zq in range(LEVELS):
                for hk in range(WH):
                    for half in range(2):
                        entry = (((head * 2 + zk) * 2 + zq) * WH + hk) * 2 + half
                        chunk, place = entry // 9, entry % 9
                        source = (zq * 2 + half) * 72 + (head * 2 + zk) * WH + hk
                        table[place * NLON + chunk, source] = 1
    return table


def layer_norm(x):
    centre = jnp.sum(x, axis=0, keepdims=True) * (1.0 / WIDTH)
    shifted = x - centre
    var = jnp.sum(shifted * shifted, axis=0, keepdims=True) * (1.0 / WIDTH)
    inv = lax.rsqrt(var + epsilon)
    return shifted * inv, inv


def norm_back(normed, inv, grad):
    mean_grad = jnp.sum(grad, axis=0, keepdims=True) * (1.0 / WIDTH)
    mean_proj = jnp.sum(grad * normed, axis=0, keepdims=True) * (1.0 / WIDTH)
    return inv * (grad - mean_grad - normed * mean_proj)


def bias_kernel(rows_ref, spread_ref, regroup_ref, bias_ref):
    regroup = regroup_ref[...]
    for slot in range(SLOTS):
        rows = rows_ref[slot].astype(f32)
        rows = jnp.concatenate([rows, jnp.zeros((72, LANES_V - 276), f32)], axis=1)
        shifted = [
            rows if step == GROUP - 1 else pltpu.roll(rows, LANES_V - (GROUP - 1 - step), 1)
            for step in range(GROUP)
        ]
        stack = jnp.concatenate(shifted, axis=0).astype(bf16)
        left = mm(regroup, stack).astype(bf16)
        for part in range(PARTS):
            full = mm(left, spread_ref[part])
            for head in range(HEADS):
                for level in range(LEVELS):
                    at = (head * 2 + level) * 24
                    bias_ref[
                        slot,
                        level * 72 + part * 24 : level * 72 + part * 24 + 24,
                        head * WTOK : (head + 1) * WTOK,
                    ] = full[at : at + 24, :]


def diagonal(full):
    return jnp.concatenate(
        [
            full[h * HEAD : (h + 1) * HEAD, h * WTOK : (h + 1) * WTOK]
            for h in range(HEADS)
        ],
        axis=0,
    )


def main_kernel(
    at_ref,
    left_ref,
    own_t_ref,
    own_c_ref,
    right_ref,
    bias_ref,
    wqkv_ref,
    wqkv_t_ref,
    wproj_ref,
    wproj_t_ref,
    wup_ref,
    wup_t_ref,
    wdown_ref,
    wdown_t_ref,
    spread_ref,
    regroup_ref,
    entry_ref,
    out_left_ref,
    out_own_ref,
    out_right_ref,
    wsum_ref,
    tsum_ref,
    x_s,
    c_s,
    ro_s,
    rg_s,
    qm_s,
    gm_s,
    acc_s,
    accd_s,
    ts_s,
    tt_s,
):
    n_left, n_own, n_right = LEFT * LAT, WW * LAT, RIGHT * LAT

    def place(axis):
        shape = (CELL_ROWS, 1) if axis == 0 else (1, CELL_ROWS)
        cell = lax.broadcasted_iota(jnp.int32, shape, axis)
        col = (cell * 43) >> 8
        base = col * LAT + (cell - col * WH)
        return jnp.concatenate([base + at_ref[s] for s in range(SLOTS)], axis=axis)

    goal = place(0)

    def pick(first, count):
        lane = lax.broadcasted_iota(jnp.int32, (288, count), 1)
        return one_hot(goal - first == lane)

    sel_l = pick(0, n_left)
    sel_o = pick(n_left, n_own)
    sel_r = pick(n_left + n_own, n_right)
    for which, own_ref, scratch in ((0, own_t_ref, x_s), (1, own_c_ref, c_s)):
        got = mm(sel_l, left_ref[which]) + mm(sel_o, own_ref[...]) + mm(sel_r, right_ref[which])
        for slot in range(SLOTS):
            for level in range(LEVELS):
                scratch[slot, level * 72 : level * 72 + 72, :] = got[
                    slot * 72 : slot * 72 + 72, level * WIDTH : (level + 1) * WIDTH
                ].astype(scratch.dtype)

    acc_s[...] = jnp.zeros_like(acc_s)
    accd_s[...] = jnp.zeros_like(accd_s)
    qm_s[...] = jnp.zeros_like(qm_s)
    gm_s[...] = jnp.zeros_like(gm_s)
    tt_s[...] = jnp.zeros_like(tt_s)
    eye_d = eye(WIDTH)
    eye_t = eye(WTOK)
    scale = HEAD ** (-0.5)

    def one_slot(slot, carry):
        x = mm(eye_d, x_s[slot].astype(bf16), NT)
        cot = mm(eye_d, c_s[slot].astype(bf16), NT)
        cot_b = cot.astype(bf16)
        na, inv_a = layer_norm(x)
        na_b = na.astype(bf16)
        qkv = mm(wqkv_t_ref[...], na_b)
        q = (qkv[:WIDTH] * scale).astype(bf16)
        k = qkv[WIDTH : 2 * WIDTH].astype(bf16)
        v = qkv[2 * WIDTH :].astype(bf16)
        k_rows = mm(eye_t, k, NT).astype(bf16)
        v_rows = mm(eye_t, v, NT).astype(bf16)
        for h in range(HEADS):
            qm_s[h * HEAD : (h + 1) * HEAD, h * WTOK : (h + 1) * WTOK] = q[
                h * HEAD : (h + 1) * HEAD
            ]
        qm = qm_s[...]
        scores = mm(k_rows, qm) + bias_ref[slot]
        top = jnp.max(scores, axis=0, keepdims=True)
        exps = jnp.exp(scores - top)
        probs = exps * (1.0 / jnp.sum(exps, axis=0, keepdims=True))
        probs_b = probs.astype(bf16)
        att_b = diagonal(mm(v, probs_b)).astype(bf16)
        hidden = x + mm(wproj_t_ref[...], att_b)
        nb, inv_b = layer_norm(hidden)
        nb_b = nb.astype(bf16)
        pre = mm(wup_t_ref[...], nb_b)
        cdf = 0.5 * (1.0 + lax.erf(pre * 0.7071067811865476))
        density = jnp.exp(-0.5 * pre * pre) * 0.3989422804014327
        act_b = (pre * cdf).astype(bf16)
        slope = cdf + pre * density
        out = hidden + mm(wdown_t_ref[...], act_b)
        ro_s[slot] = mm(eye_t, out.astype(bf16), NT)
        gpre_b = (mm(wdown_ref[...], cot_b) * slope).astype(bf16)
        accd_s[...] += mm(act_b, cot_b, NT)
        gh = cot + norm_back(nb, inv_b, mm(wup_ref[...], gpre_b))
        gh_b = gh.astype(bf16)
        acc_s[:, 768:1536] += mm(nb_b, gpre_b, NT)
        acc_s[:, 576:768] += mm(att_b, gh_b, NT)
        ga = mm(wproj_ref[...], gh_b).astype(bf16)
        for h in range(HEADS):
            gm_s[h * HEAD : (h + 1) * HEAD, h * WTOK : (h + 1) * WTOK] = ga[
                h * HEAD : (h + 1) * HEAD
            ]
        gm = gm_s[...]
        gp = mm(v_rows, gm)
        gs = probs * (gp - jnp.sum(probs * gp, axis=0, keepdims=True))
        gs_b = gs.astype(bf16)
        gq = diagonal(mm(k, gs_b)) * scale
        gk = mm(qm, gs_b, NT)
        gv = mm(gm, probs_b, NT)
        gc_b = jnp.concatenate([gq, gk, gv], axis=0).astype(bf16)
        acc_s[:, 0:576] += mm(na_b, gc_b, NT)
        gt = gh + norm_back(na, inv_a, mm(wqkv_ref[...], gc_b))
        rg_s[slot] = mm(eye_t, gt.astype(bf16), NT)

        heads = [gs[:, h * WTOK : (h + 1) * WTOK] for h in range(HEADS)]
        total = None
        for part in range(PARTS):
            rows = jnp.concatenate(
                [
                    piece[level * 72 + part * 24 : level * 72 + part * 24 + 24]
                    for piece in heads
                    for level in range(LEVELS)
                ],
                axis=0,
            ).astype(bf16)
            term = mm(rows, spread_ref[part], NT)
            total = term if total is None else total + term
        steps = lax.dot_general(
            regroup_ref[...],
            total.astype(bf16),
            (((0,), (0,)), ((), ())),
            preferred_element_type=f32,
        )
        table = steps[216:288]
        for step in range(GROUP - 1):
            table = table + pltpu.roll(steps[step * 72 : step * 72 + 72], GROUP - 1 - step, 1)
        for piece in range(4):
            ts_s[slot, piece * 72 : piece * 72 + 72, 0:69] = table[:, piece * 69 : piece * 69 + 69]
        return carry

    lax.fori_loop(0, SLOTS, one_slot, 0)

    for slot in range(SLOTS):
        values = ts_s[slot][:, 0:69].astype(bf16)
        entries = mm(entry_ref[...], values)
        for n in range(9):
            tt_s[pl.ds(slot * 9 + n, NLON, stride=48), 0:69] = entries[n * NLON : (n + 1) * NLON]
    tsum_ref[...] = tt_s[...].reshape(NLON, 48, 128).astype(bf16)

    for i in range(NLAT):
        quarter = [
            acc_s[12 * i : 12 * i + 12, g * 384 : (g + 1) * 384] for g in range(4)
        ]
        wsum_ref[i, :, 0:384] = jnp.concatenate(quarter, axis=0).astype(bf16)
        wsum_ref[i, :, 384:576] = accd_s[48 * i : 48 * i + 48, :].astype(bf16)

    goal_t = place(1)

    def put(first, count):
        row = lax.broadcasted_iota(jnp.int32, (count, 288), 0)
        return one_hot(goal_t - first == row)

    sets = (put(0, n_left), put(n_left, n_own), put(n_left + n_own, n_right))
    for which, scratch in ((0, ro_s), (1, rg_s)):
        rows = []
        for slot in range(SLOTS):
            block = scratch[slot]
            rows.append(jnp.concatenate([block[0:72], block[72:144]], axis=1))
        rows = jnp.concatenate(rows, axis=0).astype(bf16)
        for sel, ref in zip(sets, (out_left_ref, out_own_ref, out_right_ref)):
            ref[which] = mm(sel, rows).astype(bf16)


def column_pieces(z):
    top = [z[g * 12 : g * 12 + 12, 0:384] for g in range(4)]
    qkv = jnp.concatenate([top[0], top[1][:, 0:192]], axis=1)
    proj = top[1][:, 192:384]
    up = jnp.concatenate([top[2], top[3]], axis=1)
    down = z[:, 384:576]
    return ((qkv, 18, 12), (proj, 6, 12), (up, 24, 12), (down, 6, 48))


def mid_kernel(w_ref, t_ref, out_ref, buf):
    z = w_ref[0].astype(f32)
    for i in range(1, NLAT):
        z = z + w_ref[i].astype(f32)
    buf[...] = jnp.zeros_like(buf)
    place = 4
    for piece, each, rows in column_pieces(z):
        cols = piece.shape[1]
        piece = piece.astype(bf16).astype(f32)
        lane = lax.broadcasted_iota(jnp.int32, (rows, cols), 1)
        owner = lax.broadcasted_iota(jnp.int32, (NLON, cols), 0)
        col_of = lax.broadcasted_iota(jnp.int32, (NLON, cols), 1)
        mine = one_hot((col_of >= owner * each) & (col_of < (owner + 1) * each))
        part = lane - each * lax.div(lane, each)
        stack = jnp.concatenate(
            [jnp.where(part == c, piece, 0.0) for c in range(each)]
            + ([jnp.zeros((4, cols), f32)] if (each * rows) % 8 else []),
            axis=0,
        ).astype(bf16)
        flat = mm(mine, stack, NT)
        count = flat.shape[1]
        for first in range(0, count, 128):
            width = min(128, count - first)
            buf[pl.ds(place, NLON, stride=16), 0:width] = flat[:, first : first + width]
            place += 1
    out_ref[:, 0:32, :] = t_ref[:, 0:32, :]
    tail = t_ref[:, 32:48, :].astype(f32) + buf[...].reshape(NLON, 16, 128)
    out_ref[:, 32:48, :] = tail.astype(bf16)


def fin_kernel(scale, go_ref, in_ref, qkv_ref, proj_ref, up_ref, down_ref, route_ref):
    total = in_ref[0].astype(f32)
    for i in range(1, NLON):
        total = total + in_ref[i].astype(f32)
    place = 36
    for ref, each, rows in ((qkv_ref, 18, 12), (proj_ref, 6, 12), (up_ref, 24, 12), (down_ref, 6, 48)):
        count = each * rows
        lines = -(-count // 128)
        flat = jnp.concatenate([total[place + n : place + n + 1] for n in range(lines)], axis=1)
        place += lines
        wide = lines * 128
        row = lax.broadcasted_iota(jnp.int32, (rows, wide), 0)
        lane = lax.broadcasted_iota(jnp.int32, (rows, wide), 1)
        mine = lane - rows * lax.div(lane, rows) == row
        at = lax.broadcasted_iota(jnp.int32, (wide, each), 0)
        col = lax.broadcasted_iota(jnp.int32, (wide, each), 1)
        hot = jnp.where((at >= col * rows) & (at < (col + 1) * rows), 1.0, 0.0)
        spread = jnp.where(mine, jnp.broadcast_to(flat, (rows, wide)), 0.0)
        ref[...] = lax.dot_general(
            spread, hot, NN, precision=lax.Precision.HIGHEST, preferred_element_type=f32
        ) * scale
    table = total[0:36].astype(bf16).astype(f32)
    for i in range(NLAT):
        for j in range(2):
            mine = jnp.zeros((9, 128), f32)
            for slot in range(SLOTS):
                hit = jnp.where(go_ref[slot] == 2 * i + j, 1.0, 0.0)
                mine = mine + hit * table[slot * 9 : slot * 9 + 9]
            route_ref[i, j * 16 : j * 16 + 16, :] = jnp.concatenate(
                [mine, jnp.zeros((7, 128), f32)], axis=0
            ).astype(bf16)


def table_kernel(in_ref, out_ref):
    total = in_ref[0].astype(f32)
    for i in range(1, NLAT):
        total = total + in_ref[i].astype(f32)
    for j in range(2):
        out_ref[j : j + 1, :] = jnp.concatenate(
            [total[j * 16 + n : j * 16 + n + 1, 0:69] for n in range(9)], axis=1
        )


def vmem():
    return pl.BlockSpec(memory_space=pltpu.VMEM)


def smem():
    return pl.BlockSpec(memory_space=pltpu.SMEM)


def params(mib):
    return pltpu.CompilerParams(vmem_limit_bytes=mib * 1024 * 1024)


def pack(grid):
    return grid.transpose(2, 1, 0, 3).reshape(WW, LAT, LEVELS * WIDTH)


def unpack(cells):
    return cells.reshape(WW, LAT, LEVELS, WIDTH).transpose(2, 1, 0, 3)


def to_lon(x, by):
    count = lax.axis_size("lon")
    return lax.ppermute(x, "lon", [(i, (i + by) % count) for i in range(count)])


def table_bias(rows, spread, regroup):
    shaped = rows.reshape(SLOTS, HEADS, 2, 2, WH, WH * SPAN).transpose(0, 1, 2, 4, 3, 5)
    shaped = shaped.reshape(SLOTS, 72, 2 * WH * SPAN)
    return pl.pallas_call(
        bias_kernel,
        out_shape=jax.ShapeDtypeStruct((SLOTS, WTOK, ALL_Q), f32),
        in_specs=[vmem()] * 3,
        out_specs=vmem(),
        compiler_params=params(40),
        cost_estimate=pl.CostEstimate(flops=1000000000, bytes_accessed=6000000, transcendentals=0),
        name="table_bias",
    )(shaped, spread, regroup)


def block_pass(at, left, own_t, own_c, right, bias, weights, spread, regroup, entry):
    return pl.pallas_call(
        main_kernel,
        out_shape=(
            jax.ShapeDtypeStruct((2, LEFT * LAT, 2 * WIDTH), bf16),
            jax.ShapeDtypeStruct((2, WW * LAT, 2 * WIDTH), bf16),
            jax.ShapeDtypeStruct((2, RIGHT * LAT, 2 * WIDTH), bf16),
            jax.ShapeDtypeStruct((NLAT, 48, 576), bf16),
            jax.ShapeDtypeStruct((NLON, 48, 128), bf16),
        ),
        in_specs=[smem()] + [vmem()] * 16,
        out_specs=(vmem(),) * 5,
        scratch_shapes=[
            pltpu.VMEM((SLOTS, WTOK, WIDTH), f32),
            pltpu.VMEM((SLOTS, WTOK, WIDTH), f32),
            pltpu.VMEM((SLOTS, WTOK, WIDTH), f32),
            pltpu.VMEM((SLOTS, WTOK, WIDTH), f32),
            pltpu.VMEM((WIDTH, ALL_Q), bf16),
            pltpu.VMEM((WIDTH, ALL_Q), bf16),
            pltpu.VMEM((WIDTH, 1536), f32),
            pltpu.VMEM((HID, WIDTH), f32),
            pltpu.VMEM((SLOTS, 288, 128), f32),
            pltpu.VMEM((NLON * 48, 128), f32),
        ],
        compiler_params=params(56),
        name="block_pass",
    )(at, left, own_t, own_c, right, bias, *weights, spread, regroup, entry)


def local(tokens, cotangent, w_qkv, w_proj, w_up, w_down, bias_table, band_rows, lon_shift):
    latwin = bias_table.shape[0]
    lat_index = lax.axis_index("lat")
    band_ends = jnp.cumsum(band_rows)
    my_count = band_rows[lat_index]
    my_start = band_ends[lat_index] - my_count
    slot_ids = jnp.arange(SLOTS, dtype=jnp.int32)
    live = slot_ids < my_count
    row_ids = jnp.minimum(my_start + slot_ids, latwin - 1)
    shift = jnp.take(lon_shift, row_ids, axis=0)
    first = jnp.where(shift <= RIGHT, shift, shift - WW) + LEFT
    at = jnp.where(live, first * LAT + slot_ids * WH, -100000)
    go = jnp.where(live, row_ids, -1)

    own_t = pack(tokens)
    own_c = pack(cotangent)
    both = jnp.stack([own_t, own_c])
    left = to_lon(both[:, WW - LEFT :], 1).reshape(2, LEFT * LAT, 2 * WIDTH)
    right = to_lon(both[:, :RIGHT], -1).reshape(2, RIGHT * LAT, 2 * WIDTH)

    spread = jnp.asarray(spread_table(), bf16)
    regroup = jnp.asarray(regroup_table(), bf16)
    entry = jnp.asarray(entry_table(), bf16)
    bias = table_bias(jnp.take(bias_table, row_ids, axis=0), spread, regroup)
    weights = (w_qkv, w_qkv.T, w_proj, w_proj.T, w_up, w_up.T, w_down, w_down.T)
    out_left, out_own, out_right, w_sums, t_sums = block_pass(
        at,
        left,
        own_t.reshape(WW * LAT, 2 * WIDTH),
        own_c.reshape(WW * LAT, 2 * WIDTH),
        right,
        bias,
        weights,
        spread,
        regroup,
        entry,
    )

    from_right = to_lon(out_left.reshape(2, LEFT, LAT, 2 * WIDTH), -1)
    from_left = to_lon(out_right.reshape(2, RIGHT, LAT, 2 * WIDTH), 1)
    own = out_own.reshape(2, WW, LAT, 2 * WIDTH)
    cells = jnp.concatenate(
        [own[:, :RIGHT] + from_left, own[:, RIGHT : WW - LEFT], own[:, WW - LEFT :] + from_right],
        axis=1,
    )
    output, grad_tokens = unpack(cells[0]), unpack(cells[1])

    w_got = lax.all_to_all(w_sums, "lat", 0, 0)
    lon_send = pl.pallas_call(
        mid_kernel,
        out_shape=jax.ShapeDtypeStruct((NLON, 48, 128), bf16),
        in_specs=[vmem()] * 2,
        out_specs=vmem(),
        scratch_shapes=[pltpu.VMEM((NLON * 16, 128), f32)],
        compiler_params=params(40),
        name="sum_lat",
    )(w_got, t_sums)
    lon_got = lax.all_to_all(lon_send, "lon", 0, 0)
    scale_grad = float(latwin * WH * LEVELS * WW * NLON) ** (-0.5)
    grad_qkv, grad_proj, grad_up, grad_down, route = pl.pallas_call(
        functools.partial(fin_kernel, scale_grad),
        out_shape=(
            jax.ShapeDtypeStruct((12, 18), f32),
            jax.ShapeDtypeStruct((12, 6), f32),
            jax.ShapeDtypeStruct((12, 24), f32),
            jax.ShapeDtypeStruct((48, 6), f32),
            jax.ShapeDtypeStruct((NLAT, 32, 128), bf16),
        ),
        in_specs=[smem(), vmem()],
        out_specs=(vmem(),) * 5,
        compiler_params=params(40),
        name="sum_lon",
    )(go, lon_got)
    route_got = lax.all_to_all(route, "lat", 0, 0)
    grad_table = pl.pallas_call(
        table_kernel,
        out_shape=jax.ShapeDtypeStruct((2, 621), f32),
        in_specs=[vmem()],
        out_specs=vmem(),
        compiler_params=params(40),
        name="sum_table",
    )(route_got)
    return (output, grad_tokens, grad_qkv, grad_proj, grad_up, grad_down, grad_table)


def solution(mesh):
    grid = P(None, "lat", "lon", None)
    cut = P("lat", "lon")
    return jax.shard_map(
        local,
        mesh=mesh,
        in_specs=(grid, grid, P(), P(), P(), P(), P(), P(), P()),
        out_specs=(grid, grid, cut, cut, cut, cut, cut),
        check_vma=False,
    )
```

time: 746 us -> 135 us (0.18); the launches traced: 732 us -> 134 us
  waiting for transfers between devices: 204 us -> 21.2 us
  local copies, waits for them, and re-layouts: 172 us -> 16.8 us
  blocking collectives: 136 us -> 23.9 us
  starting transfers between devices: 105 us -> 37.7 us
  matrix products: 65.1 us -> 0 us
  Pallas kernels: 0 us -> 30.3 us
  other arithmetic: 30.7 us -> 2.11 us
  between operations: 20.2 us -> 2.29 us
    unnamed x29 -> x0, waiting for transfers between devices: 204 us -> none
    unnamed x2 -> x0, blocking collectives: 136 us -> none
    unnamed x26 -> x0, starting transfers between devices: 89.5 us -> none
    dot_general x21 -> x0, matrix products: 65.1 us -> none  [the longest x18 31.3 us: product(): return jnp.einsum(form, left, right, preferred_element_type=jnp.float32)]
    reshape x3 -> x2, local copies, waits for them, and re-layouts: 57.1 us -> 0.25 us  [the longest x1 0.16 us: table_bias(): shaped = shaped.reshape(SLOTS, 72, 2 * WH * SPAN)]
    another operation x7, local copies, waits for them, and re-layouts: 58.1 us -> 2.48 us  [the longest x1 0.87 us: local(): own_c.reshape(WW * LAT, 2 * WIDTH)]
    pallas_call x0 -> x5, Pallas kernels: none -> 30.3 us  [the longest x1 24.6 us: block_pass(): pl.pallas_call(main_kernel, out_shape=(jax.ShapeDtypeStruct((2, LEFT * LA...]
    scatter x16 -> x0, local copies, waits for them, and re-layouts: 27.3 us -> none
  transfers between devices with their start and end apart: 29 -> 6, of which waited for: 3 -> 3; matrix products, arithmetic and copies ran while one was open for 30% -> 11% of each run, Pallas kernels for 0% -> 1%
where the time goes in v1:
time: 135 us; the launch traced here: 134 us
  starting transfers between devices  37.7 us (28%)
  Pallas kernels  30.3 us (22%)
  blocking collectives  23.9 us (18%)
  waiting for transfers between devices  21.2 us (16%)
  local copies, waits for them, and re-layouts  16.8 us (12%)
  between operations  2.29 us (2%)
  other arithmetic  2.11 us (2%)
    pallas_call x1, Pallas kernels, block_pass(): pl.pallas_call(main_kernel, out_shape=(jax.ShapeDtypeStruct((2, LEFT * LA...  24.6 us
    all_to_all x1, blocking collectives, local(): w_got = lax.all_to_all(w_sums, 'lat', 0, 0)  23.9 us
    ppermute x4, starting transfers between devices, to_lon(): return lax.ppermute(x, 'lon', [(i, (i + by) % count) for i in range(count)])  22 us
    ppermute x4, waiting for transfers between devices, to_lon(): return lax.ppermute(x, 'lon', [(i, (i + by) % count) for i in range(count)])  16.7 us
    all_to_all x1, starting transfers between devices, local(): lon_got = lax.all_to_all(lon_send, 'lon', 0, 0)  8.34 us
    unnamed x39, local copies, waits for them, and re-layouts  7.72 us
    all_to_all x1, starting transfers between devices, local(): route_got = lax.all_to_all(route, 'lat', 0, 0)  7.31 us
    all_to_all x1, waiting for transfers between devices, local(): route_got = lax.all_to_all(route, 'lat', 0, 0)  4.48 us
  transfers between devices with their start and end apart: 6, of which 3 were waited for; matrix products, arithmetic and copies ran while one was open for 11% of the time, Pallas kernels for 1%

profile of v1, /device:TPU:1, one launch (start us, length us, event | category | flops | bytes accessed | tf_op | source)
XLA Modules:
  0.0 134.4 jit_solution(1505623151357199091)
XLA Ops:
  0.7 1.4 %copy.30 = bf16[12,24,2,192]{3,2,1,0:T(2,128)(2,1)S(1)} copy(bf16[12,24,2,192]{3,1,0,2:T(8,128)(2,1)} %bitcast.33) | data formatting | bytes 442368 | tf_op jit(solution)/shard_map/transpose | solution.py:415
  2.8 0.7 slice.32
  3.6 4.4 %collective-permute-start = (bf16[2,5,24,384]{3,2,1,0:T(8,128)(2,1)}, bf16[2,5,24,384]{3,2,1,0:T(8,128)(2,1)}, u32[]{:S(2)}, u32[]{:S(2)}) collective-permute-start(bf16[2,5,24,384]{3,2,1,0:T(8,128)(2,1)} %slice.32), channel_id=1, source_target_pairs={{0,16},{16,32},{32,48},{48,64},{64,80},{80,96},{96,112},{112,128},... | collective-permute-start | bytes 552968 | tf_op jit(solution)/shard_map/ppermute | solution.py:424
  7.9 0.7 slice.33
  8.7 10.4 %collective-permute-start.1 = (bf16[2,6,24,384]{3,2,1,0:T(8,128)(2,1)}, bf16[2,6,24,384]{3,2,1,0:T(8,128)(2,1)}, u32[]{:S(2)}, u32[]{:S(2)}) collective-permute-start(bf16[2,6,24,384]{3,2,1,0:T(8,128)(2,1)} %slice.33), channel_id=1, source_target_pairs={{0,496},{16,0},{32,16},{48,32},{64,48},{80,64},{96,80},{112,96},{1... | collective-permute-start | bytes 663560 | tf_op jit(solution)/shard_map/ppermute | solution.py:424
  21.6 0.9 reshape_reshape.6.own_t_ref
  22.5 0.9 reshape_reshape.7.own_c_ref
  23.4 0.8 copy.36
  24.8 0.7 gather_fusion.1
  26.7 0.9 copy.35
  27.5 0.9 copy.37
  28.5 0.9 copy.38.wdown_ref
  29.4 1.9 %table_bias.1.bias_ref = f32[4,144,864]{2,1,0:T(8,128)S(1)} custom-call(bf16[4,72,276]{2,1,0:T(8,128)(2,1)S(1)} %reshape.71.rows_ref, bf16[3,384,144]{2,1,0:T(8,128)(2,1)S(1)} %copy-done.2, bf16[288,288]{1,0:T(8,128)(2,1)S(1)} %copy-done.4), custom_call_target="tpu_custom_call" | custom-call | flops 1000000000 | bytes 6000000 | tf_op jit(solution)/shard_map/table_bias/pallas_call | solution.py:430
  31.3 1.3 copy-done.1
  32.6 1.2 compare_select_fusion.4.at_ref
  33.8 24.6 %block_pass.1 = (bf16[2,120,384]{2,1,0:T(8,128)(2,1)}, bf16[2,288,384]{2,1,0:T(8,128)(2,1)}, bf16[2,144,384]{2,1,0:T(8,128)(2,1)}, bf16[16,48,576]{2,1,0:T(8,128)(2,1)}, bf16[32,48,128]{2,1,0:T(8,128)(2,1)}) custom-call(s32[4]{0:T(128)} %compare_select_fusion.4.at_ref, bf16[2,120,384]{2,1,0:T(8,128)(2,1)} %bitcast.6.left_ref, ...), custom_call_target="tpu_custom_call" | custom-call | tf_op jit(solution)/shard_map/block_pass/pallas_call | solution.py:442
  58.4 23.9 %all_to_all.15.w_ref = bf16[16,48,576]{2,1,0:T(8,128)(2,1)S(1)} all-to-all(bf16[16,48,576]{2,1,0:T(8,128)(2,1)} %get-tuple-element.20), channel_id=1, replica_groups=mesh['lon'=32,'lat'=16] {'lat'}, dimensions={0} | all-to-all | bytes 1769472 | tf_op jit(solution)/shard_map/all_to_all | solution.py:517
  82.3 1.3 sum_lat.1
  83.7 8.3 %all-to-all-start.1 = ((bf16[32,48,128]{2,1,0:T(8,128)(2,1)}), bf16[32,48,128]{2,1,0:T(8,128)(2,1)S(1)}, u32[]{:S(2)}, u32[]{:S(2)}) async-start(bf16[32,48,128]{2,1,0:T(8,128)(2,1)} %sum_lat.1), calls=%async_computation.1 | async-start | bytes 786432 | tf_op jit(solution)/shard_map/all_to_all | solution.py:527
  92.0 5.3 %collective-permute-start.3 = (bf16[2,5,24,384]{3,2,1,0:T(8,128)(2,1)S(1)}, bf16[2,5,24,384]{3,2,1,0:T(8,128)(2,1)S(1)}, u32[]{:S(2)}, u32[]{:S(2)}) collective-permute-start(bf16[2,5,24,384]{3,2,1,0:T(8,128)(2,1)S(1)} %bitcast.37), channel_id=1, source_target_pairs={{0,496},{16,0},{32,16},{48,32},{64,48},{80,64},{96,80},{112,96},{1... | collective-permute-start | bytes 552968 | tf_op jit(solution)/shard_map/ppermute | solution.py:424
  97.4 0.7 compare_select_fusion.3.go_ref
  98.1 1.9 %collective-permute-start.2 = (bf16[2,6,24,384]{3,2,1,0:T(8,128)(2,1)S(1)}, bf16[2,6,24,384]{3,2,1,0:T(8,128)(2,1)S(1)}, u32[]{:S(2)}, u32[]{:S(2)}) collective-permute-start(bf16[2,6,24,384]{3,2,1,0:T(8,128)(2,1)S(1)} %bitcast.36), channel_id=1, source_target_pairs={{0,16},{16,32},{32,48},{48,64},{64,80},{80,96},{96,112},{112,128},... | collective-permute-start | bytes 663560 | tf_op jit(solution)/shard_map/ppermute | solution.py:424
  100.0 14.1 %collective-permute-done.3 = bf16[2,5,24,384]{3,2,1,0:T(8,128)(2,1)S(1)} collective-permute-done((bf16[2,5,24,384]{3,2,1,0:T(8,128)(2,1)S(1)}, bf16[2,5,24,384]{3,2,1,0:T(8,128)(2,1)S(1)}, u32[]{:S(2)}, u32[]{:S(2)}) %collective-permute-start.3) | collective-permute-done | bytes 184352 | tf_op jit(solution)/shard_map/ppermute | solution.py:424
  114.1 2.6 %collective-permute-done.2 = bf16[2,6,24,384]{3,2,1,0:T(8,128)(2,1)S(1)} collective-permute-done((bf16[2,6,24,384]{3,2,1,0:T(8,128)(2,1)S(1)}, bf16[2,6,24,384]{3,2,1,0:T(8,128)(2,1)S(1)}, u32[]{:S(2)}, u32[]{:S(2)}) %collective-permute-start.2) | collective-permute-done | bytes 221216 | tf_op jit(solution)/shard_map/ppermute | solution.py:424
  116.8 1.8 %sum_lon.1 = (f32[12,18]{1,0:T(8,128)}, f32[12,6]{1,0:T(8,128)S(1)}, f32[12,24]{1,0:T(8,128)}, f32[48,6]{1,0:T(8,128)S(1)}, bf16[16,32,128]{2,1,0:T(8,128)(2,1)}) custom-call(s32[4]{0:T(128)S(1)} %compare_select_fusion.3.go_ref, bf16[32,48,128]{2,1,0:T(8,128)(2,1)S(1)} %all-to-all-done.1.in_ref), custom_call_target="tpu_custom_call" | custom-call | tf_op jit(solution)/shard_map/sum_lon/pallas_call | solution.py:529
  118.6 7.3 %all-to-all-start.2 = ((bf16[16,32,128]{2,1,0:T(8,128)(2,1)}), bf16[16,32,128]{2,1,0:T(8,128)(2,1)S(1)}, u32[]{:S(2)}, u32[]{:S(2)}) async-start(bf16[16,32,128]{2,1,0:T(8,128)(2,1)} %get-tuple-element.26), calls=%async_computation.2 | async-start | bytes 262144 | tf_op jit(solution)/shard_map/all_to_all | solution.py:543
  126.2 0.7 copy.40
  127.1 0.7 copy.39
  127.8 0.7 copy.41
  128.5 0.7 copy.42
  129.2 4.5 %all-to-all-done.2.in_ref = bf16[16,32,128]{2,1,0:T(8,128)(2,1)S(1)} async-done(((bf16[16,32,128]{2,1,0:T(8,128)(2,1)}), bf16[16,32,128]{2,1,0:T(8,128)(2,1)S(1)}, u32[]{:S(2)}, u32[]{:S(2)}) %all-to-all-start.2) | async-done | bytes 131104 | tf_op jit(solution)/shard_map/all_to_all | solution.py:543
  133.7 0.7 sum_table.1
  (56 shorter events, 4.3 us)
Async XLA Ops:
  0.6 24.2 %copy-start = (bf16[32,19872]{1,0:T(8,128)(2,1)S(1)}, bf16[32,19872]{1,0:T(8,128)(2,1)}, u32[]{:S(2)}) copy-start(bf16[32,19872]{1,0:T(8,128)(2,1)} %param.18) | copy-start | bytes 3815428
  0.6 1.6 %copy-start.11 = (bf16[2,24,12,192]{3,1,2,0:T(8,128)(2,1)S(1)}, bf16[2,24,12,192]{3,1,2,0:T(8,128)(2,1)}, u32[]{:S(2)}) copy-start(bf16[2,24,12,192]{3,1,2,0:T(8,128)(2,1)} %param.13) | copy-start | bytes 663556
  2.3 16.8 %copy-start.12 = (s32[16]{0:T(128)S(1)}, s32[16]{0:T(128)}, u32[]{:S(2)}) copy-start(s32[16]{0:T(128)} %param.19) | copy-start | bytes 196
  2.8 20.6 %copy-start.10 = (bf16[192,192]{1,0:T(8,128)(2,1)S(1)}, bf16[192,192]{1,0:T(8,128)(2,1)}, u32[]{:S(2)}) copy-start(bf16[192,192]{1,0:T(8,128)(2,1)} %wproj_ref.1) | copy-start | bytes 221188
  2.8 21.4 %copy-start.5 = (s32[32]{0:T(128)S(1)}, s32[32]{0:T(128)}, u32[]{:S(2)}) copy-start(s32[32]{0:T(128)} %param.20) | copy-start | bytes 388
  3.6 30.3 %collective-permute-start = (bf16[2,5,24,384]{3,2,1,0:T(8,128)(2,1)}, bf16[2,5,24,384]{3,2,1,0:T(8,128)(2,1)}, u32[]{:S(2)}, u32[]{:S(2)}) collective-permute-start(bf16[2,5,24,384]{3,2,1,0:T(8,128)(2,1)} %slice.32), channel_id=1, source_target_pairs={{0,16},{16,32},{32,48},{48,64},{64,80},{80,96},{96,112},{112,128},... | collective-permute-start | bytes 552968 | tf_op jit(solution)/shard_map/ppermute | solution.py:424
  8.7 25.2 %collective-permute-start.1 = (bf16[2,6,24,384]{3,2,1,0:T(8,128)(2,1)}, bf16[2,6,24,384]{3,2,1,0:T(8,128)(2,1)}, u32[]{:S(2)}, u32[]{:S(2)}) collective-permute-start(bf16[2,6,24,384]{3,2,1,0:T(8,128)(2,1)} %slice.33), channel_id=1, source_target_pairs={{0,496},{16,0},{32,16},{48,32},{64,48},{80,64},{96,80},{112,96},{1... | collective-permute-start | bytes 663560 | tf_op jit(solution)/shard_map/ppermute | solution.py:424
  25.5 1.1 copy-start.8
  26.1 1.5 %copy-start.6 = (bf16[192,768]{1,0:T(8,128)(2,1)S(1)}, bf16[192,768]{1,0:T(8,128)(2,1)}, u32[]{:S(2)}) copy-start(bf16[192,768]{1,0:T(8,128)(2,1)} %wup_ref.1) | copy-start | bytes 884740
  26.2 2.3 %copy-start.7 = (bf16[768,192]{0,1:T(8,128)(2,1)S(1)}, bf16[768,192]{0,1:T(8,128)(2,1)}, u32[]{:S(2)}) copy-start(bf16[768,192]{0,1:T(8,128)(2,1)} %param.17) | copy-start | bytes 884740
  26.5 2.9 %copy-start.2 = (bf16[3,384,144]{2,1,0:T(8,128)(2,1)S(1)}, bf16[3,384,144]{2,1,0:T(8,128)(2,1)}, u32[]{:S(2)}) copy-start(bf16[3,384,144]{2,1,0:T(8,128)(2,1)} %constant.60.clone.spread_ref) | copy-start | bytes 995332
  26.5 2.9 %copy-start.4 = (bf16[288,288]{1,0:T(8,128)(2,1)S(1)}, bf16[288,288]{1,0:T(8,128)(2,1)}, u32[]{:S(2)}) copy-start(bf16[288,288]{1,0:T(8,128)(2,1)} %constant.61.clone.regroup_ref) | copy-start | bytes 497668
  31.3 1.3 copy-start.1
  58.4 24.0 %copy-start.3 = (bf16[32,48,128]{2,1,0:T(8,128)(2,1)S(1)}, bf16[32,48,128]{2,1,0:T(8,128)(2,1)}, u32[]{:S(2)}) copy-start(bf16[32,48,128]{2,1,0:T(8,128)(2,1)} %get-tuple-element.21.t_ref) | copy-start | bytes 1179652
  82.3 9.7 %copy-start.14 = (bf16[2,120,384]{2,1,0:T(8,128)(2,1)S(1)}, bf16[2,120,384]{2,1,0:T(8,128)(2,1)}, u32[]{:S(2)}) copy-start(bf16[2,120,384]{2,1,0:T(8,128)(2,1)} %get-tuple-element.19) | copy-start | bytes 552964
  82.3 15.7 %copy-start.9 = (bf16[2,288,384]{2,1,0:T(8,128)(2,1)S(1)}, bf16[2,288,384]{2,1,0:T(8,128)(2,1)}, u32[]{:S(2)}) copy-start(bf16[2,288,384]{2,1,0:T(8,128)(2,1)} %get-tuple-element.17) | copy-start | bytes 1327108
  82.3 15.7 %copy-start.13 = (bf16[2,144,384]{2,1,0:T(8,128)(2,1)S(1)}, bf16[2,144,384]{2,1,0:T(8,128)(2,1)}, u32[]{:S(2)}) copy-start(bf16[2,144,384]{2,1,0:T(8,128)(2,1)} %get-tuple-element.18) | copy-start | bytes 663556
  83.7 33.2 %all-to-all-start.1 = ((bf16[32,48,128]{2,1,0:T(8,128)(2,1)}), bf16[32,48,128]{2,1,0:T(8,128)(2,1)S(1)}, u32[]{:S(2)}, u32[]{:S(2)}) async-start(bf16[32,48,128]{2,1,0:T(8,128)(2,1)} %sum_lat.1), calls=%async_computation.1 | async-start | bytes 786432 | tf_op jit(solution)/shard_map/all_to_all | solution.py:527
  92.0 22.0 %collective-permute-start.3 = (bf16[2,5,24,384]{3,2,1,0:T(8,128)(2,1)S(1)}, bf16[2,5,24,384]{3,2,1,0:T(8,128)(2,1)S(1)}, u32[]{:S(2)}, u32[]{:S(2)}) collective-permute-start(bf16[2,5,24,384]{3,2,1,0:T(8,128)(2,1)S(1)} %bitcast.37), channel_id=1, source_target_pairs={{0,496},{16,0},{32,16},{48,32},{64,48},{80,64},{96,80},{112,96},{1... | collective-permute-start | bytes 552968 | tf_op jit(solution)/shard_map/ppermute | solution.py:424
  98.1 18.7 %collective-permute-start.2 = (bf16[2,6,24,384]{3,2,1,0:T(8,128)(2,1)S(1)}, bf16[2,6,24,384]{3,2,1,0:T(8,128)(2,1)S(1)}, u32[]{:S(2)}, u32[]{:S(2)}) collective-permute-start(bf16[2,6,24,384]{3,2,1,0:T(8,128)(2,1)S(1)} %bitcast.36), channel_id=1, source_target_pairs={{0,16},{16,32},{32,48},{48,64},{64,80},{80,96},{96,112},{112,128},... | collective-permute-start | bytes 663560 | tf_op jit(solution)/shard_map/ppermute | solution.py:424
  118.6 15.0 %all-to-all-start.2 = ((bf16[16,32,128]{2,1,0:T(8,128)(2,1)}), bf16[16,32,128]{2,1,0:T(8,128)(2,1)S(1)}, u32[]{:S(2)}, u32[]{:S(2)}) async-start(bf16[16,32,128]{2,1,0:T(8,128)(2,1)} %get-tuple-element.26), calls=%async_computation.2 | async-start | bytes 262144 | tf_op jit(solution)/shard_map/all_to_all | solution.py:543

commit v2 on v1

v2 whole, which is shorter than its diff:
```python
import functools

import jax
import jax.numpy as jnp
from jax import lax
from jax.experimental import pallas as pl
from jax.experimental.pallas import tpu as pltpu
from jax.sharding import PartitionSpec as P

HEADS = 6
HEAD = 32
WIDTH = 192
HID = 768
WH = 6
WW = 12
LEVELS = 2
SLOTS = 4
WTOK = 144
CELL_ROWS = 72
POS = 3312
SPAN = 23
LEFT = 5
RIGHT = 6
LAT = 24
NLAT = 16
NLON = 32
ALL_Q = HEADS * WTOK
GROUP = 4
PARTS = WW // GROUP
LANES_V = 512
HALF_V = 256
Z = 16
PER_Z = 40

bf16 = jnp.bfloat16
f32 = jnp.float32
epsilon = 1e-05

NN = (((1,), (0,)), ((), ()))
NT = (((1,), (1,)), ((), ()))


def mm(left, right, dims=NN):
    return lax.dot_general(left, right, dims, preferred_element_type=f32)


def one_hot(condition):
    return jnp.where(condition, 1.0, 0.0).astype(bf16)


def eye(count):
    rows = lax.broadcasted_iota(jnp.int32, (count, count), 0)
    cols = lax.broadcasted_iota(jnp.int32, (count, count), 1)
    return one_hot(rows == cols)


def split(x, size):
    high = (x * ((65536 + size - 1) // size)) >> 16
    return high, x - high * size


def tables_kernel(spread_ref, regroup_ref, regroup_t_ref, entry_ref, rows_ref):
    def line(count, axis):
        shape = (count, 1) if axis == 0 else (1, count)
        return lax.broadcasted_iota(jnp.int32, shape, axis)

    level, cell = split(line(WTOK, 1), 72)
    col, row = split(cell, WH)
    source = level * HALF_V + row * SPAN + col + (WW - GROUP)
    place = lax.broadcasted_iota(jnp.int32, (LANES_V, WTOK), 0)
    for part in range(PARTS):
        spread_ref[part] = one_hot(place == source - GROUP * part)

    lane = lax.broadcasted_iota(jnp.int32, (288, 288), 1)
    high, low = split(line(288, 0), 24)
    step, row = split(low, WH)
    regroup_ref[...] = one_hot(lane == step * 72 + high * WH + row)
    step, low = split(line(288, 0), 72)
    high, row = split(low, WH)
    regroup_t_ref[...] = one_hot(lane == (high * GROUP + step) * WH + row)

    place, chunk = split(line(288, 0), NLON)
    at = chunk * 9 + place
    high, hk = split(at >> 1, WH)
    source = ((high & 1) * 2 + (at & 1)) * 72 + (high >> 1) * WH + hk
    entry_ref[...] = one_hot(lane == source)

    high, low = split(line(SLOTS * 144, 0), 72)
    pair, hk = split(low, WH)
    source = ((pair * 2 + (high & 1)) * WH + hk) * 8 + (high >> 1)
    rows_ref[...] = one_hot(lax.broadcasted_iota(jnp.int32, (SLOTS * 144, 1152), 1) == source)


def make_tables():
    return pl.pallas_call(
        tables_kernel,
        out_shape=(
            jax.ShapeDtypeStruct((PARTS, LANES_V, WTOK), bf16),
            jax.ShapeDtypeStruct((288, 288), bf16),
            jax.ShapeDtypeStruct((288, 288), bf16),
            jax.ShapeDtypeStruct((288, 288), bf16),
            jax.ShapeDtypeStruct((SLOTS * 144, 1152), bf16),
        ),
        out_specs=(vmem(),) * 5,
        compiler_params=params(16),
        cost_estimate=pl.CostEstimate(flops=6000000000, bytes_accessed=20000000, transcendentals=0),
        name="index_tables",
    )()


def layer_norm(x):
    centre = jnp.sum(x, axis=0, keepdims=True) * (1.0 / WIDTH)
    shifted = x - centre
    var = jnp.sum(shifted * shifted, axis=0, keepdims=True) * (1.0 / WIDTH)
    inv = lax.rsqrt(var + epsilon)
    return shifted * inv, inv


def norm_back(normed, inv, grad):
    mean_grad = jnp.sum(grad, axis=0, keepdims=True) * (1.0 / WIDTH)
    mean_proj = jnp.sum(grad * normed, axis=0, keepdims=True) * (1.0 / WIDTH)
    return inv * (grad - mean_grad - normed * mean_proj)


def transpose_into(source_ref, target_ref):
    count = source_ref.shape[1]
    for first in range(0, count, 256):
        size = min(256, count - first)
        target_ref[first : first + size, :] = mm(
            eye(size), source_ref[:, first : first + size], NT
        ).astype(bf16)


def prep_kernel(
    lat_ref,
    band_ref,
    table_ref,
    rows_ref,
    spread_ref,
    regroup_ref,
    wqkv_ref,
    wproj_ref,
    wup_ref,
    wdown_t_ref,
    bias_ref,
    wqkv_t_ref,
    wproj_t_ref,
    wup_t_ref,
    wdown_ref,
    flat_s,
    line_s,
):
    start, count = my_rows(lat_ref, band_ref)
    slot_of = lax.broadcasted_iota(jnp.int32, (8, 2 * NLAT), 0)
    row_of = lax.broadcasted_iota(jnp.int32, (8, 2 * NLAT), 1)
    flat_s[...] = mm(one_hot((row_of == start + slot_of) & (slot_of < count)), table_ref[...])
    for i in range(144):
        line_s[i * 8 : i * 8 + 8, 0:138] = flat_s[:, 138 * i : 138 * i + 138]
    lines = mm(rows_ref[...], line_s[:, 0:138].astype(bf16))

    transpose_into(wqkv_ref, wqkv_t_ref)
    transpose_into(wproj_ref, wproj_t_ref)
    transpose_into(wup_ref, wup_t_ref)
    transpose_into(wdown_t_ref, wdown_ref)
    regroup = regroup_ref[...]
    blank = jnp.zeros((72, HALF_V - 138), f32)
    for slot in range(SLOTS):
        at = slot * 144
        rows = jnp.concatenate([lines[at : at + 72], blank, lines[at + 72 : at + 144], blank], axis=1)
        shifted = [
            rows if step == GROUP - 1 else pltpu.roll(rows, LANES_V - (GROUP - 1 - step), 1)
            for step in range(GROUP)
        ]
        stack = jnp.concatenate(shifted, axis=0).astype(bf16)
        left = mm(regroup, stack).astype(bf16)
        for part in range(PARTS):
            full = mm(left, spread_ref[part])
            for head in range(HEADS):
                for level in range(LEVELS):
                    at = (head * 2 + level) * 24
                    bias_ref[
                        slot,
                        level * 72 + part * 24 : level * 72 + part * 24 + 24,
                        head * WTOK : (head + 1) * WTOK,
                    ] = full[at : at + 24, :]


def diagonal(full):
    return jnp.concatenate(
        [
            full[h * HEAD : (h + 1) * HEAD, h * WTOK : (h + 1) * WTOK]
            for h in range(HEADS)
        ],
        axis=0,
    )


def pack_kernel(order_ref, tok_ref, cot_ref, to_right_ref, to_left_ref):
    cut = (WW - LEFT) * LAT
    for which, ref in ((0, tok_ref), (1, cot_ref)):
        low, high = ref[0].astype(f32), ref[1].astype(f32)
        both = jnp.concatenate([low[cut:], high[cut:]], axis=1)
        to_right_ref[which] = both.astype(bf16)
        both = jnp.concatenate([low[: RIGHT * LAT], high[: RIGHT * LAT]], axis=1)
        to_left_ref[which] = both.astype(bf16)


def my_rows(lat_ref, band_ref):
    lat = lat_ref[0]
    start = jnp.int32(0)
    for i in range(NLAT):
        start = start + jnp.where(i < lat, band_ref[i], 0)
    return start, band_ref[lat]


def main_kernel(
    lat_ref,
    half_ref,
    band_ref,
    shift_ref,
    left_ref,
    own_t_ref,
    own_c_ref,
    right_ref,
    bias_ref,
    wqkv_ref,
    wqkv_t_ref,
    wproj_ref,
    wproj_t_ref,
    wup_ref,
    wup_t_ref,
    wdown_ref,
    wdown_t_ref,
    spread_ref,
    regroup_ref,
    entry_ref,
    out_left_ref,
    out_own_ref,
    out_right_ref,
    wsum_ref,
    keep_ref,
    give_ref,
    x_s,
    c_s,
    ro_s,
    rg_s,
    qm_s,
    gm_s,
    acc_s,
    accd_s,
    accq_s,
    ts_s,
    tt_s,
):
    n_left, n_own, n_right = LEFT * LAT, WW * LAT, RIGHT * LAT

    start, count = my_rows(lat_ref, band_ref)
    at = []
    for s in range(SLOTS):
        shift = shift_ref[jnp.minimum(start + s, 2 * NLAT - 1)]
        first = jnp.where(shift <= RIGHT, shift, shift - WW) + LEFT
        at.append(jnp.where(s < count, first * LAT + s * WH, -100000))

    def place(axis):
        shape = (CELL_ROWS, 1) if axis == 0 else (1, CELL_ROWS)
        cell = lax.broadcasted_iota(jnp.int32, shape, axis)
        col = (cell * 43) >> 8
        base = col * LAT + (cell - col * WH)
        return jnp.concatenate([base + at[s] for s in range(SLOTS)], axis=axis)

    goal = place(0)

    def pick(first, count):
        lane = lax.broadcasted_iota(jnp.int32, (288, count), 1)
        return one_hot(goal - first == lane)

    sel_l = pick(0, n_left)
    sel_o = pick(n_left, n_own)
    sel_r = pick(n_left + n_own, n_right)
    for which, own_ref, scratch in ((0, own_t_ref, x_s), (1, own_c_ref, c_s)):
        edge = mm(sel_l, left_ref[which]) + mm(sel_r, right_ref[which])
        for level in range(LEVELS):
            got = edge[:, level * WIDTH : (level + 1) * WIDTH] + mm(sel_o, own_ref[level])
            for slot in range(SLOTS):
                scratch[slot, level * 72 : level * 72 + 72, :] = got[slot * 72 : slot * 72 + 72]

    acc_s[...] = jnp.zeros_like(acc_s)
    accd_s[...] = jnp.zeros_like(accd_s)
    qm_s[...] = jnp.zeros_like(qm_s)
    gm_s[...] = jnp.zeros_like(gm_s)
    tt_s[...] = jnp.zeros_like(tt_s)
    eye_d = eye(WIDTH)
    eye_t = eye(WTOK)
    scale = HEAD ** (-0.5)

    def one_slot(slot):
        x = mm(eye_d, x_s[slot].astype(bf16), NT)
        yield
        cot = mm(eye_d, c_s[slot].astype(bf16), NT)
        yield
        cot_b = cot.astype(bf16)
        na, inv_a = layer_norm(x)
        na_b = na.astype(bf16)
        qkv = mm(wqkv_t_ref[...], na_b)
        yield
        q = (qkv[:WIDTH] * scale).astype(bf16)
        k = qkv[WIDTH : 2 * WIDTH].astype(bf16)
        v = qkv[2 * WIDTH :].astype(bf16)
        k_rows = mm(eye_t, k, NT).astype(bf16)
        yield
        v_rows = mm(eye_t, v, NT).astype(bf16)
        yield
        for h in range(HEADS):
            qm_s[slot, h * HEAD : (h + 1) * HEAD, h * WTOK : (h + 1) * WTOK] = q[
                h * HEAD : (h + 1) * HEAD
            ]
        qm = qm_s[slot]
        scores = mm(k_rows, qm) + bias_ref[slot]
        yield
        top = jnp.max(scores, axis=0, keepdims=True)
        exps = jnp.exp(scores - top)
        probs = exps * (1.0 / jnp.sum(exps, axis=0, keepdims=True))
        probs_b = probs.astype(bf16)
        att_b = diagonal(mm(v, probs_b)).astype(bf16)
        yield
        hidden = x + mm(wproj_t_ref[...], att_b)
        yield
        nb, inv_b = layer_norm(hidden)
        nb_b = nb.astype(bf16)
        pre = mm(wup_t_ref[...], nb_b)
        yield
        cdf = 0.5 * (1.0 + lax.erf(pre * 0.7071067811865476))
        density = jnp.exp(-0.5 * pre * pre) * 0.3989422804014327
        act_b = (pre * cdf).astype(bf16)
        slope = cdf + pre * density
        out = hidden + mm(wdown_t_ref[...], act_b)
        yield
        ro_s[slot] = mm(eye_t, out.astype(bf16), NT)
        yield
        gpre_b = (mm(wdown_ref[...], cot_b) * slope).astype(bf16)
        yield
        accd_s[...] += mm(act_b, cot_b, NT)
        yield
        gh = cot + norm_back(nb, inv_b, mm(wup_ref[...], gpre_b))
        yield
        gh_b = gh.astype(bf16)
        acc_s[:, 768:1536] += mm(nb_b, gpre_b, NT)
        yield
        acc_s[:, 576:768] += mm(att_b, gh_b, NT)
        yield
        ga = mm(wproj_ref[...], gh_b).astype(bf16)
        yield
        for h in range(HEADS):
            gm_s[slot, h * HEAD : (h + 1) * HEAD, h * WTOK : (h + 1) * WTOK] = ga[
                h * HEAD : (h + 1) * HEAD
            ]
        gm = gm_s[slot]
        gp = mm(v_rows, gm)
        yield
        gs = probs * (gp - jnp.sum(probs * gp, axis=0, keepdims=True))
        gs_b = gs.astype(bf16)
        gq = diagonal(mm(k, gs_b)) * scale
        yield
        gk = mm(qm, gs_b, NT)
        yield
        gv = mm(gm, probs_b, NT)
        yield
        gc_b = jnp.concatenate([gq, gk, gv], axis=0).astype(bf16)
        acc_s[:, 0:576] += mm(na_b, gc_b, NT)
        yield
        gt = gh + norm_back(na, inv_a, mm(wqkv_ref[...], gc_b))
        yield
        rg_s[slot] = mm(eye_t, gt.astype(bf16), NT)
        yield

        heads = [gs[:, h * WTOK : (h + 1) * WTOK] for h in range(HEADS)]
        total = None
        for part in range(PARTS):
            rows = jnp.concatenate(
                [
                    piece[level * 72 + part * 24 : level * 72 + part * 24 + 24]
                    for piece in heads
                    for level in range(LEVELS)
                ],
                axis=0,
            ).astype(bf16)
            term = mm(rows, spread_ref[part], NT)
            total = term if total is None else total + term
            yield
        steps = mm(regroup_ref[...], total.astype(bf16))
        yield
        table = steps[216:288]
        for step in range(GROUP - 1):
            table = table + pltpu.roll(steps[step * 72 : step * 72 + 72], GROUP - 1 - step, 1)
        for piece, first in enumerate((0, 69, HALF_V, HALF_V + 69)):
            ts_s[slot, piece * 72 : piece * 72 + 72, 0:69] = table[:, first : first + 69]

    for first in range(0, SLOTS, 4):
        runs = [one_slot(slot) for slot in range(first, first + 4)]
        while runs:
            runs = [run for run in runs if next(run, run) is not run]

    for slot in range(SLOTS):
        values = ts_s[slot][:, 0:69].astype(bf16)
        entries = mm(entry_ref[...], values)
        for n in range(9):
            tt_s[pl.ds(slot * 9 + n, NLON, stride=PER_Z), 0:69] = entries[
                n * NLON : (n + 1) * NLON
            ]
    size = Z * PER_Z
    half = half_ref[0]
    mine = tt_s[pl.ds(pl.multiple_of(half * size, 8), size), :]
    keep_ref[...] = mine.reshape(Z, PER_Z, 128).astype(bf16)
    other = tt_s[pl.ds(pl.multiple_of((1 - half) * size, 8), size), :]
    give_ref[...] = other.reshape(Z, PER_Z, 128).astype(bf16)

    for x in range(2):
        accq_s[:, x * 384 : x * 384 + 288] = acc_s[:, x * 288 : x * 288 + 288]
        accq_s[:, x * 384 + 288 : x * 384 + 384] = acc_s[:, 576 + x * 96 : 576 + x * 96 + 96]
    for x in range(2):
        for i in range(NLAT):
            top = accq_s[12 * i : 12 * i + 12, x * 384 : x * 384 + 384]
            low = acc_s[12 * i : 12 * i + 12, 768 + x * 384 : 768 + x * 384 + 384]
            down = [
                accd_s[48 * i + g * 24 : 48 * i + g * 24 + 24, x * 96 : x * 96 + 96]
                for g in range(2)
            ]
            both = jnp.concatenate([top, low], axis=0)
            wsum_ref[x * NLAT + i] = jnp.concatenate([both] + down, axis=1).astype(bf16)

    goal_t = place(1)

    def put(first, count):
        row = lax.broadcasted_iota(jnp.int32, (count, 288), 0)
        return one_hot(goal_t - first == row)

    put_l, put_o, put_r = put(0, n_left), put(n_left, n_own), put(n_left + n_own, n_right)
    for which, scratch in ((0, ro_s), (1, rg_s)):
        levels = [
            jnp.concatenate(
                [scratch[slot, level * 72 : level * 72 + 72] for slot in range(SLOTS)], axis=0
            )
            for level in range(LEVELS)
        ]
        for level in range(LEVELS):
            out_own_ref[which, level] = mm(put_o, levels[level].astype(bf16)).astype(bf16)
        rows = jnp.concatenate(levels, axis=1).astype(bf16)
        out_left_ref[which] = mm(put_l, rows).astype(bf16)
        out_right_ref[which] = mm(put_r, rows).astype(bf16)


def mid_kernel(
    w_ref,
    keep_ref,
    got_ref,
    own_ref,
    from_left_ref,
    from_right_ref,
    out_ref,
    cells_ref,
    grad_ref,
):
    for which, ref in ((0, cells_ref), (1, grad_ref)):
        for level in range(LEVELS):
            lanes = slice(level * WIDTH, (level + 1) * WIDTH)
            own = own_ref[which, level].astype(f32)
            first, last = from_left_ref[which], from_right_ref[which]
            near, far = RIGHT * LAT, (WW - LEFT) * LAT
            ref[level] = jnp.concatenate(
                [
                    own[:near] + first.astype(f32)[:, lanes],
                    own[near:far],
                    own[far:] + last.astype(f32)[:, lanes],
                ],
                axis=0,
            ).astype(bf16)
    total = w_ref[0].astype(f32)
    for i in range(1, 2 * NLAT):
        total = total + w_ref[i].astype(f32)
    qkv, proj = total[0:12, 0:288], total[0:12, 288:384]
    up = total[12:24, 0:384]
    down = [
        total[0:12, 384:480],
        total[12:24, 384:480],
        total[0:12, 480:576],
        total[12:24, 480:576],
    ]
    for z in range(Z):
        part = jnp.concatenate(
            [
                jnp.concatenate(
                    [qkv[:, 18 * z : 18 * z + 18], proj[:, 6 * z : 6 * z + 6]], axis=1
                ),
                up[:, 24 * z : 24 * z + 24],
                jnp.concatenate([piece[:, 6 * z : 6 * z + 6] for piece in down], axis=1),
                jnp.zeros((PER_Z - 36, 24), f32),
            ],
            axis=0,
        )
        table = keep_ref[z, :, 0:69].astype(f32) + got_ref[z, :, 0:69].astype(f32)
        out_ref[z] = jnp.concatenate(
            [table, part, jnp.zeros((PER_Z, 128 - 93), f32)], axis=1
        ).astype(bf16)


def fin_kernel(scale, lat_ref, band_ref, in_ref, qkv_ref, proj_ref, up_ref, down_ref, route_ref):
    total = in_ref[0].astype(f32)
    for i in range(1, Z):
        total = total + in_ref[i].astype(f32)
    qkv_ref[...] = total[0:12, 69:87] * scale
    proj_ref[...] = total[0:12, 87:93] * scale
    up_ref[...] = total[12:24, 69:93] * scale
    down_ref[...] = (
        jnp.concatenate([total[24:36, 69 + 6 * g : 75 + 6 * g] for g in range(4)], axis=0) * scale
    )
    table = total[0:36].astype(bf16).astype(f32)
    start, count = my_rows(lat_ref, band_ref)
    goes = [jnp.where(slot < count, start + slot, -1) for slot in range(SLOTS)]
    for i in range(NLAT):
        for j in range(2):
            mine = jnp.zeros((9, 128), f32)
            for slot in range(SLOTS):
                hit = jnp.where(goes[slot] == 2 * i + j, 1.0, 0.0)
                mine = mine + hit * table[slot * 9 : slot * 9 + 9]
            route_ref[i, j * 16 : j * 16 + 16, :] = jnp.concatenate(
                [mine, jnp.zeros((7, 128), f32)], axis=0
            ).astype(bf16)


def table_kernel(in_ref, out_ref):
    total = in_ref[0].astype(f32)
    for i in range(1, NLAT):
        total = total + in_ref[i].astype(f32)
    for j in range(2):
        out_ref[j : j + 1, :] = jnp.concatenate(
            [total[j * 16 + n : j * 16 + n + 1, 0:69] for n in range(9)], axis=1
        )


def vmem():
    return pl.BlockSpec(memory_space=pltpu.VMEM)


def smem():
    return pl.BlockSpec(memory_space=pltpu.SMEM)


def params(mib):
    return pltpu.CompilerParams(vmem_limit_bytes=mib * 1024 * 1024)


def to_lon(x, by):
    count = lax.axis_size("lon")
    return lax.ppermute(x, "lon", [(i, (i + by) % count) for i in range(count)])


def prepare(lat, band_rows, bias_table, tables, w_qkv, w_proj, w_up, w_down):
    w_down_t = w_down.T
    bias, w_qkv_t, w_proj_t, w_up_t, w_down = pl.pallas_call(
        prep_kernel,
        out_shape=(
            jax.ShapeDtypeStruct((SLOTS, WTOK, ALL_Q), f32),
            jax.ShapeDtypeStruct((3 * WIDTH, WIDTH), bf16),
            jax.ShapeDtypeStruct((WIDTH, WIDTH), bf16),
            jax.ShapeDtypeStruct((HID, WIDTH), bf16),
            jax.ShapeDtypeStruct((HID, WIDTH), bf16),
        ),
        in_specs=[smem()] * 2 + [vmem()] * 8,
        out_specs=(vmem(),) * 5,
        scratch_shapes=[pltpu.VMEM((8, HEADS * POS), f32), pltpu.VMEM((1152, HALF_V), f32)],
        compiler_params=params(24),
        cost_estimate=pl.CostEstimate(flops=1000000000, bytes_accessed=6000000, transcendentals=0),
        name="prepare",
    )(lat, band_rows, bias_table, *tables, w_qkv, w_proj, w_up, w_down_t)
    return bias, (w_qkv, w_qkv_t, w_proj, w_proj_t, w_up, w_up_t, w_down, w_down_t)


def block_pass(lat, half, band_rows, lon_shift, left, own_t, own_c, right, bias, weights, tables):
    return pl.pallas_call(
        main_kernel,
        out_shape=(
            jax.ShapeDtypeStruct((2, LEFT * LAT, 2 * WIDTH), bf16),
            jax.ShapeDtypeStruct((2, LEVELS, WW * LAT, WIDTH), bf16),
            jax.ShapeDtypeStruct((2, RIGHT * LAT, 2 * WIDTH), bf16),
            jax.ShapeDtypeStruct((2 * NLAT, 24, 576), bf16),
            jax.ShapeDtypeStruct((Z, PER_Z, 128), bf16),
            jax.ShapeDtypeStruct((Z, PER_Z, 128), bf16),
        ),
        in_specs=[smem()] * 4 + [vmem()] * 16,
        out_specs=(vmem(),) * 6,
        scratch_shapes=[
            pltpu.VMEM((SLOTS, WTOK, WIDTH), f32),
            pltpu.VMEM((SLOTS, WTOK, WIDTH), f32),
            pltpu.VMEM((SLOTS, WTOK, WIDTH), f32),
            pltpu.VMEM((SLOTS, WTOK, WIDTH), f32),
            pltpu.VMEM((SLOTS, WIDTH, ALL_Q), bf16),
            pltpu.VMEM((SLOTS, WIDTH, ALL_Q), bf16),
            pltpu.VMEM((WIDTH, 1536), f32),
            pltpu.VMEM((HID, WIDTH), f32),
            pltpu.VMEM((WIDTH, 768), f32),
            pltpu.VMEM((SLOTS, 288, 128), f32),
            pltpu.VMEM((NLON * PER_Z, 128), f32),
        ],
        compiler_params=params(32),
        name="block_pass",
    )(lat, half, band_rows, lon_shift, left, own_t, own_c, right, bias, *weights, *tables)


def local(tokens, cotangent, w_qkv, w_proj, w_up, w_down, bias_table, band_rows, lon_shift):
    latwin = bias_table.shape[0]
    lat = lax.axis_index("lat").reshape(1)
    half = (lax.axis_index("lon") // Z).reshape(1)

    own_t = tokens.transpose(0, 2, 1, 3).reshape(LEVELS, WW * LAT, WIDTH)
    own_c = cotangent.transpose(0, 2, 1, 3).reshape(LEVELS, WW * LAT, WIDTH)
    spread, regroup, regroup_t, entry, rows = make_tables()
    to_right, to_left = pl.pallas_call(
        pack_kernel,
        out_shape=(
            jax.ShapeDtypeStruct((2, LEFT * LAT, 2 * WIDTH), bf16),
            jax.ShapeDtypeStruct((2, RIGHT * LAT, 2 * WIDTH), bf16),
        ),
        in_specs=[pl.BlockSpec(memory_space=pl.ANY)] + [vmem()] * 2,
        out_specs=(vmem(),) * 2,
        compiler_params=params(16),
        name="pack_edges",
    )(regroup, own_t, own_c)
    left = to_lon(to_right, 1)
    right = to_lon(to_left, -1)

    bias, weights = prepare(
        lat, band_rows, bias_table, (rows, spread, regroup), w_qkv, w_proj, w_up, w_down
    )
    out_left, out_own, out_right, w_sums, t_keep, t_give = block_pass(
        lat,
        half,
        band_rows,
        lon_shift,
        left,
        own_t,
        own_c,
        right,
        bias,
        weights,
        (spread, regroup_t, entry),
    )

    from_right = to_lon(out_left, -1)
    from_left = to_lon(out_right, 1)
    t_got = to_lon(t_give, Z)
    near = [[(x * Z + z) * NLAT + i for x in range(2) for i in range(NLAT)] for z in range(Z)]
    ring = [[x * Z + z for z in range(Z)] for x in range(2)]
    w_got = lax.all_to_all(w_sums, ("lon", "lat"), 0, 0, axis_index_groups=near)
    cells_shape = jax.ShapeDtypeStruct((LEVELS, WW * LAT, WIDTH), bf16)
    lon_send, cells, grads = pl.pallas_call(
        mid_kernel,
        out_shape=(jax.ShapeDtypeStruct((Z, PER_Z, 128), bf16), cells_shape, cells_shape),
        in_specs=[vmem()] * 6,
        out_specs=(vmem(),) * 3,
        compiler_params=params(24),
        name="sum_lat",
    )(w_got, t_keep, t_got, out_own, from_left, from_right)
    output = cells.reshape(LEVELS, WW, LAT, WIDTH).transpose(0, 2, 1, 3)
    grad_tokens = grads.reshape(LEVELS, WW, LAT, WIDTH).transpose(0, 2, 1, 3)

    lon_got = lax.all_to_all(lon_send, "lon", 0, 0, axis_index_groups=ring)
    scale_grad = float(latwin * WH * LEVELS * WW * NLON) ** (-0.5)
    grad_qkv, grad_proj, grad_up, grad_down, route = pl.pallas_call(
        functools.partial(fin_kernel, scale_grad),
        out_shape=(
            jax.ShapeDtypeStruct((12, 18), f32),
            jax.ShapeDtypeStruct((12, 6), f32),
            jax.ShapeDtypeStruct((12, 24), f32),
            jax.ShapeDtypeStruct((48, 6), f32),
            jax.ShapeDtypeStruct((NLAT, 32, 128), bf16),
        ),
        in_specs=[smem(), smem(), vmem()],
        out_specs=(vmem(),) * 5,
        compiler_params=params(24),
        name="sum_lon",
    )(lat, band_rows, lon_got)
    route_got = lax.all_to_all(route, "lat", 0, 0)
    grad_table = pl.pallas_call(
        table_kernel,
        out_shape=jax.ShapeDtypeStruct((2, 621), f32),
        in_specs=[vmem()],
        out_specs=vmem(),
        compiler_params=params(24),
        name="sum_table",
    )(route_got)
    return (output, grad_tokens, grad_qkv, grad_proj, grad_up, grad_down, grad_table)


def solution(mesh):
    grid = P(None, "lat", "lon", None)
    cut = P("lat", "lon")
    return jax.shard_map(
        local,
        mesh=mesh,
        in_specs=(grid, grid, P(), P(), P(), P(), P(), P(), P()),
        out_specs=(grid, grid, cut, cut, cut, cut, cut),
        check_vma=False,
    )
```

time: 135 us -> 108 us (0.80)
  local copies, waits for them, and re-layouts: 16.8 us -> 5.88 us
  blocking collectives: 23.9 us -> 15.2 us
  starting transfers between devices: 37.7 us -> 44.2 us
  Pallas kernels: 30.3 us -> 23.9 us
  waiting for transfers between devices: 21.2 us -> 17 us
  other arithmetic: 2.11 us -> 0 us
  between operations: 2.29 us -> 0.9 us
    pallas_call x1, Pallas kernels: 24.6 us -> 14.5 us  [block_pass(): pl.pallas_call(main_kernel, out_shape=(jax.ShapeDtypeStruct((2, LEFT * LA...]
    all_to_all x1, blocking collectives: 23.9 us -> 15.2 us  [local(): lon_got = lax.all_to_all(lon_send, 'lon', 0, 0, axis_index_groups=ring)]
    ppermute x4 -> x5, waiting for transfers between devices: 16.7 us -> 10.3 us  [to_lon(): return lax.ppermute(x, 'lon', [(i, (i + by) % count) for i in range(count)])]
    pallas_call x2 -> x4, Pallas kernels: 3.23 us -> 7.35 us  [the longest x1 3.82 us: prepare(): pl.pallas_call(prep_kernel, out_shape=(jax.ShapeDtypeStruct((SLOTS, WTOK,...]
    ppermute x4 -> x5, starting transfers between devices: 22 us -> 25.5 us  [to_lon(): return lax.ppermute(x, 'lon', [(i, (i + by) % count) for i in range(count)])]
    all_to_all x1, starting transfers between devices: 7.31 us -> 10.2 us  [local(): route_got = lax.all_to_all(route, 'lat', 0, 0)]
    another operation x7 -> x0, local copies, waits for them, and re-layouts: 2.48 us -> none  [the longest x1 0.87 us: local(): own_c.reshape(WW * LAT, 2 * WIDTH)]
    transpose x3 -> x0, local copies, waits for them, and re-layouts: 1.92 us -> none  [the longest x2 1.69 us: pack(): return grid.transpose(2, 1, 0, 3).reshape(WW, LAT, LEVELS * WIDTH)]
  transfers between devices with their start and end apart: 6 -> 7, of which waited for: 3 -> 3; matrix products, arithmetic and copies ran while one was open for 11% -> 1% of each run, Pallas kernels for 1% -> 4%
where the time goes in v2:
time: 108 us; the launch traced here: 107 us
  starting transfers between devices  44.2 us (41%)
  Pallas kernels  23.9 us (22%)
  waiting for transfers between devices  17 us (16%)
  blocking collectives  15.2 us (14%)
  local copies, waits for them, and re-layouts  5.88 us (5%)
    ppermute x5, starting transfers between devices, to_lon(): return lax.ppermute(x, 'lon', [(i, (i + by) % count) for i in range(count)])  25.5 us
    all_to_all x1, blocking collectives, local(): lon_got = lax.all_to_all(lon_send, 'lon', 0, 0, axis_index_groups=ring)  15.2 us
    pallas_call x1, Pallas kernels, block_pass(): pl.pallas_call(main_kernel, out_shape=(jax.ShapeDtypeStruct((2, LEFT * LA...  14.5 us
    ppermute x5, waiting for transfers between devices, to_lon(): return lax.ppermute(x, 'lon', [(i, (i + by) % count) for i in range(count)])  10.3 us
    all_to_all x1, starting transfers between devices, local(): route_got = lax.all_to_all(route, 'lat', 0, 0)  10.2 us
    all_to_all x1, starting transfers between devices, local(): w_got = lax.all_to_all(w_sums, ('lon', 'lat'), 0, 0, axis_index_groups=near)  8.49 us
    all_to_all x1, waiting for transfers between devices, local(): route_got = lax.all_to_all(route, 'lat', 0, 0)  6.31 us
    unnamed x40, local copies, waits for them, and re-layouts  5.88 us
  transfers between devices with their start and end apart: 7, of which 3 were waited for; matrix products, arithmetic and copies ran while one was open for 1% of the time, Pallas kernels for 4%

profile of v2, /device:TPU:1, one launch (start us, length us, event | category | flops | bytes accessed | tf_op | source)
XLA Modules:
  0.0 107.2 jit_solution(1922872793071779456)
XLA Ops:
  0.6 0.0 copy-start.6
  0.6 0.0 copy-start.4
  0.7 0.9 index_tables.1
  1.6 0.7 copy-done.15
  2.3 0.9 pack_edges.1
  3.2 12.9 %collective-permute-start.1 = (bf16[2,144,384]{2,1,0:T(8,128)(2,1)}, bf16[2,144,384]{2,1,0:T(8,128)(2,1)}, u32[]{:S(2)}, u32[]{:S(2)}) collective-permute-start(bf16[2,144,384]{2,1,0:T(8,128)(2,1)} %get-tuple-element.35), channel_id=1, source_target_pairs={{0,496},{16,0},{32,16},{48,32},{64,48},{80,64},{96,80},{112,96},{1... | collective-permute-start | bytes 663560 | tf_op jit(solution)/shard_map/ppermute | solution.py:554
  16.0 1.9 %collective-permute-start = (bf16[2,120,384]{2,1,0:T(8,128)(2,1)}, bf16[2,120,384]{2,1,0:T(8,128)(2,1)}, u32[]{:S(2)}, u32[]{:S(2)}) collective-permute-start(bf16[2,120,384]{2,1,0:T(8,128)(2,1)} %get-tuple-element.34), channel_id=1, source_target_pairs={{0,16},{16,32},{32,48},{48,64},{64,80},{80,96},{96,112},{112,128},... | collective-permute-start | bytes 552968 | tf_op jit(solution)/shard_map/ppermute | solution.py:554
  18.0 0.0 copy-start.1
  18.0 1.0 copy-done.1
  19.0 1.0 copy-done.3
  20.0 0.9 copy-done.8
  20.9 0.9 copy-done.11
  21.9 0.0 copy-start.18
  21.9 3.8 %prepare.1 = (f32[4,144,864]{2,1,0:T(8,128)S(1)}, bf16[576,192]{1,0:T(8,128)(2,1)S(1)}, bf16[192,192]{1,0:T(8,128)(2,1)S(1)}, bf16[768,192]{1,0:T(8,128)(2,1)S(1)}, bf16[768,192]{1,0:T(8,128)(2,1)S(1)}) custom-call(s32[1]{0:T(128)} %bitcast.lat_ref, s32[16]{0:T(128)S(1)} %copy-done.17, bf16[32,19872]{1,0:T(8,128)(2,1)S(1)} %copy-done, ...), custom_call_target="tpu_custom_call" | custom-call | flops 1000000000 | bytes 6000000 | tf_op jit(solution)/shard_map/prepare/pallas_call | solution.py:559
  25.7 0.0 collective-permute-done.left_ref
  25.7 0.0 collective-permute-done.1.right_ref
  25.8 14.5 %block_pass.1 = (bf16[2,120,384]{2,1,0:T(8,128)(2,1)S(1)}, bf16[2,2,288,192]{3,2,1,0:T(8,128)(2,1)S(1)}, bf16[2,144,384]{2,1,0:T(8,128)(2,1)S(1)}, bf16[32,24,57...) custom-call(s32[1]{0:T(128)} %bitcast.lat_ref, s32[1]{0:T(128)} %bitcast.1.half_ref, ...), custom_call_target="tpu_custom_call" | custom-call | tf_op jit(solution)/shard_map/block_pass/pallas_call | solution.py:579
  40.3 8.5 %all-to-all-start = ((bf16[32,24,576]{2,1,0:T(8,128)(2,1)}), bf16[32,24,576]{2,1,0:T(8,128)(2,1)S(1)}, u32[]{:S(2)}, u32[]{:S(2)}) async-start(bf16[32,24,576]{2,1,0:T(8,128)(2,1)} %get-tuple-element.45), calls=%async_computation | async-start | bytes 1966080 | tf_op jit(solution)/shard_map/all_to_all | solution.py:653
  48.8 1.9 %collective-permute-start.3 = (bf16[2,144,384]{2,1,0:T(8,128)(2,1)S(1)}, bf16[2,144,384]{2,1,0:T(8,128)(2,1)S(1)}, u32[]{:S(2)}, u32[]{:S(2)}) collective-permute-start(bf16[2,144,384]{2,1,0:T(8,128)(2,1)S(1)} %get-tuple-element.49), channel_id=1, source_target_pairs={{0,16},{16,32},{32,48},{48,64},{64,80},{80,96},{96,112},{112,128},... | collective-permute-start | bytes 663560 | tf_op jit(solution)/shard_map/ppermute | solution.py:554
  50.7 5.5 %collective-permute-start.4 = (bf16[2,120,384]{2,1,0:T(8,128)(2,1)S(1)}, bf16[2,120,384]{2,1,0:T(8,128)(2,1)S(1)}, u32[]{:S(2)}, u32[]{:S(2)}) collective-permute-start(bf16[2,120,384]{2,1,0:T(8,128)(2,1)S(1)} %get-tuple-element.50), channel_id=1, source_target_pairs={{0,496},{16,0},{32,16},{48,32},{64,48},{80,64},{96,80},{112,96},{1... | collective-permute-start | bytes 552968 | tf_op jit(solution)/shard_map/ppermute | solution.py:554
  56.2 3.3 %collective-permute-start.2 = (bf16[16,40,128]{2,1,0:T(8,128)(2,1)S(1)}, bf16[16,40,128]{2,1,0:T(8,128)(2,1)S(1)}, u32[]{:S(2)}, u32[]{:S(2)}) collective-permute-start(bf16[16,40,128]{2,1,0:T(8,128)(2,1)S(1)} %get-tuple-element.47), channel_id=1, source_target_pairs={{0,256},{16,272},{32,288},{48,304},{64,320},{80,336},{96,352},{112... | collective-permute-start | bytes 491528 | tf_op jit(solution)/shard_map/ppermute | solution.py:554
  59.5 10.3 %collective-permute-done.2.got_ref = bf16[16,40,128]{2,1,0:T(8,128)(2,1)S(1)} collective-permute-done((bf16[16,40,128]{2,1,0:T(8,128)(2,1)S(1)}, bf16[16,40,128]{2,1,0:T(8,128)(2,1)S(1)}, u32[]{:S(2)}, u32[]{:S(2)}) %collective-permute-start.2) | collective-permute-done | bytes 163872 | tf_op jit(solution)/shard_map/ppermute | solution.py:554
  69.8 0.0 collective-permute-done.4.from_right_ref
  69.8 0.4 all-to-all-done.w_ref
  70.2 1.7 %sum_lat.1 = (bf16[16,40,128]{2,1,0:T(8,128)(2,1)S(1)}, bf16[2,288,192]{2,1,0:T(8,128)(2,1)}, bf16[2,288,192]{2,1,0:T(8,128)(2,1)}) custom-call(bf16[32,24,576]{2,1,0:T(8,128)(2,1)S(1)} %all-to-all-done.w_ref, bf16[16,40,128]{2,1,0:T(8,128)(2,1)S(1)} %get-tuple-element.46.keep_ref, bf16[16,40,128]{2,1,0:T(8,128)(2,1)S(1)} %collective-permute-done.2.got_ref, ...), custom_call_target="tpu_custom_call" | custom-call | tf_op jit(solution)/shard_map/sum_lat/pallas_call | solution.py:655
  72.0 15.2 %all_to_all.15.in_ref = bf16[16,40,128]{2,1,0:T(8,128)(2,1)S(1)} all-to-all(bf16[16,40,128]{2,1,0:T(8,128)(2,1)S(1)} %get-tuple-element.53), channel_id=1, replica_groups={{0,16,32,48,64,80,96,112,128,144,160,176,192,208,224,240},{256,272,288,..., dimensions={0} | all-to-all | bytes 327680 | tf_op jit(solution)/shard_map/all_to_all | solution.py:666
  87.2 1.4 %sum_lon.1 = (f32[12,18]{1,0:T(8,128)}, f32[12,6]{1,0:T(8,128)S(1)}, f32[12,24]{1,0:T(8,128)}, f32[48,6]{1,0:T(8,128)S(1)}, bf16[16,32,128]{2,1,0:T(8,128)(2,1)}) custom-call(s32[1]{0:T(128)} %bitcast.lat_ref, s32[16]{0:T(128)S(1)} %copy-done.17, bf16[16,40,128]{2,1,0:T(8,128)(2,1)S(1)} %all_to_all.15.in_ref), custom_call_target="tpu_custom_call" | custom-call | tf_op jit(solution)/shard_map/sum_lon/pallas_call | solution.py:668
  88.6 10.2 %all-to-all-start.2 = ((bf16[16,32,128]{2,1,0:T(8,128)(2,1)}), bf16[16,32,128]{2,1,0:T(8,128)(2,1)S(1)}, u32[]{:S(2)}, u32[]{:S(2)}) async-start(bf16[16,32,128]{2,1,0:T(8,128)(2,1)} %get-tuple-element.58), calls=%async_computation.2 | async-start | bytes 262144 | tf_op jit(solution)/shard_map/all_to_all | solution.py:682
  98.9 0.7 copy.16
  99.5 0.7 copy.17
  100.2 6.3 %all-to-all-done.2.in_ref = bf16[16,32,128]{2,1,0:T(8,128)(2,1)S(1)} async-done(((bf16[16,32,128]{2,1,0:T(8,128)(2,1)}), bf16[16,32,128]{2,1,0:T(8,128)(2,1)S(1)}, u32[]{:S(2)}, u32[]{:S(2)}) %all-to-all-start.2) | async-done | bytes 131104 | tf_op jit(solution)/shard_map/all_to_all | solution.py:682
  106.5 0.7 sum_table.1
  (30 shorter events, 0.1 us)
Async XLA Ops:
  0.6 1.6 %copy-start.6 = (bf16[2,24,12,192]{3,1,2,0:T(8,128)(2,1)S(1)}, bf16[2,24,12,192]{3,1,2,0:T(8,128)(2,1)}, u32[]{:S(2)}) copy-start(bf16[2,24,12,192]{3,1,2,0:T(8,128)(2,1)} %param.10) | copy-start | bytes 663556
  0.6 1.6 %copy-start.4 = (bf16[2,24,12,192]{3,1,2,0:T(8,128)(2,1)S(1)}, bf16[2,24,12,192]{3,1,2,0:T(8,128)(2,1)}, u32[]{:S(2)}) copy-start(bf16[2,24,12,192]{3,1,2,0:T(8,128)(2,1)} %param.9) | copy-start | bytes 663556
  0.7 17.3 %copy-start.17 = (s32[16]{0:T(128)S(1)}, s32[16]{0:T(128)}, u32[]{:S(2)}) copy-start(s32[16]{0:T(128)} %band_ref.5) | copy-start | bytes 196
  0.7 17.3 %copy-start.12 = (bf16[192,192]{1,0:T(8,128)(2,1)S(1)}, bf16[192,192]{1,0:T(8,128)(2,1)}, u32[]{:S(2)}) copy-start(bf16[192,192]{1,0:T(8,128)(2,1)} %wproj_ref.3) | copy-start | bytes 221188
  0.7 17.3 %copy-start = (bf16[32,19872]{1,0:T(8,128)(2,1)S(1)}, bf16[32,19872]{1,0:T(8,128)(2,1)}, u32[]{:S(2)}) copy-start(bf16[32,19872]{1,0:T(8,128)(2,1)} %table_ref.1) | copy-start | bytes 3815428
  1.6 0.7 copy-start.15
  2.3 0.9 copy-start.10
  2.3 0.9 copy-start.13
  3.2 22.6 %collective-permute-start.1 = (bf16[2,144,384]{2,1,0:T(8,128)(2,1)}, bf16[2,144,384]{2,1,0:T(8,128)(2,1)}, u32[]{:S(2)}, u32[]{:S(2)}) collective-permute-start(bf16[2,144,384]{2,1,0:T(8,128)(2,1)} %get-tuple-element.35), channel_id=1, source_target_pairs={{0,496},{16,0},{32,16},{48,32},{64,48},{80,64},{96,80},{112,96},{1... | collective-permute-start | bytes 663560 | tf_op jit(solution)/shard_map/ppermute | solution.py:554
  16.0 9.7 %collective-permute-start = (bf16[2,120,384]{2,1,0:T(8,128)(2,1)}, bf16[2,120,384]{2,1,0:T(8,128)(2,1)}, u32[]{:S(2)}, u32[]{:S(2)}) collective-permute-start(bf16[2,120,384]{2,1,0:T(8,128)(2,1)} %get-tuple-element.34), channel_id=1, source_target_pairs={{0,16},{16,32},{32,48},{48,64},{64,80},{80,96},{96,112},{112,128},... | collective-permute-start | bytes 552968 | tf_op jit(solution)/shard_map/ppermute | solution.py:554
  18.0 1.0 copy-start.1
  19.0 1.0 copy-start.3
  19.9 0.9 copy-start.8
  20.9 0.9 copy-start.11
  21.8 3.9 %copy-start.2 = (bf16[192,768]{1,0:T(8,128)(2,1)S(1)}, bf16[192,768]{1,0:T(8,128)(2,1)}, u32[]{:S(2)}) copy-start(bf16[192,768]{1,0:T(8,128)(2,1)} %wup_ref.3) | copy-start | bytes 884740
  21.8 3.9 %copy-start.5 = (bf16[2,24,12,192]{3,1,2,0:T(8,128)(2,1)S(1)}, bf16[2,24,12,192]{3,1,2,0:T(8,128)(2,1)}, u32[]{:S(2)}) copy-start(bf16[2,24,12,192]{3,1,2,0:T(8,128)(2,1)} %param.9) | copy-start | bytes 663556
  21.8 3.9 %copy-start.7 = (bf16[2,24,12,192]{3,1,2,0:T(8,128)(2,1)S(1)}, bf16[2,24,12,192]{3,1,2,0:T(8,128)(2,1)}, u32[]{:S(2)}) copy-start(bf16[2,24,12,192]{3,1,2,0:T(8,128)(2,1)} %param.10) | copy-start | bytes 663556
  21.8 3.9 %copy-start.9 = (bf16[192,576]{1,0:T(8,128)(2,1)S(1)}, bf16[192,576]{1,0:T(8,128)(2,1)}, u32[]{:S(2)}) copy-start(bf16[192,576]{1,0:T(8,128)(2,1)} %wqkv_ref.3) | copy-start | bytes 663556
  21.8 3.9 %copy-start.14 = (bf16[288,288]{1,0:T(8,128)(2,1)S(1)}, bf16[288,288]{1,0:T(8,128)(2,1)}, u32[]{:S(2)}) copy-start(bf16[288,288]{1,0:T(8,128)(2,1)} %copy-done.13) | copy-start | bytes 497668
  21.9 3.9 %copy-start.16 = (bf16[288,288]{1,0:T(8,128)(2,1)S(1)}, bf16[288,288]{1,0:T(8,128)(2,1)}, u32[]{:S(2)}) copy-start(bf16[288,288]{1,0:T(8,128)(2,1)} %copy-done.15) | copy-start | bytes 497668
  21.9 3.9 %copy-start.18 = (s32[32]{0:T(128)S(1)}, s32[32]{0:T(128)}, u32[]{:S(2)}) copy-start(s32[32]{0:T(128)} %shift_ref.1) | copy-start | bytes 388
  40.3 29.9 %all-to-all-start = ((bf16[32,24,576]{2,1,0:T(8,128)(2,1)}), bf16[32,24,576]{2,1,0:T(8,128)(2,1)S(1)}, u32[]{:S(2)}, u32[]{:S(2)}) async-start(bf16[32,24,576]{2,1,0:T(8,128)(2,1)} %get-tuple-element.45), calls=%async_computation | async-start | bytes 1966080 | tf_op jit(solution)/shard_map/all_to_all | solution.py:653
  48.8 21.0 %collective-permute-start.3 = (bf16[2,144,384]{2,1,0:T(8,128)(2,1)S(1)}, bf16[2,144,384]{2,1,0:T(8,128)(2,1)S(1)}, u32[]{:S(2)}, u32[]{:S(2)}) collective-permute-start(bf16[2,144,384]{2,1,0:T(8,128)(2,1)S(1)} %get-tuple-element.49), channel_id=1, source_target_pairs={{0,16},{16,32},{32,48},{48,64},{64,80},{80,96},{96,112},{112,128},... | collective-permute-start | bytes 663560 | tf_op jit(solution)/shard_map/ppermute | solution.py:554
  50.7 19.1 %collective-permute-start.4 = (bf16[2,120,384]{2,1,0:T(8,128)(2,1)S(1)}, bf16[2,120,384]{2,1,0:T(8,128)(2,1)S(1)}, u32[]{:S(2)}, u32[]{:S(2)}) collective-permute-start(bf16[2,120,384]{2,1,0:T(8,128)(2,1)S(1)} %get-tuple-element.50), channel_id=1, source_target_pairs={{0,496},{16,0},{32,16},{48,32},{64,48},{80,64},{96,80},{112,96},{1... | collective-permute-start | bytes 552968 | tf_op jit(solution)/shard_map/ppermute | solution.py:554
  56.2 13.6 %collective-permute-start.2 = (bf16[16,40,128]{2,1,0:T(8,128)(2,1)S(1)}, bf16[16,40,128]{2,1,0:T(8,128)(2,1)S(1)}, u32[]{:S(2)}, u32[]{:S(2)}) collective-permute-start(bf16[16,40,128]{2,1,0:T(8,128)(2,1)S(1)} %get-tuple-element.47), channel_id=1, source_target_pairs={{0,256},{16,272},{32,288},{48,304},{64,320},{80,336},{96,352},{112... | collective-permute-start | bytes 491528 | tf_op jit(solution)/shard_map/ppermute | solution.py:554
  88.6 17.9 %all-to-all-start.2 = ((bf16[16,32,128]{2,1,0:T(8,128)(2,1)}), bf16[16,32,128]{2,1,0:T(8,128)(2,1)S(1)}, u32[]{:S(2)}, u32[]{:S(2)}) async-start(bf16[16,32,128]{2,1,0:T(8,128)(2,1)} %get-tuple-element.58), calls=%async_computation.2 | async-start | bytes 262144 | tf_op jit(solution)/shard_map/all_to_all | solution.py:682

commit v3 on v2

--- a/solution.py
+++ b/solution.py
@@ -31,6 +31,7 @@
 HALF_V = 256
 Z = 16
 PER_Z = 40
+SEND = 32
 
 bf16 = jnp.bfloat16
 f32 = jnp.float32
@@ -59,11 +60,35 @@
     return high, x - high * size
 
 
-def tables_kernel(spread_ref, regroup_ref, regroup_t_ref, entry_ref, rows_ref):
-    def line(count, axis):
-        shape = (count, 1) if axis == 0 else (1, count)
-        return lax.broadcasted_iota(jnp.int32, shape, axis)
-
+def line(count, axis):
+    shape = (count, 1) if axis == 0 else (1, count)
+    return lax.broadcasted_iota(jnp.int32, shape, axis)
+
+
+def regroup_matrix():
+    high, low = split(line(288, 0), 24)
+    step, row = split(low, WH)
+    lane = lax.broadcasted_iota(jnp.int32, (288, 288), 1)
+    return one_hot(lane == step * 72 + high * WH + row)
+
+
+def regroup_back_matrix():
+    step, low = split(line(288, 0), 72)
+    high, row = split(low, WH)
+    lane = lax.broadcasted_iota(jnp.int32, (288, 288), 1)
+    return one_hot(lane == (high * GROUP + step) * WH + row)
+
+
+def entry_matrix():
+    place, chunk = split(line(288, 0), NLON)
+    at = chunk * 9 + place
+    high, hk = split(at >> 1, WH)
+    source = ((high & 1) * 2 + (at & 1)) * 72 + (high >> 1) * WH + hk
+    lane = lax.broadcasted_iota(jnp.int32, (288, 288), 1)
+    return one_hot(lane == source)
+
+
+def tables_kernel(spread_ref, rows_ref):
     level, cell = split(line(WTOK, 1), 72)
     col, row = split(cell, WH)
     source = level * HALF_V + row * SPAN + col + (WW - GROUP)
@@ -71,20 +96,6 @@
     for part in range(PARTS):
         spread_ref[part] = one_hot(place == source - GROUP * part)
 
-    lane = lax.broadcasted_iota(jnp.int32, (288, 288), 1)
-    high, low = split(line(288, 0), 24)
-    step, row = split(low, WH)
-    regroup_ref[...] = one_hot(lane == step * 72 + high * WH + row)
-    step, low = split(line(288, 0), 72)
-    high, row = split(low, WH)
-    regroup_t_ref[...] = one_hot(lane == (high * GROUP + step) * WH + row)
-
-    place, chunk = split(line(288, 0), NLON)
-    at = chunk * 9 + place
-    high, hk = split(at >> 1, WH)
-    source = ((high & 1) * 2 + (at & 1)) * 72 + (high >> 1) * WH + hk
-    entry_ref[...] = one_hot(lane == source)
-
     high, low = split(line(SLOTS * 144, 0), 72)
     pair, hk = split(low, WH)
     source = ((pair * 2 + (high & 1)) * WH + hk) * 8 + (high >> 1)
@@ -96,12 +107,9 @@
         tables_kernel,
         out_shape=(
             jax.ShapeDtypeStruct((PARTS, LANES_V, WTOK), bf16),
-            jax.ShapeDtypeStruct((288, 288), bf16),
-            jax.ShapeDtypeStruct((288, 288), bf16),
-            jax.ShapeDtypeStruct((288, 288), bf16),
             jax.ShapeDtypeStruct((SLOTS * 144, 1152), bf16),
         ),
-        out_specs=(vmem(),) * 5,
+        out_specs=(vmem(),) * 2,
         compiler_params=params(16),
         cost_estimate=pl.CostEstimate(flops=6000000000, bytes_accessed=20000000, transcendentals=0),
         name="index_tables",
@@ -137,16 +145,7 @@
     table_ref,
     rows_ref,
     spread_ref,
-    regroup_ref,
-    wqkv_ref,
-    wproj_ref,
-    wup_ref,
-    wdown_t_ref,
     bias_ref,
-    wqkv_t_ref,
-    wproj_t_ref,
-    wup_t_ref,
-    wdown_ref,
     flat_s,
     line_s,
 ):
@@ -158,11 +157,7 @@
         line_s[i * 8 : i * 8 + 8, 0:138] = flat_s[:, 138 * i : 138 * i + 138]
     lines = mm(rows_ref[...], line_s[:, 0:138].astype(bf16))
 
-    transpose_into(wqkv_ref, wqkv_t_ref)
-    transpose_into(wproj_ref, wproj_t_ref)
-    transpose_into(wup_ref, wup_t_ref)
-    transpose_into(wdown_t_ref, wdown_ref)
-    regroup = regroup_ref[...]
+    regroup = regroup_matrix()
     blank = jnp.zeros((72, HALF_V - 138), f32)
     for slot in range(SLOTS):
         at = slot * 144
@@ -213,15 +208,90 @@
     return start, band_ref[lat]
 
 
-def main_kernel(
+def early_kernel(
     lat_ref,
-    half_ref,
     band_ref,
     shift_ref,
-    left_ref,
     own_t_ref,
     own_c_ref,
+    wqkv_ref,
+    wproj_ref,
+    wup_ref,
+    wdown_t_ref,
+    x_own_ref,
+    c_own_ref,
+    sel_l_ref,
+    sel_r_ref,
+    put_l_ref,
+    put_o_ref,
+    put_r_ref,
+    wqkv_t_ref,
+    wproj_t_ref,
+    wup_t_ref,
+    wdown_ref,
+    regroup_ref,
+    entry_ref,
+):
+    regroup_ref[...] = regroup_back_matrix()
+    entry_ref[...] = entry_matrix()
+    n_left, n_own, n_right = LEFT * LAT, WW * LAT, RIGHT * LAT
+
+    start, count = my_rows(lat_ref, band_ref)
+    at = []
+    for s in range(SLOTS):
+        shift = shift_ref[jnp.minimum(start + s, 2 * NLAT - 1)]
+        first = jnp.where(shift <= RIGHT, shift, shift - WW) + LEFT
+        at.append(jnp.where(s < count, first * LAT + s * WH, -100000))
+
+    def place(axis):
+        shape = (CELL_ROWS, 1) if axis == 0 else (1, CELL_ROWS)
+        cell = lax.broadcasted_iota(jnp.int32, shape, axis)
+        col = (cell * 43) >> 8
+        base = col * LAT + (cell - col * WH)
+        return jnp.concatenate([base + at[s] for s in range(SLOTS)], axis=axis)
+
+    goal = place(0)
+
+    def pick(first, count):
+        lane = lax.broadcasted_iota(jnp.int32, (288, count), 1)
+        return one_hot(goal - first == lane)
+
+    sel_l_ref[...] = pick(0, n_left)
+    sel_r_ref[...] = pick(n_left + n_own, n_right)
+    sel_o = pick(n_left, n_own)
+    for own_ref, into_ref in ((own_t_ref, x_own_ref), (own_c_ref, c_own_ref)):
+        for level in range(LEVELS):
+            got = mm(sel_o, own_ref[level])
+            for slot in range(SLOTS):
+                into_ref[slot, level * 72 : level * 72 + 72, :] = got[slot * 72 : slot * 72 + 72]
+
+    goal_t = place(1)
+
+    def put(first, count):
+        row = lax.broadcasted_iota(jnp.int32, (count, 288), 0)
+        return one_hot(goal_t - first == row)
+
+    put_l_ref[...] = put(0, n_left)
+    put_o_ref[...] = put(n_left, n_own)
+    put_r_ref[...] = put(n_left + n_own, n_right)
+
+    transpose_into(wqkv_ref, wqkv_t_ref)
+    transpose_into(wproj_ref, wproj_t_ref)
+    transpose_into(wup_ref, wup_t_ref)
+    transpose_into(wdown_t_ref, wdown_ref)
+
+
+def main_kernel(
+    half_ref,
+    left_ref,
     right_ref,
+    x_own_ref,
+    c_own_ref,
+    sel_l_ref,
+    sel_r_ref,
+    put_l_ref,
+    put_o_ref,
+    put_r_ref,
     bias_ref,
     wqkv_ref,
     wqkv_t_ref,
@@ -252,37 +322,15 @@
     ts_s,
     tt_s,
 ):
-    n_left, n_own, n_right = LEFT * LAT, WW * LAT, RIGHT * LAT
-
-    start, count = my_rows(lat_ref, band_ref)
-    at = []
-    for s in range(SLOTS):
-        shift = shift_ref[jnp.minimum(start + s, 2 * NLAT - 1)]
-        first = jnp.where(shift <= RIGHT, shift, shift - WW) + LEFT
-        at.append(jnp.where(s < count, first * LAT + s * WH, -100000))
-
-    def place(axis):
-        shape = (CELL_ROWS, 1) if axis == 0 else (1, CELL_ROWS)
-        cell = lax.broadcasted_iota(jnp.int32, shape, axis)
-        col = (cell * 43) >> 8
-        base = col * LAT + (cell - col * WH)
-        return jnp.concatenate([base + at[s] for s in range(SLOTS)], axis=axis)
-
-    goal = place(0)
-
-    def pick(first, count):
-        lane = lax.broadcasted_iota(jnp.int32, (288, count), 1)
-        return one_hot(goal - first == lane)
-
-    sel_l = pick(0, n_left)
-    sel_o = pick(n_left, n_own)
-    sel_r = pick(n_left + n_own, n_right)
-    for which, own_ref, scratch in ((0, own_t_ref, x_s), (1, own_c_ref, c_s)):
-        edge = mm(sel_l, left_ref[which]) + mm(sel_r, right_ref[which])
+    for which, own_ref, scratch in ((0, x_own_ref, x_s), (1, c_own_ref, c_s)):
+        edge = mm(sel_l_ref[...], left_ref[which]) + mm(sel_r_ref[...], right_ref[which])
         for level in range(LEVELS):
-            got = edge[:, level * WIDTH : (level + 1) * WIDTH] + mm(sel_o, own_ref[level])
             for slot in range(SLOTS):
-                scratch[slot, level * 72 : level * 72 + 72, :] = got[slot * 72 : slot * 72 + 72]
+                rows = slice(level * 72, level * 72 + 72)
+                scratch[slot, rows, :] = (
+                    own_ref[slot, rows, :]
+                    + edge[slot * 72 : slot * 72 + 72, level * WIDTH : (level + 1) * WIDTH]
+                )
 
     acc_s[...] = jnp.zeros_like(acc_s)
     accd_s[...] = jnp.zeros_like(accd_s)
@@ -428,13 +476,6 @@
             both = jnp.concatenate([top, low], axis=0)
             wsum_ref[x * NLAT + i] = jnp.concatenate([both] + down, axis=1).astype(bf16)
 
-    goal_t = place(1)
-
-    def put(first, count):
-        row = lax.broadcasted_iota(jnp.int32, (count, 288), 0)
-        return one_hot(goal_t - first == row)
-
-    put_l, put_o, put_r = put(0, n_left), put(n_left, n_own), put(n_left + n_own, n_right)
     for which, scratch in ((0, ro_s), (1, rg_s)):
         levels = [
             jnp.concatenate(
@@ -443,37 +484,18 @@
             for level in range(LEVELS)
         ]
         for level in range(LEVELS):
-            out_own_ref[which, level] = mm(put_o, levels[level].astype(bf16)).astype(bf16)
+            out_own_ref[which, level] = mm(put_o_ref[...], levels[level].astype(bf16)).astype(bf16)
         rows = jnp.concatenate(levels, axis=1).astype(bf16)
-        out_left_ref[which] = mm(put_l, rows).astype(bf16)
-        out_right_ref[which] = mm(put_r, rows).astype(bf16)
+        out_left_ref[which] = mm(put_l_ref[...], rows).astype(bf16)
+        out_right_ref[which] = mm(put_r_ref[...], rows).astype(bf16)
 
 
 def mid_kernel(
     w_ref,
     keep_ref,
     got_ref,
-    own_ref,
-    from_left_ref,
-    from_right_ref,
     out_ref,
-    cells_ref,
-    grad_ref,
 ):
-    for which, ref in ((0, cells_ref), (1, grad_ref)):
-        for level in range(LEVELS):
-            lanes = slice(level * WIDTH, (level + 1) * WIDTH)
-            own = own_ref[which, level].astype(f32)
-            first, last = from_left_ref[which], from_right_ref[which]
-            near, far = RIGHT * LAT, (WW - LEFT) * LAT
-            ref[level] = jnp.concatenate(
-                [
-                    own[:near] + first.astype(f32)[:, lanes],
-                    own[near:far],
-                    own[far:] + last.astype(f32)[:, lanes],
-                ],
-                axis=0,
-            ).astype(bf16)
     total = w_ref[0].astype(f32)
     for i in range(1, 2 * NLAT):
         total = total + w_ref[i].astype(f32)
@@ -493,20 +515,49 @@
                 ),
                 up[:, 24 * z : 24 * z + 24],
                 jnp.concatenate([piece[:, 6 * z : 6 * z + 6] for piece in down], axis=1),
-                jnp.zeros((PER_Z - 36, 24), f32),
             ],
             axis=0,
         )
         table = keep_ref[z, :, 0:69].astype(f32) + got_ref[z, :, 0:69].astype(f32)
+        rest = jnp.concatenate(
+            [
+                jnp.concatenate([table[32:36, 23 * n : 23 * n + 23] for n in range(3)], axis=0),
+                part[32:36, 0:23],
+            ],
+            axis=0,
+        )
+        rest = jnp.concatenate([rest, jnp.zeros((SEND - 16, 23), f32)], axis=0)
+        last = jnp.concatenate([jnp.zeros((12, 1), f32), part[32:36, 23:24]], axis=0)
+        last = jnp.concatenate([last, jnp.zeros((SEND - 16, 1), f32)], axis=0)
         out_ref[z] = jnp.concatenate(
-            [table, part, jnp.zeros((PER_Z, 128 - 93), f32)], axis=1
+            [table[0:SEND], part[0:SEND], rest, last, jnp.zeros((SEND, 11), f32)], axis=1
         ).astype(bf16)
+
+
+def cells_kernel(own_ref, from_left_ref, from_right_ref, cells_ref, grad_ref):
+    for which, ref in ((0, cells_ref), (1, grad_ref)):
+        for level in range(LEVELS):
+            lanes = slice(level * WIDTH, (level + 1) * WIDTH)
+            own = own_ref[which, level].astype(f32)
+            first, last = from_left_ref[which], from_right_ref[which]
+            near, far = RIGHT * LAT, (WW - LEFT) * LAT
+            ref[level] = jnp.concatenate(
+                [
+                    own[:near] + first.astype(f32)[:, lanes],
+                    own[near:far],
+                    own[far:] + last.astype(f32)[:, lanes],
+                ],
+                axis=0,
+            ).astype(bf16)
 
 
 def fin_kernel(scale, lat_ref, band_ref, in_ref, qkv_ref, proj_ref, up_ref, down_ref, route_ref):
     total = in_ref[0].astype(f32)
     for i in range(1, Z):
         total = total + in_ref[i].astype(f32)
+    extra = jnp.concatenate([total[4 * n : 4 * n + 4, 93:116] for n in range(3)], axis=1)
+    extra = jnp.concatenate([extra, total[12:16, 93:117], jnp.zeros((4, 35), f32)], axis=1)
+    total = jnp.concatenate([total, extra], axis=0)
     qkv_ref[...] = total[0:12, 69:87] * scale
     proj_ref[...] = total[0:12, 87:93] * scale
     up_ref[...] = total[12:24, 69:93] * scale
@@ -554,28 +605,38 @@
     return lax.ppermute(x, "lon", [(i, (i + by) % count) for i in range(count)])
 
 
-def prepare(lat, band_rows, bias_table, tables, w_qkv, w_proj, w_up, w_down):
-    w_down_t = w_down.T
-    bias, w_qkv_t, w_proj_t, w_up_t, w_down = pl.pallas_call(
+def prepare(lat, band_rows, bias_table, tables):
+    return pl.pallas_call(
         prep_kernel,
-        out_shape=(
-            jax.ShapeDtypeStruct((SLOTS, WTOK, ALL_Q), f32),
-            jax.ShapeDtypeStruct((3 * WIDTH, WIDTH), bf16),
-            jax.ShapeDtypeStruct((WIDTH, WIDTH), bf16),
-            jax.ShapeDtypeStruct((HID, WIDTH), bf16),
-            jax.ShapeDtypeStruct((HID, WIDTH), bf16),
-        ),
-        in_specs=[smem()] * 2 + [vmem()] * 8,
-        out_specs=(vmem(),) * 5,
+        out_shape=jax.ShapeDtypeStruct((SLOTS, WTOK, ALL_Q), f32),
+        in_specs=[smem()] * 2 + [vmem()] * 3,
+        out_specs=vmem(),
         scratch_shapes=[pltpu.VMEM((8, HEADS * POS), f32), pltpu.VMEM((1152, HALF_V), f32)],
         compiler_params=params(24),
         cost_estimate=pl.CostEstimate(flops=1000000000, bytes_accessed=6000000, transcendentals=0),
         name="prepare",
-    )(lat, band_rows, bias_table, *tables, w_qkv, w_proj, w_up, w_down_t)
-    return bias, (w_qkv, w_qkv_t, w_proj, w_proj_t, w_up, w_up_t, w_down, w_down_t)
-
-
-def block_pass(lat, half, band_rows, lon_shift, left, own_t, own_c, right, bias, weights, tables):
+    )(lat, band_rows, bias_table, *tables)
+
+
+def early_part(lat, band_rows, lon_shift, own_t, own_c, w_qkv, w_proj, w_up, w_down_t):
+    windows = jax.ShapeDtypeStruct((SLOTS, WTOK, WIDTH), f32)
+    n_left, n_own, n_right = LEFT * LAT, WW * LAT, RIGHT * LAT
+    shapes = ((288, n_left), (288, n_right), (n_left, 288), (n_own, 288), (n_right, 288))
+    flips = ((3 * WIDTH, WIDTH), (WIDTH, WIDTH), (HID, WIDTH), (HID, WIDTH))
+    flips = flips + ((288, 288), (288, 288))
+    return pl.pallas_call(
+        early_kernel,
+        out_shape=(windows, windows)
+        + tuple(jax.ShapeDtypeStruct(shape, bf16) for shape in shapes + flips),
+        in_specs=[smem()] * 3 + [vmem()] * 6,
+        out_specs=(vmem(),) * 13,
+        compiler_params=params(24),
+        cost_estimate=pl.CostEstimate(flops=1000000000, bytes_accessed=6000000, transcendentals=0),
+        name="own_cells",
+    )(lat, band_rows, lon_shift, own_t, own_c, w_qkv, w_proj, w_up, w_down_t)
+
+
+def block_pass(half, left, right, early, bias, weights, tables):
     return pl.pallas_call(
         main_kernel,
         out_shape=(
@@ -586,7 +647,7 @@
             jax.ShapeDtypeStruct((Z, PER_Z, 128), bf16),
             jax.ShapeDtypeStruct((Z, PER_Z, 128), bf16),
         ),
-        in_specs=[smem()] * 4 + [vmem()] * 16,
+        in_specs=[smem()] + [vmem()] * 21,
         out_specs=(vmem(),) * 6,
         scratch_shapes=[
             pltpu.VMEM((SLOTS, WTOK, WIDTH), f32),
@@ -603,7 +664,7 @@
         ],
         compiler_params=params(32),
         name="block_pass",
-    )(lat, half, band_rows, lon_shift, left, own_t, own_c, right, bias, *weights, *tables)
+    )(half, left, right, *early, bias, *weights, *tables)
 
 
 def local(tokens, cotangent, w_qkv, w_proj, w_up, w_down, bias_table, band_rows, lon_shift):
@@ -613,7 +674,7 @@
 
     own_t = tokens.transpose(0, 2, 1, 3).reshape(LEVELS, WW * LAT, WIDTH)
     own_c = cotangent.transpose(0, 2, 1, 3).reshape(LEVELS, WW * LAT, WIDTH)
-    spread, regroup, regroup_t, entry, rows = make_tables()
+    spread, rows = make_tables()
     to_right, to_left = pl.pallas_call(
         pack_kernel,
         out_shape=(
@@ -624,42 +685,48 @@
         out_specs=(vmem(),) * 2,
         compiler_params=params(16),
         name="pack_edges",
-    )(regroup, own_t, own_c)
+    )(rows, own_t, own_c)
     left = to_lon(to_right, 1)
     right = to_lon(to_left, -1)
 
-    bias, weights = prepare(
-        lat, band_rows, bias_table, (rows, spread, regroup), w_qkv, w_proj, w_up, w_down
+    bias = prepare(lat, band_rows, bias_table, (rows, spread))
+    w_down_t = w_down.T
+    early = early_part(
+        lat, band_rows, lon_shift, own_t, own_c, w_qkv, w_proj, w_up, w_down_t
     )
+    flip = early[7:]
+    weights = (w_qkv, flip[0], w_proj, flip[1], w_up, flip[2], flip[3], w_down_t)
     out_left, out_own, out_right, w_sums, t_keep, t_give = block_pass(
-        lat,
-        half,
-        band_rows,
-        lon_shift,
-        left,
-        own_t,
-        own_c,
-        right,
-        bias,
-        weights,
-        (spread, regroup_t, entry),
+        half, left, right, early[:7], bias, weights, (spread, flip[4], flip[5])
     )
 
+    t_got = to_lon(t_give, Z)
     from_right = to_lon(out_left, -1)
     from_left = to_lon(out_right, 1)
-    t_got = to_lon(t_give, Z)
     near = [[(x * Z + z) * NLAT + i for x in range(2) for i in range(NLAT)] for z in range(Z)]
     ring = [[x * Z + z for z in range(Z)] for x in range(2)]
     w_got = lax.all_to_all(w_sums, ("lon", "lat"), 0, 0, axis_index_groups=near)
     cells_shape = jax.ShapeDtypeStruct((LEVELS, WW * LAT, WIDTH), bf16)
-    lon_send, cells, grads = pl.pallas_call(
+    w_got, t_got, from_left, from_right = lax.optimization_barrier(
+        (w_got, t_got, from_left, from_right)
+    )
+    cells, grads = pl.pallas_call(
+        cells_kernel,
+        out_shape=(cells_shape, cells_shape),
+        in_specs=[vmem()] * 3,
+        out_specs=(vmem(),) * 2,
+        compiler_params=params(16),
+        cost_estimate=pl.CostEstimate(flops=100000000, bytes_accessed=3000000, transcendentals=0),
+        name="join_cells",
+    )(out_own, from_left, from_right)
+    lon_send = pl.pallas_call(
         mid_kernel,
-        out_shape=(jax.ShapeDtypeStruct((Z, PER_Z, 128), bf16), cells_shape, cells_shape),
-        in_specs=[vmem()] * 6,
-        out_specs=(vmem(),) * 3,
+        out_shape=jax.ShapeDtypeStruct((Z, SEND, 128), bf16),
+        in_specs=[vmem()] * 3,
+        out_specs=vmem(),
         compiler_params=params(24),
         name="sum_lat",
-    )(w_got, t_keep, t_got, out_own, from_left, from_right)
+    )(w_got, t_keep, t_got)
     output = cells.reshape(LEVELS, WW, LAT, WIDTH).transpose(0, 2, 1, 3)
     grad_tokens = grads.reshape(LEVELS, WW, LAT, WIDTH).transpose(0, 2, 1, 3)
 

time: 108 us -> 106 us (0.981)
  local copies, waits for them, and re-layouts: 5.88 us -> 2.52 us
  Pallas kernels: 23.9 us -> 26 us
    unnamed x40 -> x28, local copies, waits for them, and re-layouts: 5.88 us -> 2.52 us
    pallas_call x2 -> x4, Pallas kernels: 5.57 us -> 8.5 us  [the longest x1 4.05 us: prepare(): pl.pallas_call(prep_kernel, out_shape=jax.ShapeDtypeStruct((SLOTS, WTOK,...]
    ppermute x5, waiting for transfers between devices: 10.3 us -> 12 us  [to_lon(): return lax.ppermute(x, 'lon', [(i, (i + by) % count) for i in range(count)])]
  transfers between devices with their start and end apart: 7 -> 7, of which waited for: 3 -> 4; matrix products, arithmetic and copies ran while one was open for 1% -> 1% of each run, Pallas kernels for 4% -> 6%
where the time goes in v3:
time: 106 us
  starting transfers between devices  43.8 us (41%)
  Pallas kernels  26 us (25%)
  waiting for transfers between devices  17.7 us (17%)
  blocking collectives  14.6 us (14%)
  local copies, waits for them, and re-layouts  2.52 us (2%)
    ppermute x5, starting transfers between devices, to_lon(): return lax.ppermute(x, 'lon', [(i, (i + by) % count) for i in range(count)])  25.5 us
    all_to_all x1, blocking collectives, local(): lon_got = lax.all_to_all(lon_send, 'lon', 0, 0, axis_index_groups=ring)  14.6 us
    pallas_call x1, Pallas kernels, block_pass(): pl.pallas_call(main_kernel, out_shape=(jax.ShapeDtypeStruct((2, LEFT * LA...  14 us
    ppermute x5, waiting for transfers between devices, to_lon(): return lax.ppermute(x, 'lon', [(i, (i + by) % count) for i in range(count)])  12 us
    all_to_all x1, starting transfers between devices, local(): route_got = lax.all_to_all(route, 'lat', 0, 0)  9.5 us
    all_to_all x1, starting transfers between devices, local(): w_got = lax.all_to_all(w_sums, ('lon', 'lat'), 0, 0, axis_index_groups=near)  8.79 us
    all_to_all x1, waiting for transfers between devices, local(): route_got = lax.all_to_all(route, 'lat', 0, 0)  5.31 us
    pallas_call x1, Pallas kernels, prepare(): pl.pallas_call(prep_kernel, out_shape=jax.ShapeDtypeStruct((SLOTS, WTOK,...  4.05 us
  transfers between devices with their start and end apart: 7, of which 4 were waited for; matrix products, arithmetic and copies ran while one was open for 1% of the time, Pallas kernels for 6%

profile of v3, /device:TPU:1, one launch (start us, length us, event | category | flops | bytes accessed | tf_op | source)
XLA Modules:
  0.0 105.5 jit_solution(4581663242450603554)
XLA Ops:
  0.6 0.0 copy-start.5
  0.6 0.0 copy-start.3
  0.7 0.6 index_tables.1
  1.2 0.0 copy-start
  1.2 0.0 copy-start.9
  1.2 0.4 copy-done.5
  1.6 0.1 copy-done.3
  1.7 0.9 pack_edges.1
  2.6 12.9 %collective-permute-start.1 = (bf16[2,144,384]{2,1,0:T(8,128)(2,1)}, bf16[2,144,384]{2,1,0:T(8,128)(2,1)}, u32[]{:S(2)}, u32[]{:S(2)}) collective-permute-start(bf16[2,144,384]{2,1,0:T(8,128)(2,1)} %get-tuple-element.43), channel_id=1, source_target_pairs={{0,496},{16,0},{32,16},{48,32},{64,48},{80,64},{96,80},{112,96},{1... | collective-permute-start | bytes 663560 | tf_op jit(solution)/shard_map/ppermute | solution.py:605
  15.4 1.9 %collective-permute-start = (bf16[2,120,384]{2,1,0:T(8,128)(2,1)}, bf16[2,120,384]{2,1,0:T(8,128)(2,1)}, u32[]{:S(2)}, u32[]{:S(2)}) collective-permute-start(bf16[2,120,384]{2,1,0:T(8,128)(2,1)} %get-tuple-element.42), channel_id=1, source_target_pairs={{0,16},{16,32},{32,48},{48,64},{64,80},{80,96},{96,112},{112,128},... | collective-permute-start | bytes 552968 | tf_op jit(solution)/shard_map/ppermute | solution.py:605
  17.4 0.0 copy-start.4
  17.4 0.0 copy-start.6
  17.5 4.1 %prepare.1.bias_ref = f32[4,144,864]{2,1,0:T(8,128)S(1)} custom-call(s32[1]{0:T(128)} %bitcast.5.lat_ref, s32[16]{0:T(128)S(1)} %copy-done.9, bf16[32,19872]{1,0:T(8,128)(2,1)S(1)} %copy-done, bf16[576,1152]{1,0:T(8,128)(2,1)S(1)} %get-tuple-element.41.order_ref.rows_ref, bf16[3,512,144]{2,1,0:T(8,128)(2,1)S(1)} %get-tuple-element.51.spread_ref), custom_call_target="tpu_custom_call" | custom-call | flops 1000000000 | bytes 6000000 | tf_op jit(solution)/shard_map/prepare/pallas_call | solution.py:609
  21.6 1.6 %own_cells.1 = (f32[4,144,192]{2,1,0:T(8,128)S(1)}, f32[4,144,192]{2,1,0:T(8,128)S(1)}, bf16[288,120]{1,0:T(8,128)(2,1)S(1)}, bf16[288,144]{1,0:T(8,128)(2,1)S(1...) custom-call(s32[1]{0:T(128)} %bitcast.5.lat_ref, ...), custom_call_target="tpu_custom_call" | custom-call | flops 1000000000 | bytes 6000000 | tf_op jit(solution)/shard_map/own_cells/pallas_call | solution.py:627
  23.3 1.7 %collective-permute-done.left_ref = bf16[2,120,384]{2,1,0:T(8,128)(2,1)} collective-permute-done((bf16[2,120,384]{2,1,0:T(8,128)(2,1)}, bf16[2,120,384]{2,1,0:T(8,128)(2,1)}, u32[]{:S(2)}, u32[]{:S(2)}) %collective-permute-start) | collective-permute-done | bytes 184352 | tf_op jit(solution)/shard_map/ppermute | solution.py:605
  24.9 14.0 %block_pass.1 = (bf16[2,120,384]{2,1,0:T(8,128)(2,1)S(1)}, bf16[2,2,288,192]{3,2,1,0:T(8,128)(2,1)S(1)}, bf16[2,144,384]{2,1,0:T(8,128)(2,1)S(1)}, bf16[32,24,57...) custom-call(s32[1]{0:T(128)} %bitcast.half_ref, ...), custom_call_target="tpu_custom_call" | custom-call | tf_op jit(solution)/shard_map/block_pass/pallas_call | solution.py:640
  38.9 0.7 copy-done.10
  39.6 8.8 %all-to-all-start = ((bf16[32,24,576]{2,1,0:T(8,128)(2,1)}), bf16[32,24,576]{2,1,0:T(8,128)(2,1)S(1)}, u32[]{:S(2)}, u32[]{:S(2)}) async-start(bf16[32,24,576]{2,1,0:T(8,128)(2,1)} %get-tuple-element.59), calls=%async_computation | async-start | bytes 1966080 | tf_op jit(solution)/shard_map/all_to_all | solution.py:708
  48.4 1.9 %collective-permute-start.3 = (bf16[2,144,384]{2,1,0:T(8,128)(2,1)S(1)}, bf16[2,144,384]{2,1,0:T(8,128)(2,1)S(1)}, u32[]{:S(2)}, u32[]{:S(2)}) collective-permute-start(bf16[2,144,384]{2,1,0:T(8,128)(2,1)S(1)} %get-tuple-element.61), channel_id=1, source_target_pairs={{0,16},{16,32},{32,48},{48,64},{64,80},{80,96},{96,112},{112,128},... | collective-permute-start | bytes 663560 | tf_op jit(solution)/shard_map/ppermute | solution.py:605
  50.3 5.5 %collective-permute-start.4 = (bf16[2,120,384]{2,1,0:T(8,128)(2,1)S(1)}, bf16[2,120,384]{2,1,0:T(8,128)(2,1)S(1)}, u32[]{:S(2)}, u32[]{:S(2)}) collective-permute-start(bf16[2,120,384]{2,1,0:T(8,128)(2,1)S(1)} %get-tuple-element.62), channel_id=1, source_target_pairs={{0,496},{16,0},{32,16},{48,32},{64,48},{80,64},{96,80},{112,96},{1... | collective-permute-start | bytes 552968 | tf_op jit(solution)/shard_map/ppermute | solution.py:605
  55.8 3.3 %collective-permute-start.2 = (bf16[16,40,128]{2,1,0:T(8,128)(2,1)S(1)}, bf16[16,40,128]{2,1,0:T(8,128)(2,1)S(1)}, u32[]{:S(2)}, u32[]{:S(2)}) collective-permute-start(bf16[16,40,128]{2,1,0:T(8,128)(2,1)S(1)} %copy-done.11), channel_id=1, source_target_pairs={{0,256},{16,272},{32,288},{48,304},{64,320},{80,336},{96,352},{112... | collective-permute-start | bytes 491528 | tf_op jit(solution)/shard_map/ppermute | solution.py:605
  59.1 10.3 %collective-permute-done.2.got_ref = bf16[16,40,128]{2,1,0:T(8,128)(2,1)S(1)} collective-permute-done((bf16[16,40,128]{2,1,0:T(8,128)(2,1)S(1)}, bf16[16,40,128]{2,1,0:T(8,128)(2,1)S(1)}, u32[]{:S(2)}, u32[]{:S(2)}) %collective-permute-start.2) | collective-permute-done | bytes 163872 | tf_op jit(solution)/shard_map/ppermute | solution.py:605
  69.5 0.4 all-to-all-done.w_ref
  69.8 1.8 %sum_lat.1 = bf16[16,32,128]{2,1,0:T(8,128)(2,1)S(1)} custom-call(bf16[32,24,576]{2,1,0:T(8,128)(2,1)S(1)} %all-to-all-done.w_ref, bf16[16,40,128]{2,1,0:T(8,128)(2,1)S(1)} %get-tuple-element.68.keep_ref, bf16[16,40,128]{2,1,0:T(8,128)(2,1)S(1)} %collective-permute-done.2.got_ref), custom_call_target="tpu_custom_call" | custom-call | tf_op jit(solution)/shard_map/sum_lat/pallas_call | solution.py:722
  71.7 14.6 %all_to_all.15.in_ref = bf16[16,32,128]{2,1,0:T(8,128)(2,1)S(1)} all-to-all(bf16[16,32,128]{2,1,0:T(8,128)(2,1)S(1)} %sum_lat.1), channel_id=1, replica_groups={{0,16,32,48,64,80,96,112,128,144,160,176,192,208,224,240},{256,272,288,..., dimensions={0} | all-to-all | bytes 262144 | tf_op jit(solution)/shard_map/all_to_all | solution.py:733
  86.3 1.4 %sum_lon.1 = (f32[12,18]{1,0:T(8,128)}, f32[12,6]{1,0:T(8,128)S(1)}, f32[12,24]{1,0:T(8,128)}, f32[48,6]{1,0:T(8,128)S(1)}, bf16[16,32,128]{2,1,0:T(8,128)(2,1)}) custom-call(s32[1]{0:T(128)} %bitcast.5.lat_ref, s32[16]{0:T(128)S(1)} %copy-done.9, bf16[16,32,128]{2,1,0:T(8,128)(2,1)S(1)} %all_to_all.15.in_ref), custom_call_target="tpu_custom_call" | custom-call | tf_op jit(solution)/shard_map/sum_lon/pallas_call | solution.py:735
  87.7 9.5 %all-to-all-start.2 = ((bf16[16,32,128]{2,1,0:T(8,128)(2,1)}), bf16[16,32,128]{2,1,0:T(8,128)(2,1)S(1)}, u32[]{:S(2)}, u32[]{:S(2)}) async-start(bf16[16,32,128]{2,1,0:T(8,128)(2,1)} %get-tuple-element.74), calls=%async_computation.2 | async-start | bytes 262144 | tf_op jit(solution)/shard_map/all_to_all | solution.py:749
  97.2 1.0 join_cells.1
  98.2 0.7 copy.16
  98.8 0.7 copy.17
  99.5 5.3 %all-to-all-done.2.in_ref = bf16[16,32,128]{2,1,0:T(8,128)(2,1)S(1)} async-done(((bf16[16,32,128]{2,1,0:T(8,128)(2,1)}), bf16[16,32,128]{2,1,0:T(8,128)(2,1)S(1)}, u32[]{:S(2)}, u32[]{:S(2)}) %all-to-all-start.2) | async-done | bytes 131104 | tf_op jit(solution)/shard_map/all_to_all | solution.py:749
  104.8 0.7 sum_table.1
  (20 shorter events, 0.1 us)
Async XLA Ops:
  0.6 1.0 copy-start.5
  0.6 1.0 copy-start.3
  1.2 16.2 %copy-start = (bf16[32,19872]{1,0:T(8,128)(2,1)S(1)}, bf16[32,19872]{1,0:T(8,128)(2,1)}, u32[]{:S(2)}) copy-start(bf16[32,19872]{1,0:T(8,128)(2,1)} %table_ref.1) | copy-start | bytes 3815428
  1.2 16.2 %copy-start.9 = (s32[16]{0:T(128)S(1)}, s32[16]{0:T(128)}, u32[]{:S(2)}) copy-start(s32[16]{0:T(128)} %band_ref.5) | copy-start | bytes 196
  2.6 22.4 %collective-permute-start.1 = (bf16[2,144,384]{2,1,0:T(8,128)(2,1)}, bf16[2,144,384]{2,1,0:T(8,128)(2,1)}, u32[]{:S(2)}, u32[]{:S(2)}) collective-permute-start(bf16[2,144,384]{2,1,0:T(8,128)(2,1)} %get-tuple-element.43), channel_id=1, source_target_pairs={{0,496},{16,0},{32,16},{48,32},{64,48},{80,64},{96,80},{112,96},{1... | collective-permute-start | bytes 663560 | tf_op jit(solution)/shard_map/ppermute | solution.py:605
  15.4 9.5 %collective-permute-start = (bf16[2,120,384]{2,1,0:T(8,128)(2,1)}, bf16[2,120,384]{2,1,0:T(8,128)(2,1)}, u32[]{:S(2)}, u32[]{:S(2)}) collective-permute-start(bf16[2,120,384]{2,1,0:T(8,128)(2,1)} %get-tuple-element.42), channel_id=1, source_target_pairs={{0,16},{16,32},{32,48},{48,64},{64,80},{80,96},{96,112},{112,128},... | collective-permute-start | bytes 552968 | tf_op jit(solution)/shard_map/ppermute | solution.py:605
  17.4 4.1 %copy-start.1 = (bf16[192,768]{1,0:T(8,128)(2,1)S(1)}, bf16[192,768]{1,0:T(8,128)(2,1)}, u32[]{:S(2)}) copy-start(bf16[192,768]{1,0:T(8,128)(2,1)} %wup_ref.3) | copy-start | bytes 884740
  17.4 4.1 %copy-start.2 = (bf16[768,192]{0,1:T(8,128)(2,1)S(1)}, bf16[768,192]{0,1:T(8,128)(2,1)}, u32[]{:S(2)}) copy-start(bf16[768,192]{0,1:T(8,128)(2,1)} %param.14) | copy-start | bytes 884740
  17.4 4.1 %copy-start.4 = (bf16[2,24,12,192]{3,1,2,0:T(8,128)(2,1)S(1)}, bf16[2,24,12,192]{3,1,2,0:T(8,128)(2,1)}, u32[]{:S(2)}) copy-start(bf16[2,24,12,192]{3,1,2,0:T(8,128)(2,1)} %param.9) | copy-start | bytes 663556
  17.4 4.1 %copy-start.6 = (bf16[2,24,12,192]{3,1,2,0:T(8,128)(2,1)S(1)}, bf16[2,24,12,192]{3,1,2,0:T(8,128)(2,1)}, u32[]{:S(2)}) copy-start(bf16[2,24,12,192]{3,1,2,0:T(8,128)(2,1)} %param.10) | copy-start | bytes 663556
  17.4 4.1 %copy-start.7 = (bf16[192,576]{1,0:T(8,128)(2,1)S(1)}, bf16[192,576]{1,0:T(8,128)(2,1)}, u32[]{:S(2)}) copy-start(bf16[192,576]{1,0:T(8,128)(2,1)} %wqkv_ref.3) | copy-start | bytes 663556
  17.5 4.1 %copy-start.8 = (bf16[192,192]{1,0:T(8,128)(2,1)S(1)}, bf16[192,192]{1,0:T(8,128)(2,1)}, u32[]{:S(2)}) copy-start(bf16[192,192]{1,0:T(8,128)(2,1)} %wproj_ref.3) | copy-start | bytes 221188
  17.5 4.1 %copy-start.12 = (s32[32]{0:T(128)S(1)}, s32[32]{0:T(128)}, u32[]{:S(2)}) copy-start(s32[32]{0:T(128)} %shift_ref.1) | copy-start | bytes 388
  38.9 0.7 copy-start.10
  39.6 16.2 %copy-start.11 = (bf16[16,40,128]{2,1,0:T(8,128)(2,1)S(1)}, bf16[16,40,128]{2,1,0:T(8,128)(2,1)}, u32[]{:S(2)}) copy-start(bf16[16,40,128]{2,1,0:T(8,128)(2,1)} %copy-done.10) | copy-start | bytes 491524
  39.6 30.2 %all-to-all-start = ((bf16[32,24,576]{2,1,0:T(8,128)(2,1)}), bf16[32,24,576]{2,1,0:T(8,128)(2,1)S(1)}, u32[]{:S(2)}, u32[]{:S(2)}) async-start(bf16[32,24,576]{2,1,0:T(8,128)(2,1)} %get-tuple-element.59), calls=%async_computation | async-start | bytes 1966080 | tf_op jit(solution)/shard_map/all_to_all | solution.py:708
  48.4 21.0 %collective-permute-start.3 = (bf16[2,144,384]{2,1,0:T(8,128)(2,1)S(1)}, bf16[2,144,384]{2,1,0:T(8,128)(2,1)S(1)}, u32[]{:S(2)}, u32[]{:S(2)}) collective-permute-start(bf16[2,144,384]{2,1,0:T(8,128)(2,1)S(1)} %get-tuple-element.61), channel_id=1, source_target_pairs={{0,16},{16,32},{32,48},{48,64},{64,80},{80,96},{96,112},{112,128},... | collective-permute-start | bytes 663560 | tf_op jit(solution)/shard_map/ppermute | solution.py:605
  50.3 19.1 %collective-permute-start.4 = (bf16[2,120,384]{2,1,0:T(8,128)(2,1)S(1)}, bf16[2,120,384]{2,1,0:T(8,128)(2,1)S(1)}, u32[]{:S(2)}, u32[]{:S(2)}) collective-permute-start(bf16[2,120,384]{2,1,0:T(8,128)(2,1)S(1)} %get-tuple-element.62), channel_id=1, source_target_pairs={{0,496},{16,0},{32,16},{48,32},{64,48},{80,64},{96,80},{112,96},{1... | collective-permute-start | bytes 552968 | tf_op jit(solution)/shard_map/ppermute | solution.py:605
  55.8 13.6 %collective-permute-start.2 = (bf16[16,40,128]{2,1,0:T(8,128)(2,1)S(1)}, bf16[16,40,128]{2,1,0:T(8,128)(2,1)S(1)}, u32[]{:S(2)}, u32[]{:S(2)}) collective-permute-start(bf16[16,40,128]{2,1,0:T(8,128)(2,1)S(1)} %copy-done.11), channel_id=1, source_target_pairs={{0,256},{16,272},{32,288},{48,304},{64,320},{80,336},{96,352},{112... | collective-permute-start | bytes 491528 | tf_op jit(solution)/shard_map/ppermute | solution.py:605
  87.7 17.2 %all-to-all-start.2 = ((bf16[16,32,128]{2,1,0:T(8,128)(2,1)}), bf16[16,32,128]{2,1,0:T(8,128)(2,1)S(1)}, u32[]{:S(2)}, u32[]{:S(2)}) async-start(bf16[16,32,128]{2,1,0:T(8,128)(2,1)} %get-tuple-element.74), calls=%async_computation.2 | async-start | bytes 262144 | tf_op jit(solution)/shard_map/all_to_all | solution.py:749

commit v4 on v3

--- a/solution.py
+++ b/solution.py
@@ -564,18 +564,14 @@
     down_ref[...] = (
         jnp.concatenate([total[24:36, 69 + 6 * g : 75 + 6 * g] for g in range(4)], axis=0) * scale
     )
-    table = total[0:36].astype(bf16).astype(f32)
+    table = total[0:36].astype(bf16)
     start, count = my_rows(lat_ref, band_ref)
-    goes = [jnp.where(slot < count, start + slot, -1) for slot in range(SLOTS)]
-    for i in range(NLAT):
-        for j in range(2):
-            mine = jnp.zeros((9, 128), f32)
-            for slot in range(SLOTS):
-                hit = jnp.where(goes[slot] == 2 * i + j, 1.0, 0.0)
-                mine = mine + hit * table[slot * 9 : slot * 9 + 9]
-            route_ref[i, j * 16 : j * 16 + 16, :] = jnp.concatenate(
-                [mine, jnp.zeros((7, 128), f32)], axis=0
-            ).astype(bf16)
+    spot = line(NLAT * 32, 0)
+    row, place = spot >> 4, spot & 15
+    live = (row >= start) & (row < start + count) & (place < 9)
+    wanted = jnp.where(live, (row - start) * 9 + place, -1)
+    hits = one_hot(lax.broadcasted_iota(jnp.int32, (NLAT * 32, 36), 1) == wanted)
+    route_ref[...] = mm(hits, table).reshape(NLAT, 32, 128).astype(bf16)
 
 
 def table_kernel(in_ref, out_ref):
@@ -707,8 +703,16 @@
     ring = [[x * Z + z for z in range(Z)] for x in range(2)]
     w_got = lax.all_to_all(w_sums, ("lon", "lat"), 0, 0, axis_index_groups=near)
     cells_shape = jax.ShapeDtypeStruct((LEVELS, WW * LAT, WIDTH), bf16)
-    w_got, t_got, from_left, from_right = lax.optimization_barrier(
-        (w_got, t_got, from_left, from_right)
+    lon_send = pl.pallas_call(
+        mid_kernel,
+        out_shape=jax.ShapeDtypeStruct((Z, SEND, 128), bf16),
+        in_specs=[vmem()] * 3,
+        out_specs=vmem(),
+        compiler_params=params(24),
+        name="sum_lat",
+    )(w_got, t_keep, t_got)
+    lon_send, from_left, from_right = lax.optimization_barrier(
+        (lon_send, from_left, from_right)
     )
     cells, grads = pl.pallas_call(
         cells_kernel,
@@ -719,14 +723,6 @@
         cost_estimate=pl.CostEstimate(flops=100000000, bytes_accessed=3000000, transcendentals=0),
         name="join_cells",
     )(out_own, from_left, from_right)
-    lon_send = pl.pallas_call(
-        mid_kernel,
-        out_shape=jax.ShapeDtypeStruct((Z, SEND, 128), bf16),
-        in_specs=[vmem()] * 3,
-        out_specs=vmem(),
-        compiler_params=params(24),
-        name="sum_lat",
-    )(w_got, t_keep, t_got)
     output = cells.reshape(LEVELS, WW, LAT, WIDTH).transpose(0, 2, 1, 3)
     grad_tokens = grads.reshape(LEVELS, WW, LAT, WIDTH).transpose(0, 2, 1, 3)
 

time: 106 us -> 106 us (level)
  transfers between devices with their start and end apart: 7 -> 7, of which waited for: 4 -> 4; matrix products, arithmetic and copies ran while one was open for 1% -> 1% of each run, Pallas kernels for 6% -> 8%
where the time goes in v4:
time: 106 us
  starting transfers between devices  43.8 us (41%)
  Pallas kernels  26.1 us (25%)
  waiting for transfers between devices  17.7 us (17%)
  blocking collectives  14.6 us (14%)
  local copies, waits for them, and re-layouts  2.52 us (2%)
    ppermute x5, starting transfers between devices, to_lon(): return lax.ppermute(x, 'lon', [(i, (i + by) % count) for i in range(count)])  25.5 us
    all_to_all x1, blocking collectives, local(): lon_got = lax.all_to_all(lon_send, 'lon', 0, 0, axis_index_groups=ring)  14.6 us
    pallas_call x1, Pallas kernels, block_pass(): pl.pallas_call(main_kernel, out_shape=(jax.ShapeDtypeStruct((2, LEFT * LA...  14 us
    ppermute x5, waiting for transfers between devices, to_lon(): return lax.ppermute(x, 'lon', [(i, (i + by) % count) for i in range(count)])  12 us
    all_to_all x1, starting transfers between devices, local(): route_got = lax.all_to_all(route, 'lat', 0, 0)  9.49 us
    all_to_all x1, starting transfers between devices, local(): w_got = lax.all_to_all(w_sums, ('lon', 'lat'), 0, 0, axis_index_groups=near)  8.79 us
    all_to_all x1, waiting for transfers between devices, local(): route_got = lax.all_to_all(route, 'lat', 0, 0)  5.31 us
    pallas_call x1, Pallas kernels, prepare(): pl.pallas_call(prep_kernel, out_shape=jax.ShapeDtypeStruct((SLOTS, WTOK,...  4.05 us
  transfers between devices with their start and end apart: 7, of which 4 were waited for; matrix products, arithmetic and copies ran while one was open for 1% of the time, Pallas kernels for 8%

profile of v4, /device:TPU:1, one launch (start us, length us, event | category | flops | bytes accessed | tf_op | source)
XLA Modules:
  0.0 105.6 jit_solution(5559312527004323913)
XLA Ops:
  0.6 0.0 copy-start.5
  0.6 0.0 copy-start.3
  0.7 0.6 index_tables.1
  1.2 0.0 copy-start
  1.2 0.0 copy-start.9
  1.2 0.4 copy-done.5
  1.6 0.1 copy-done.3
  1.7 0.9 pack_edges.1
  2.6 12.9 %collective-permute-start.1 = (bf16[2,144,384]{2,1,0:T(8,128)(2,1)}, bf16[2,144,384]{2,1,0:T(8,128)(2,1)}, u32[]{:S(2)}, u32[]{:S(2)}) collective-permute-start(bf16[2,144,384]{2,1,0:T(8,128)(2,1)} %get-tuple-element.42), channel_id=1, source_target_pairs={{0,496},{16,0},{32,16},{48,32},{64,48},{80,64},{96,80},{112,96},{1... | collective-permute-start | bytes 663560 | tf_op jit(solution)/shard_map/ppermute | solution.py:601
  15.4 1.9 %collective-permute-start = (bf16[2,120,384]{2,1,0:T(8,128)(2,1)}, bf16[2,120,384]{2,1,0:T(8,128)(2,1)}, u32[]{:S(2)}, u32[]{:S(2)}) collective-permute-start(bf16[2,120,384]{2,1,0:T(8,128)(2,1)} %get-tuple-element.41), channel_id=1, source_target_pairs={{0,16},{16,32},{32,48},{48,64},{64,80},{80,96},{96,112},{112,128},... | collective-permute-start | bytes 552968 | tf_op jit(solution)/shard_map/ppermute | solution.py:601
  17.4 0.0 copy-start.4
  17.4 0.0 copy-start.6
  17.5 4.1 %prepare.1.bias_ref = f32[4,144,864]{2,1,0:T(8,128)S(1)} custom-call(s32[1]{0:T(128)} %bitcast.5.lat_ref, s32[16]{0:T(128)S(1)} %copy-done.9, bf16[32,19872]{1,0:T(8,128)(2,1)S(1)} %copy-done, bf16[576,1152]{1,0:T(8,128)(2,1)S(1)} %get-tuple-element.40.order_ref.rows_ref, bf16[3,512,144]{2,1,0:T(8,128)(2,1)S(1)} %get-tuple-element.50.spread_ref), custom_call_target="tpu_custom_call" | custom-call | flops 1000000000 | bytes 6000000 | tf_op jit(solution)/shard_map/prepare/pallas_call | solution.py:605
  21.6 1.6 %own_cells.1 = (f32[4,144,192]{2,1,0:T(8,128)S(1)}, f32[4,144,192]{2,1,0:T(8,128)S(1)}, bf16[288,120]{1,0:T(8,128)(2,1)S(1)}, bf16[288,144]{1,0:T(8,128)(2,1)S(1...) custom-call(s32[1]{0:T(128)} %bitcast.5.lat_ref, ...), custom_call_target="tpu_custom_call" | custom-call | flops 1000000000 | bytes 6000000 | tf_op jit(solution)/shard_map/own_cells/pallas_call | solution.py:623
  23.3 1.7 %collective-permute-done.left_ref = bf16[2,120,384]{2,1,0:T(8,128)(2,1)} collective-permute-done((bf16[2,120,384]{2,1,0:T(8,128)(2,1)}, bf16[2,120,384]{2,1,0:T(8,128)(2,1)}, u32[]{:S(2)}, u32[]{:S(2)}) %collective-permute-start) | collective-permute-done | bytes 184352 | tf_op jit(solution)/shard_map/ppermute | solution.py:601
  24.9 14.0 %block_pass.1 = (bf16[2,120,384]{2,1,0:T(8,128)(2,1)S(1)}, bf16[2,2,288,192]{3,2,1,0:T(8,128)(2,1)S(1)}, bf16[2,144,384]{2,1,0:T(8,128)(2,1)S(1)}, bf16[32,24,57...) custom-call(s32[1]{0:T(128)} %bitcast.half_ref, ...), custom_call_target="tpu_custom_call" | custom-call | tf_op jit(solution)/shard_map/block_pass/pallas_call | solution.py:636
  38.9 0.7 copy-done.10
  39.6 8.8 %all-to-all-start = ((bf16[32,24,576]{2,1,0:T(8,128)(2,1)}), bf16[32,24,576]{2,1,0:T(8,128)(2,1)S(1)}, u32[]{:S(2)}, u32[]{:S(2)}) async-start(bf16[32,24,576]{2,1,0:T(8,128)(2,1)} %get-tuple-element.58), calls=%async_computation | async-start | bytes 1966080 | tf_op jit(solution)/shard_map/all_to_all | solution.py:704
  48.4 1.9 %collective-permute-start.3 = (bf16[2,144,384]{2,1,0:T(8,128)(2,1)S(1)}, bf16[2,144,384]{2,1,0:T(8,128)(2,1)S(1)}, u32[]{:S(2)}, u32[]{:S(2)}) collective-permute-start(bf16[2,144,384]{2,1,0:T(8,128)(2,1)S(1)} %get-tuple-element.61), channel_id=1, source_target_pairs={{0,16},{16,32},{32,48},{48,64},{64,80},{80,96},{96,112},{112,128},... | collective-permute-start | bytes 663560 | tf_op jit(solution)/shard_map/ppermute | solution.py:601
  50.3 5.5 %collective-permute-start.4 = (bf16[2,120,384]{2,1,0:T(8,128)(2,1)S(1)}, bf16[2,120,384]{2,1,0:T(8,128)(2,1)S(1)}, u32[]{:S(2)}, u32[]{:S(2)}) collective-permute-start(bf16[2,120,384]{2,1,0:T(8,128)(2,1)S(1)} %get-tuple-element.62), channel_id=1, source_target_pairs={{0,496},{16,0},{32,16},{48,32},{64,48},{80,64},{96,80},{112,96},{1... | collective-permute-start | bytes 552968 | tf_op jit(solution)/shard_map/ppermute | solution.py:601
  55.8 3.3 %collective-permute-start.2 = (bf16[16,40,128]{2,1,0:T(8,128)(2,1)S(1)}, bf16[16,40,128]{2,1,0:T(8,128)(2,1)S(1)}, u32[]{:S(2)}, u32[]{:S(2)}) collective-permute-start(bf16[16,40,128]{2,1,0:T(8,128)(2,1)S(1)} %copy-done.11), channel_id=1, source_target_pairs={{0,256},{16,272},{32,288},{48,304},{64,320},{80,336},{96,352},{112... | collective-permute-start | bytes 491528 | tf_op jit(solution)/shard_map/ppermute | solution.py:601
  59.1 10.3 %collective-permute-done.2.got_ref = bf16[16,40,128]{2,1,0:T(8,128)(2,1)S(1)} collective-permute-done((bf16[16,40,128]{2,1,0:T(8,128)(2,1)S(1)}, bf16[16,40,128]{2,1,0:T(8,128)(2,1)S(1)}, u32[]{:S(2)}, u32[]{:S(2)}) %collective-permute-start.2) | collective-permute-done | bytes 163872 | tf_op jit(solution)/shard_map/ppermute | solution.py:601
  69.5 0.4 all-to-all-done.w_ref
  69.8 1.8 %sum_lat.1 = bf16[16,32,128]{2,1,0:T(8,128)(2,1)S(1)} custom-call(bf16[32,24,576]{2,1,0:T(8,128)(2,1)S(1)} %all-to-all-done.w_ref, bf16[16,40,128]{2,1,0:T(8,128)(2,1)S(1)} %get-tuple-element.59.keep_ref, bf16[16,40,128]{2,1,0:T(8,128)(2,1)S(1)} %collective-permute-done.2.got_ref), custom_call_target="tpu_custom_call" | custom-call | tf_op jit(solution)/shard_map/sum_lat/pallas_call | solution.py:706
  71.7 14.6 %all_to_all.15.in_ref = bf16[16,32,128]{2,1,0:T(8,128)(2,1)S(1)} all-to-all(bf16[16,32,128]{2,1,0:T(8,128)(2,1)S(1)} %sum_lat.1), channel_id=1, replica_groups={{0,16,32,48,64,80,96,112,128,144,160,176,192,208,224,240},{256,272,288,..., dimensions={0} | all-to-all | bytes 262144 | tf_op jit(solution)/shard_map/all_to_all | solution.py:729
  86.3 1.5 %sum_lon.1 = (f32[12,18]{1,0:T(8,128)}, f32[12,6]{1,0:T(8,128)S(1)}, f32[12,24]{1,0:T(8,128)}, f32[48,6]{1,0:T(8,128)S(1)}, bf16[16,32,128]{2,1,0:T(8,128)(2,1)}) custom-call(s32[1]{0:T(128)} %bitcast.5.lat_ref, s32[16]{0:T(128)S(1)} %copy-done.9, bf16[16,32,128]{2,1,0:T(8,128)(2,1)S(1)} %all_to_all.15.in_ref), custom_call_target="tpu_custom_call" | custom-call | tf_op jit(solution)/shard_map/sum_lon/pallas_call | solution.py:731
  87.8 9.5 %all-to-all-start.2 = ((bf16[16,32,128]{2,1,0:T(8,128)(2,1)}), bf16[16,32,128]{2,1,0:T(8,128)(2,1)S(1)}, u32[]{:S(2)}, u32[]{:S(2)}) async-start(bf16[16,32,128]{2,1,0:T(8,128)(2,1)} %get-tuple-element.72), calls=%async_computation.2 | async-start | bytes 262144 | tf_op jit(solution)/shard_map/all_to_all | solution.py:745
  97.3 1.0 join_cells.1
  98.3 0.7 copy.16
  99.0 0.7 copy.17
  99.6 5.3 %all-to-all-done.2.in_ref = bf16[16,32,128]{2,1,0:T(8,128)(2,1)S(1)} async-done(((bf16[16,32,128]{2,1,0:T(8,128)(2,1)}), bf16[16,32,128]{2,1,0:T(8,128)(2,1)S(1)}, u32[]{:S(2)}, u32[]{:S(2)}) %all-to-all-start.2) | async-done | bytes 131104 | tf_op jit(solution)/shard_map/all_to_all | solution.py:745
  104.9 0.7 sum_table.1
  (20 shorter events, 0.1 us)
Async XLA Ops:
  0.6 1.0 copy-start.5
  0.6 1.0 copy-start.3
  1.2 16.2 %copy-start = (bf16[32,19872]{1,0:T(8,128)(2,1)S(1)}, bf16[32,19872]{1,0:T(8,128)(2,1)}, u32[]{:S(2)}) copy-start(bf16[32,19872]{1,0:T(8,128)(2,1)} %table_ref.1) | copy-start | bytes 3815428
  1.2 16.2 %copy-start.9 = (s32[16]{0:T(128)S(1)}, s32[16]{0:T(128)}, u32[]{:S(2)}) copy-start(s32[16]{0:T(128)} %band_ref.5) | copy-start | bytes 196
  2.6 22.4 %collective-permute-start.1 = (bf16[2,144,384]{2,1,0:T(8,128)(2,1)}, bf16[2,144,384]{2,1,0:T(8,128)(2,1)}, u32[]{:S(2)}, u32[]{:S(2)}) collective-permute-start(bf16[2,144,384]{2,1,0:T(8,128)(2,1)} %get-tuple-element.42), channel_id=1, source_target_pairs={{0,496},{16,0},{32,16},{48,32},{64,48},{80,64},{96,80},{112,96},{1... | collective-permute-start | bytes 663560 | tf_op jit(solution)/shard_map/ppermute | solution.py:601
  15.4 9.5 %collective-permute-start = (bf16[2,120,384]{2,1,0:T(8,128)(2,1)}, bf16[2,120,384]{2,1,0:T(8,128)(2,1)}, u32[]{:S(2)}, u32[]{:S(2)}) collective-permute-start(bf16[2,120,384]{2,1,0:T(8,128)(2,1)} %get-tuple-element.41), channel_id=1, source_target_pairs={{0,16},{16,32},{32,48},{48,64},{64,80},{80,96},{96,112},{112,128},... | collective-permute-start | bytes 552968 | tf_op jit(solution)/shard_map/ppermute | solution.py:601
  17.4 4.1 %copy-start.1 = (bf16[192,768]{1,0:T(8,128)(2,1)S(1)}, bf16[192,768]{1,0:T(8,128)(2,1)}, u32[]{:S(2)}) copy-start(bf16[192,768]{1,0:T(8,128)(2,1)} %wup_ref.3) | copy-start | bytes 884740
  17.4 4.1 %copy-start.2 = (bf16[768,192]{0,1:T(8,128)(2,1)S(1)}, bf16[768,192]{0,1:T(8,128)(2,1)}, u32[]{:S(2)}) copy-start(bf16[768,192]{0,1:T(8,128)(2,1)} %param.14) | copy-start | bytes 884740
  17.4 4.1 %copy-start.4 = (bf16[2,24,12,192]{3,1,2,0:T(8,128)(2,1)S(1)}, bf16[2,24,12,192]{3,1,2,0:T(8,128)(2,1)}, u32[]{:S(2)}) copy-start(bf16[2,24,12,192]{3,1,2,0:T(8,128)(2,1)} %param.9) | copy-start | bytes 663556
  17.4 4.1 %copy-start.6 = (bf16[2,24,12,192]{3,1,2,0:T(8,128)(2,1)S(1)}, bf16[2,24,12,192]{3,1,2,0:T(8,128)(2,1)}, u32[]{:S(2)}) copy-start(bf16[2,24,12,192]{3,1,2,0:T(8,128)(2,1)} %param.10) | copy-start | bytes 663556
  17.4 4.1 %copy-start.7 = (bf16[192,576]{1,0:T(8,128)(2,1)S(1)}, bf16[192,576]{1,0:T(8,128)(2,1)}, u32[]{:S(2)}) copy-start(bf16[192,576]{1,0:T(8,128)(2,1)} %wqkv_ref.3) | copy-start | bytes 663556
  17.5 4.1 %copy-start.8 = (bf16[192,192]{1,0:T(8,128)(2,1)S(1)}, bf16[192,192]{1,0:T(8,128)(2,1)}, u32[]{:S(2)}) copy-start(bf16[192,192]{1,0:T(8,128)(2,1)} %wproj_ref.3) | copy-start | bytes 221188
  17.5 4.1 %copy-start.12 = (s32[32]{0:T(128)S(1)}, s32[32]{0:T(128)}, u32[]{:S(2)}) copy-start(s32[32]{0:T(128)} %shift_ref.1) | copy-start | bytes 388
  38.9 0.7 copy-start.10
  39.6 16.2 %copy-start.11 = (bf16[16,40,128]{2,1,0:T(8,128)(2,1)S(1)}, bf16[16,40,128]{2,1,0:T(8,128)(2,1)}, u32[]{:S(2)}) copy-start(bf16[16,40,128]{2,1,0:T(8,128)(2,1)} %copy-done.10) | copy-start | bytes 491524
  39.6 30.2 %all-to-all-start = ((bf16[32,24,576]{2,1,0:T(8,128)(2,1)}), bf16[32,24,576]{2,1,0:T(8,128)(2,1)S(1)}, u32[]{:S(2)}, u32[]{:S(2)}) async-start(bf16[32,24,576]{2,1,0:T(8,128)(2,1)} %get-tuple-element.58), calls=%async_computation | async-start | bytes 1966080 | tf_op jit(solution)/shard_map/all_to_all | solution.py:704
  48.4 23.3 %collective-permute-start.3 = (bf16[2,144,384]{2,1,0:T(8,128)(2,1)S(1)}, bf16[2,144,384]{2,1,0:T(8,128)(2,1)S(1)}, u32[]{:S(2)}, u32[]{:S(2)}) collective-permute-start(bf16[2,144,384]{2,1,0:T(8,128)(2,1)S(1)} %get-tuple-element.61), channel_id=1, source_target_pairs={{0,16},{16,32},{32,48},{48,64},{64,80},{80,96},{96,112},{112,128},... | collective-permute-start | bytes 663560 | tf_op jit(solution)/shard_map/ppermute | solution.py:601
  50.3 21.3 %collective-permute-start.4 = (bf16[2,120,384]{2,1,0:T(8,128)(2,1)S(1)}, bf16[2,120,384]{2,1,0:T(8,128)(2,1)S(1)}, u32[]{:S(2)}, u32[]{:S(2)}) collective-permute-start(bf16[2,120,384]{2,1,0:T(8,128)(2,1)S(1)} %get-tuple-element.62), channel_id=1, source_target_pairs={{0,496},{16,0},{32,16},{48,32},{64,48},{80,64},{96,80},{112,96},{1... | collective-permute-start | bytes 552968 | tf_op jit(solution)/shard_map/ppermute | solution.py:601
  55.8 13.6 %collective-permute-start.2 = (bf16[16,40,128]{2,1,0:T(8,128)(2,1)S(1)}, bf16[16,40,128]{2,1,0:T(8,128)(2,1)S(1)}, u32[]{:S(2)}, u32[]{:S(2)}) collective-permute-start(bf16[16,40,128]{2,1,0:T(8,128)(2,1)S(1)} %copy-done.11), channel_id=1, source_target_pairs={{0,256},{16,272},{32,288},{48,304},{64,320},{80,336},{96,352},{112... | collective-permute-start | bytes 491528 | tf_op jit(solution)/shard_map/ppermute | solution.py:601
  87.8 17.1 %all-to-all-start.2 = ((bf16[16,32,128]{2,1,0:T(8,128)(2,1)}), bf16[16,32,128]{2,1,0:T(8,128)(2,1)S(1)}, u32[]{:S(2)}, u32[]{:S(2)}) async-start(bf16[16,32,128]{2,1,0:T(8,128)(2,1)} %get-tuple-element.72), calls=%async_computation.2 | async-start | bytes 262144 | tf_op jit(solution)/shard_map/all_to_all | solution.py:745

commit v5 on v4

--- a/solution.py
+++ b/solution.py
@@ -460,7 +460,7 @@
     mine = tt_s[pl.ds(pl.multiple_of(half * size, 8), size), :]
     keep_ref[...] = mine.reshape(Z, PER_Z, 128).astype(bf16)
     other = tt_s[pl.ds(pl.multiple_of((1 - half) * size, 8), size), :]
-    give_ref[...] = other.reshape(Z, PER_Z, 128).astype(bf16)
+    give_ref[...] = mm(eye(80), other[:, 0:80].astype(bf16), NT).astype(bf16)
 
     for x in range(2):
         accq_s[:, x * 384 : x * 384 + 288] = acc_s[:, x * 288 : x * 288 + 288]
@@ -474,7 +474,15 @@
                 for g in range(2)
             ]
             both = jnp.concatenate([top, low], axis=0)
-            wsum_ref[x * NLAT + i] = jnp.concatenate([both] + down, axis=1).astype(bf16)
+            both = jnp.concatenate([both] + down, axis=1)
+            wsum_ref[x * NLAT + i] = jnp.concatenate(
+                [both[:, 128 * n : 128 * n + 128] for n in range(4)]
+                + [
+                    jnp.concatenate([both[0:12, 512:576], both[12:24, 512:576]], axis=1),
+                    jnp.zeros((4, 128), f32),
+                ],
+                axis=0,
+            ).astype(bf16)
 
     for which, scratch in ((0, ro_s), (1, rg_s)):
         levels = [
@@ -499,6 +507,12 @@
     total = w_ref[0].astype(f32)
     for i in range(1, 2 * NLAT):
         total = total + w_ref[i].astype(f32)
+    half = jnp.concatenate([total[96:108, 0:64], total[96:108, 64:128]], axis=0)
+    total = jnp.concatenate([total[24 * n : 24 * n + 24] for n in range(4)] + [half], axis=1)
+    got = got_ref[...]
+    got = jnp.concatenate(
+        [mm(eye(128), got[:, 128 * n : 128 * n + 128], NT) for n in range(5)], axis=0
+    )
     qkv, proj = total[0:12, 0:288], total[0:12, 288:384]
     up = total[12:24, 0:384]
     down = [
@@ -518,7 +532,7 @@
             ],
             axis=0,
         )
-        table = keep_ref[z, :, 0:69].astype(f32) + got_ref[z, :, 0:69].astype(f32)
+        table = keep_ref[z, :, 0:69].astype(f32) + got[z * PER_Z : (z + 1) * PER_Z, 0:69]
         rest = jnp.concatenate(
             [
                 jnp.concatenate([table[32:36, 23 * n : 23 * n + 23] for n in range(3)], axis=0),
@@ -639,9 +653,9 @@
             jax.ShapeDtypeStruct((2, LEFT * LAT, 2 * WIDTH), bf16),
             jax.ShapeDtypeStruct((2, LEVELS, WW * LAT, WIDTH), bf16),
             jax.ShapeDtypeStruct((2, RIGHT * LAT, 2 * WIDTH), bf16),
-            jax.ShapeDtypeStruct((2 * NLAT, 24, 576), bf16),
+            jax.ShapeDtypeStruct((2 * NLAT, 112, 128), bf16),
             jax.ShapeDtypeStruct((Z, PER_Z, 128), bf16),
-            jax.ShapeDtypeStruct((Z, PER_Z, 128), bf16),
+            jax.ShapeDtypeStruct((80, Z * PER_Z), bf16),
         ),
         in_specs=[smem()] + [vmem()] * 21,
         out_specs=(vmem(),) * 6,

time: 106 us -> 103 us (0.972)
  starting transfers between devices: 43.8 us -> 41.7 us
    ppermute x5, waiting for transfers between devices: 12 us -> 10 us  [to_lon(): return lax.ppermute(x, 'lon', [(i, (i + by) % count) for i in range(count)])]
    all_to_all x1, starting transfers between devices: 9.49 us -> 7.52 us  [local(): route_got = lax.all_to_all(route, 'lat', 0, 0)]
    all_to_all x1, waiting for transfers between devices: 0.39 us -> 1.75 us  [local(): w_got = lax.all_to_all(w_sums, ('lon', 'lat'), 0, 0, axis_index_groups=near)]
    unnamed x28 -> x24, local copies, waits for them, and re-layouts: 2.52 us -> 1.85 us
where the time goes in v5:
time: 103 us
  starting transfers between devices  41.7 us (40%)
  Pallas kernels  26.1 us (25%)
  waiting for transfers between devices  17.1 us (17%)
  blocking collectives  15.3 us (15%)
  local copies, waits for them, and re-layouts  1.85 us (2%)
    ppermute x5, starting transfers between devices, to_lon(): return lax.ppermute(x, 'lon', [(i, (i + by) % count) for i in range(count)])  25.5 us
    all_to_all x1, blocking collectives, local(): lon_got = lax.all_to_all(lon_send, 'lon', 0, 0, axis_index_groups=ring)  15.3 us
    pallas_call x1, Pallas kernels, block_pass(): pl.pallas_call(main_kernel, out_shape=(jax.ShapeDtypeStruct((2, LEFT * LA...  14.5 us
    ppermute x5, waiting for transfers between devices, to_lon(): return lax.ppermute(x, 'lon', [(i, (i + by) % count) for i in range(count)])  10 us
    all_to_all x1, starting transfers between devices, local(): w_got = lax.all_to_all(w_sums, ('lon', 'lat'), 0, 0, axis_index_groups=near)  8.65 us
    all_to_all x1, starting transfers between devices, local(): route_got = lax.all_to_all(route, 'lat', 0, 0)  7.52 us
    all_to_all x1, waiting for transfers between devices, local(): route_got = lax.all_to_all(route, 'lat', 0, 0)  5.31 us
    pallas_call x1, Pallas kernels, prepare(): pl.pallas_call(prep_kernel, out_shape=jax.ShapeDtypeStruct((SLOTS, WTOK,...  4.05 us
  transfers between devices with their start and end apart: 7, of which 4 were waited for; matrix products, arithmetic and copies ran while one was open for 1% of the time, Pallas kernels for 8%

profile of v5, /device:TPU:1, one launch (start us, length us, event | category | flops | bytes accessed | tf_op | source)
XLA Modules:
  0.0 102.8 jit_solution(14359993234449618477)
XLA Ops:
  0.6 0.0 copy-start.5
  0.6 0.0 copy-start.3
  0.7 0.6 index_tables.1
  1.2 0.0 copy-start
  1.2 0.4 copy-done.5
  1.6 0.1 copy-done.3
  1.7 0.9 pack_edges.1
  2.6 12.9 %collective-permute-start.1 = (bf16[2,144,384]{2,1,0:T(8,128)(2,1)}, bf16[2,144,384]{2,1,0:T(8,128)(2,1)}, u32[]{:S(2)}, u32[]{:S(2)}) collective-permute-start(bf16[2,144,384]{2,1,0:T(8,128)(2,1)} %get-tuple-element.42), channel_id=1, source_target_pairs={{0,496},{16,0},{32,16},{48,32},{64,48},{80,64},{96,80},{112,96},{1... | collective-permute-start | bytes 663560 | tf_op jit(solution)/shard_map/ppermute | solution.py:615
  15.4 1.9 %collective-permute-start = (bf16[2,120,384]{2,1,0:T(8,128)(2,1)}, bf16[2,120,384]{2,1,0:T(8,128)(2,1)}, u32[]{:S(2)}, u32[]{:S(2)}) collective-permute-start(bf16[2,120,384]{2,1,0:T(8,128)(2,1)} %get-tuple-element.41), channel_id=1, source_target_pairs={{0,16},{16,32},{32,48},{48,64},{64,80},{80,96},{96,112},{112,128},... | collective-permute-start | bytes 552968 | tf_op jit(solution)/shard_map/ppermute | solution.py:615
  17.4 0.0 copy-start.2
  17.4 0.0 copy-start.4
  17.5 0.0 copy-start.8
  17.5 0.0 copy-start.10
  17.5 4.1 %prepare.1.bias_ref = f32[4,144,864]{2,1,0:T(8,128)S(1)} custom-call(s32[1]{0:T(128)} %bitcast.5.lat_ref, s32[16]{0:T(128)S(1)} %copy-done.9, bf16[32,19872]{1,0:T(8,128)(2,1)S(1)} %copy-done, bf16[576,1152]{1,0:T(8,128)(2,1)S(1)} %get-tuple-element.40.order_ref.rows_ref, bf16[3,512,144]{2,1,0:T(8,128)(2,1)S(1)} %get-tuple-element.50.spread_ref), custom_call_target="tpu_custom_call" | custom-call | flops 1000000000 | bytes 6000000 | tf_op jit(solution)/shard_map/prepare/pallas_call | solution.py:619
  21.6 1.6 %own_cells.1 = (f32[4,144,192]{2,1,0:T(8,128)S(1)}, f32[4,144,192]{2,1,0:T(8,128)S(1)}, bf16[288,120]{1,0:T(8,128)(2,1)S(1)}, bf16[288,144]{1,0:T(8,128)(2,1)S(1...) custom-call(s32[1]{0:T(128)} %bitcast.5.lat_ref, ...), custom_call_target="tpu_custom_call" | custom-call | flops 1000000000 | bytes 6000000 | tf_op jit(solution)/shard_map/own_cells/pallas_call | solution.py:637
  23.3 1.7 %collective-permute-done.left_ref = bf16[2,120,384]{2,1,0:T(8,128)(2,1)} collective-permute-done((bf16[2,120,384]{2,1,0:T(8,128)(2,1)}, bf16[2,120,384]{2,1,0:T(8,128)(2,1)}, u32[]{:S(2)}, u32[]{:S(2)}) %collective-permute-start) | collective-permute-done | bytes 184352 | tf_op jit(solution)/shard_map/ppermute | solution.py:615
  24.9 14.5 %block_pass.1 = (bf16[2,120,384]{2,1,0:T(8,128)(2,1)S(1)}, bf16[2,2,288,192]{3,2,1,0:T(8,128)(2,1)S(1)}, bf16[2,144,384]{2,1,0:T(8,128)(2,1)S(1)}, bf16[32,112,1...) custom-call(s32[1]{0:T(128)} %bitcast.half_ref, ...), custom_call_target="tpu_custom_call" | custom-call | tf_op jit(solution)/shard_map/block_pass/pallas_call | solution.py:650
  39.4 8.7 %all-to-all-start = ((bf16[32,112,128]{2,1,0:T(8,128)(2,1)}), bf16[32,112,128]{2,1,0:T(8,128)(2,1)S(1)}, u32[]{:S(2)}, u32[]{:S(2)}) async-start(bf16[32,112,128]{2,1,0:T(8,128)(2,1)} %get-tuple-element.58), calls=%async_computation | async-start | bytes 1835008 | tf_op jit(solution)/shard_map/all_to_all | solution.py:718
  48.1 1.9 %collective-permute-start.3 = (bf16[2,144,384]{2,1,0:T(8,128)(2,1)S(1)}, bf16[2,144,384]{2,1,0:T(8,128)(2,1)S(1)}, u32[]{:S(2)}, u32[]{:S(2)}) collective-permute-start(bf16[2,144,384]{2,1,0:T(8,128)(2,1)S(1)} %get-tuple-element.61), channel_id=1, source_target_pairs={{0,16},{16,32},{32,48},{48,64},{64,80},{80,96},{96,112},{112,128},... | collective-permute-start | bytes 663560 | tf_op jit(solution)/shard_map/ppermute | solution.py:615
  50.0 5.5 %collective-permute-start.4 = (bf16[2,120,384]{2,1,0:T(8,128)(2,1)S(1)}, bf16[2,120,384]{2,1,0:T(8,128)(2,1)S(1)}, u32[]{:S(2)}, u32[]{:S(2)}) collective-permute-start(bf16[2,120,384]{2,1,0:T(8,128)(2,1)S(1)} %get-tuple-element.62), channel_id=1, source_target_pairs={{0,496},{16,0},{32,16},{48,32},{64,48},{80,64},{96,80},{112,96},{1... | collective-permute-start | bytes 552968 | tf_op jit(solution)/shard_map/ppermute | solution.py:615
  55.5 3.3 %collective-permute-start.2 = (bf16[80,640]{1,0:T(8,128)(2,1)S(1)}, bf16[80,640]{1,0:T(8,128)(2,1)S(1)}, u32[]{:S(2)}, u32[]{:S(2)}) collective-permute-start(bf16[80,640]{1,0:T(8,128)(2,1)S(1)} %get-tuple-element.60), channel_id=1, source_target_pairs={{0,256},{16,272},{32,288},{48,304},{64,320},{80,336},{96,352},{112... | collective-permute-start | bytes 307208 | tf_op jit(solution)/shard_map/ppermute | solution.py:615
  58.8 8.3 %collective-permute-done.2.got_ref = bf16[80,640]{1,0:T(8,128)(2,1)S(1)} collective-permute-done((bf16[80,640]{1,0:T(8,128)(2,1)S(1)}, bf16[80,640]{1,0:T(8,128)(2,1)S(1)}, u32[]{:S(2)}, u32[]{:S(2)}) %collective-permute-start.2) | collective-permute-done | bytes 102432 | tf_op jit(solution)/shard_map/ppermute | solution.py:615
  67.1 1.8 %all-to-all-done.w_ref = bf16[32,112,128]{2,1,0:T(8,128)(2,1)S(1)} async-done(((bf16[32,112,128]{2,1,0:T(8,128)(2,1)}), bf16[32,112,128]{2,1,0:T(8,128)(2,1)S(1)}, u32[]{:S(2)}, u32[]{:S(2)}) %all-to-all-start) | async-done | bytes 917536 | tf_op jit(solution)/shard_map/all_to_all | solution.py:718
  68.8 1.3 %sum_lat.1 = bf16[16,32,128]{2,1,0:T(8,128)(2,1)S(1)} custom-call(bf16[32,112,128]{2,1,0:T(8,128)(2,1)S(1)} %all-to-all-done.w_ref, bf16[16,40,128]{2,1,0:T(8,128)(2,1)S(1)} %get-tuple-element.59.keep_ref, bf16[80,640]{1,0:T(8,128)(2,1)S(1)} %collective-permute-done.2.got_ref), custom_call_target="tpu_custom_call" | custom-call | tf_op jit(solution)/shard_map/sum_lat/pallas_call | solution.py:720
  70.2 15.3 %all_to_all.15.in_ref = bf16[16,32,128]{2,1,0:T(8,128)(2,1)S(1)} all-to-all(bf16[16,32,128]{2,1,0:T(8,128)(2,1)S(1)} %sum_lat.1), channel_id=1, replica_groups={{0,16,32,48,64,80,96,112,128,144,160,176,192,208,224,240},{256,272,288,..., dimensions={0} | all-to-all | bytes 262144 | tf_op jit(solution)/shard_map/all_to_all | solution.py:743
  85.5 1.5 %sum_lon.1 = (f32[12,18]{1,0:T(8,128)}, f32[12,6]{1,0:T(8,128)S(1)}, f32[12,24]{1,0:T(8,128)}, f32[48,6]{1,0:T(8,128)S(1)}, bf16[16,32,128]{2,1,0:T(8,128)(2,1)}) custom-call(s32[1]{0:T(128)} %bitcast.5.lat_ref, s32[16]{0:T(128)S(1)} %copy-done.9, bf16[16,32,128]{2,1,0:T(8,128)(2,1)S(1)} %all_to_all.15.in_ref), custom_call_target="tpu_custom_call" | custom-call | tf_op jit(solution)/shard_map/sum_lon/pallas_call | solution.py:745
  86.9 7.5 %all-to-all-start.2 = ((bf16[16,32,128]{2,1,0:T(8,128)(2,1)}), bf16[16,32,128]{2,1,0:T(8,128)(2,1)S(1)}, u32[]{:S(2)}, u32[]{:S(2)}) async-start(bf16[16,32,128]{2,1,0:T(8,128)(2,1)} %get-tuple-element.72), calls=%async_computation.2 | async-start | bytes 262144 | tf_op jit(solution)/shard_map/all_to_all | solution.py:759
  94.4 1.0 join_cells.1
  95.4 0.7 copy.16
  96.1 0.7 copy.17
  96.8 5.3 %all-to-all-done.2.in_ref = bf16[16,32,128]{2,1,0:T(8,128)(2,1)S(1)} async-done(((bf16[16,32,128]{2,1,0:T(8,128)(2,1)}), bf16[16,32,128]{2,1,0:T(8,128)(2,1)S(1)}, u32[]{:S(2)}, u32[]{:S(2)}) %all-to-all-start.2) | async-done | bytes 131104 | tf_op jit(solution)/shard_map/all_to_all | solution.py:759
  102.1 0.7 sum_table.1
  (16 shorter events, 0.0 us)
Async XLA Ops:
  0.6 1.0 copy-start.5
  0.6 1.0 %copy-start.3 = (bf16[2,24,12,192]{3,1,2,0:T(8,128)(2,1)S(1)}, bf16[2,24,12,192]{3,1,2,0:T(8,128)(2,1)}, u32[]{:S(2)}) copy-start(bf16[2,24,12,192]{3,1,2,0:T(8,128)(2,1)} %param.9) | copy-start | bytes 663556
  1.2 16.2 %copy-start = (bf16[32,19872]{1,0:T(8,128)(2,1)S(1)}, bf16[32,19872]{1,0:T(8,128)(2,1)}, u32[]{:S(2)}) copy-start(bf16[32,19872]{1,0:T(8,128)(2,1)} %table_ref.1) | copy-start | bytes 3815428
  1.2 16.2 %copy-start.9 = (s32[16]{0:T(128)S(1)}, s32[16]{0:T(128)}, u32[]{:S(2)}) copy-start(s32[16]{0:T(128)} %band_ref.5) | copy-start | bytes 196
  2.6 22.4 %collective-permute-start.1 = (bf16[2,144,384]{2,1,0:T(8,128)(2,1)}, bf16[2,144,384]{2,1,0:T(8,128)(2,1)}, u32[]{:S(2)}, u32[]{:S(2)}) collective-permute-start(bf16[2,144,384]{2,1,0:T(8,128)(2,1)} %get-tuple-element.42), channel_id=1, source_target_pairs={{0,496},{16,0},{32,16},{48,32},{64,48},{80,64},{96,80},{112,96},{1... | collective-permute-start | bytes 663560 | tf_op jit(solution)/shard_map/ppermute | solution.py:615
  15.4 9.5 %collective-permute-start = (bf16[2,120,384]{2,1,0:T(8,128)(2,1)}, bf16[2,120,384]{2,1,0:T(8,128)(2,1)}, u32[]{:S(2)}, u32[]{:S(2)}) collective-permute-start(bf16[2,120,384]{2,1,0:T(8,128)(2,1)} %get-tuple-element.41), channel_id=1, source_target_pairs={{0,16},{16,32},{32,48},{48,64},{64,80},{80,96},{96,112},{112,128},... | collective-permute-start | bytes 552968 | tf_op jit(solution)/shard_map/ppermute | solution.py:615
  17.4 4.1 %copy-start.1 = (bf16[192,768]{1,0:T(8,128)(2,1)S(1)}, bf16[192,768]{1,0:T(8,128)(2,1)}, u32[]{:S(2)}) copy-start(bf16[192,768]{1,0:T(8,128)(2,1)} %wup_ref.3) | copy-start | bytes 884740
  17.4 4.1 %copy-start.2 = (bf16[768,192]{0,1:T(8,128)(2,1)S(1)}, bf16[768,192]{0,1:T(8,128)(2,1)}, u32[]{:S(2)}) copy-start(bf16[768,192]{0,1:T(8,128)(2,1)} %param.14) | copy-start | bytes 884740
  17.4 4.1 %copy-start.4 = (bf16[2,24,12,192]{3,1,2,0:T(8,128)(2,1)S(1)}, bf16[2,24,12,192]{3,1,2,0:T(8,128)(2,1)}, u32[]{:S(2)}) copy-start(bf16[2,24,12,192]{3,1,2,0:T(8,128)(2,1)} %param.9) | copy-start | bytes 663556
  17.4 4.1 %copy-start.6 = (bf16[2,24,12,192]{3,1,2,0:T(8,128)(2,1)S(1)}, bf16[2,24,12,192]{3,1,2,0:T(8,128)(2,1)}, u32[]{:S(2)}) copy-start(bf16[2,24,12,192]{3,1,2,0:T(8,128)(2,1)} %param.10) | copy-start | bytes 663556
  17.4 4.1 %copy-start.7 = (bf16[192,576]{1,0:T(8,128)(2,1)S(1)}, bf16[192,576]{1,0:T(8,128)(2,1)}, u32[]{:S(2)}) copy-start(bf16[192,576]{1,0:T(8,128)(2,1)} %wqkv_ref.3) | copy-start | bytes 663556
  17.5 4.1 %copy-start.8 = (bf16[192,192]{1,0:T(8,128)(2,1)S(1)}, bf16[192,192]{1,0:T(8,128)(2,1)}, u32[]{:S(2)}) copy-start(bf16[192,192]{1,0:T(8,128)(2,1)} %wproj_ref.3) | copy-start | bytes 221188
  17.5 4.1 %copy-start.10 = (s32[32]{0:T(128)S(1)}, s32[32]{0:T(128)}, u32[]{:S(2)}) copy-start(s32[32]{0:T(128)} %shift_ref.1) | copy-start | bytes 388
  39.4 29.4 %all-to-all-start = ((bf16[32,112,128]{2,1,0:T(8,128)(2,1)}), bf16[32,112,128]{2,1,0:T(8,128)(2,1)S(1)}, u32[]{:S(2)}, u32[]{:S(2)}) async-start(bf16[32,112,128]{2,1,0:T(8,128)(2,1)} %get-tuple-element.58), calls=%async_computation | async-start | bytes 1835008 | tf_op jit(solution)/shard_map/all_to_all | solution.py:718
  48.1 22.1 %collective-permute-start.3 = (bf16[2,144,384]{2,1,0:T(8,128)(2,1)S(1)}, bf16[2,144,384]{2,1,0:T(8,128)(2,1)S(1)}, u32[]{:S(2)}, u32[]{:S(2)}) collective-permute-start(bf16[2,144,384]{2,1,0:T(8,128)(2,1)S(1)} %get-tuple-element.61), channel_id=1, source_target_pairs={{0,16},{16,32},{32,48},{48,64},{64,80},{80,96},{96,112},{112,128},... | collective-permute-start | bytes 663560 | tf_op jit(solution)/shard_map/ppermute | solution.py:615
  50.0 20.2 %collective-permute-start.4 = (bf16[2,120,384]{2,1,0:T(8,128)(2,1)S(1)}, bf16[2,120,384]{2,1,0:T(8,128)(2,1)S(1)}, u32[]{:S(2)}, u32[]{:S(2)}) collective-permute-start(bf16[2,120,384]{2,1,0:T(8,128)(2,1)S(1)} %get-tuple-element.62), channel_id=1, source_target_pairs={{0,496},{16,0},{32,16},{48,32},{64,48},{80,64},{96,80},{112,96},{1... | collective-permute-start | bytes 552968 | tf_op jit(solution)/shard_map/ppermute | solution.py:615
  55.5 11.6 %collective-permute-start.2 = (bf16[80,640]{1,0:T(8,128)(2,1)S(1)}, bf16[80,640]{1,0:T(8,128)(2,1)S(1)}, u32[]{:S(2)}, u32[]{:S(2)}) collective-permute-start(bf16[80,640]{1,0:T(8,128)(2,1)S(1)} %get-tuple-element.60), channel_id=1, source_target_pairs={{0,256},{16,272},{32,288},{48,304},{64,320},{80,336},{96,352},{112... | collective-permute-start | bytes 307208 | tf_op jit(solution)/shard_map/ppermute | solution.py:615
  86.9 15.2 %all-to-all-start.2 = ((bf16[16,32,128]{2,1,0:T(8,128)(2,1)}), bf16[16,32,128]{2,1,0:T(8,128)(2,1)S(1)}, u32[]{:S(2)}, u32[]{:S(2)}) async-start(bf16[16,32,128]{2,1,0:T(8,128)(2,1)} %get-tuple-element.72), calls=%async_computation.2 | async-start | bytes 262144 | tf_op jit(solution)/shard_map/all_to_all | solution.py:759
